TPU v7x, 32 devices: a whole 2x2x4 slice. The times are simulated.
32 devices in a mesh: seq: 4 (over z), head: 4 (over y, x), dp: 2 (over core).
Axes of the slice: x: 2, y: 2, z: 4, core: 2. Of those that a mesh axis runs over, the one named last changes fastest.
Arguments:
- hidden_in: bfloat16 [2, 6144, 1024], P('dp', 'seq'), may hold values from -6 to 6
- doc_ids: int32 [2, 6144], P('dp', 'seq'), may hold values from 0 to 4, as said below
- norm_gain: float32 [1024], replicated, may hold values from 0.5 to 1.5
- w_gate: bfloat16 [1024, 2048], P(None, 'head'), may hold values from -0.1875 to 0.1875
- w_value: bfloat16 [1024, 2048], P(None, 'head'), may hold values from -0.1875 to 0.1875
- w_bc: bfloat16 [1024, 256], replicated, may hold values from -0.09375 to 0.09375
- w_step: bfloat16 [1024, 32], P(None, 'head'), may hold values from -0.1875 to 0.1875
- conv_value: float32 [5, 2048], P(None, 'head'), may hold values from -3 to 3
- conv_bc: float32 [5, 256], replicated, may hold values from -3 to 3
- dt_bias: float32 [32], P('head'), may hold values from -1 to 1
- a_log: float32 [32], P('head'), may hold values from -20 to -2
- d_skip: float32 [32], P('head'), may hold values from 0.5 to 2
- out_gain: float32 [2048], P('head'), may hold values from 0.5 to 1.5
- w_out: bfloat16 [2048, 1024], P('head'), may hold values from -0.125 to 0.125
- cotangent: bfloat16 [2, 6144, 1024], P('dp', 'seq', 'head'), may hold values from -6 to 6
Outputs:
- block_out: bfloat16 [2, 6144, 1024], P('dp', 'seq', 'head')
- grad_in: bfloat16 [2, 6144, 1024], P('dp', 'seq')
- grad_norm_gain: float32 [1024], replicated
- grad_w_gate: float32 [1024, 2048], P(None, 'head')
- grad_w_value: float32 [1024, 2048], P(None, 'head')
- grad_w_bc: float32 [1024, 256], replicated
- grad_w_step: float32 [1024, 32], P(None, 'head')
- grad_conv_value: float32 [5, 2048], P(None, 'head')
- grad_conv_bc: float32 [5, 256], replicated
- grad_dt_bias: float32 [32], P('head')
- grad_a_log: float32 [32], P('head')
- grad_d_skip: float32 [32], P('head')
- grad_out_gain: float32 [2048], P('head')
- grad_w_out: float32 [2048, 1024], P('head')
Inputs may be any that keep to these rules, and one draw needn't show every extreme that they name: `doc_ids`: each sequence's document numbers start at 0 and never fall; a document is a run of equal numbers.
All inputs are finite; a program needn't handle non-finite values.
Results may differ from a plain program's by a relative error of at most 0.025.
The roundings to bfloat16 on the way count: a program that leaves them out, or rounds other values in their place, can miss the bound.
Values may be sent and summed in bfloat16 or wider, within the bound.
A program may use at most 320 MiB of HBM per device.

v0:
```python
import jax
import jax.numpy as jnp
from jax import lax
from jax.sharding import PartitionSpec as P

BLOCK = 256


HIGHEST = lax.Precision.HIGHEST
eps = 1e-05


def from_behind(block, axis, distance):
    devices = range(lax.axis_size(axis))
    route = [(i - distance, i) for i in devices if i - distance in devices]
    return lax.ppermute(block, axis, route)


def prefix(array, axis, combine, identity):
    devices, here = (lax.axis_size(axis), lax.axis_index(axis))
    everything = jax.tree.map(
        lambda part, kind: lax.all_gather(part.astype(kind), axis),
        array,
        (jnp.bfloat16, jnp.bfloat16),
    )
    start = jax.tree.map(
        lambda part, zero: jnp.broadcast_to(jnp.asarray(zero, part.dtype), part.shape),
        array,
        identity,
    )

    def turn(k, before):
        reached = k < here
        new = combine(
            before, jax.tree.map(lambda part, own: part[k].astype(own.dtype), everything, array)
        )
        return jax.tree.map(lambda a, b: jnp.where(reached, a, b), new, before)

    return lax.fori_loop(0, devices, turn, start)


def prefix_2(array, axis, join, neutral):
    count = lax.axis_size(axis)
    place = lax.axis_index(axis)
    ahead = count - 1 - place
    gathered = jax.tree.map(
        lambda a, kind: lax.all_gather(a.astype(kind), axis),
        array,
        jax.tree.map(lambda a: jnp.bfloat16 if a.dtype == jnp.float32 else a.dtype, array),
    )
    state = jax.tree.map(lambda a, e: jnp.zeros_like(a) + jnp.asarray(e, a.dtype), array, neutral)

    def one(turn, state):
        source = count - 1 - turn
        return join(
            state,
            jax.tree.map(
                lambda a, own: lax.dynamic_index_in_dim(a, source, 0, False).astype(own.dtype),
                gathered,
                array,
            ),
        )

    return lax.fori_loop(0, ahead, one, state)


def ssd_block(carry, block):
    state_in, doc_prev = carry
    x_heads, b_mat, c_mat, step_size, log_decay, doc_row = block
    size = log_decay.shape[0]
    cum_decay = jnp.cumsum(log_decay, axis=0)
    where_at = jnp.arange(size)
    causal = (where_at[:, None] >= where_at[None, :]) & (doc_row[:, None] == doc_row[None, :])
    spread = cum_decay[:, None, :] - cum_decay[None, :, :]
    decay = jnp.where(causal[:, :, None], jnp.exp(jnp.where(causal[:, :, None], spread, 0.0)), 0.0)
    scores = jnp.einsum("tn,sn->ts", c_mat, b_mat, precision=HIGHEST)
    mixing = scores[:, :, None] * decay * step_size[None, :, :]
    y_intra = jnp.einsum("tsh,shp->thp", mixing, x_heads, precision=HIGHEST)
    carried = (doc_row == doc_prev).astype(jnp.float32)
    y_inter = (
        jnp.einsum("tn,hpn->thp", c_mat, state_in, precision=HIGHEST)
        * (jnp.exp(cum_decay) * carried[:, None])[:, :, None]
    )
    doc_last = doc_row[size - 1]
    to_end = (
        jnp.exp(cum_decay[size - 1][None, :] - cum_decay)
        * (doc_row == doc_last).astype(jnp.float32)[:, None]
        * step_size
    )
    kept = jnp.exp(cum_decay[size - 1]) * (doc_last == doc_prev).astype(jnp.float32)
    state_out = kept[:, None, None] * state_in + jnp.einsum(
        "sh,shp,sn->hpn", to_end, x_heads, b_mat, precision=HIGHEST
    )
    return ((state_out, doc_last), y_intra + y_inter)


def chain_combine(earlier, later):
    return (earlier[0] * later[0], later[0][:, None, None] * earlier[1] + later[1])


def on_device(
    hidden_in,
    doc_ids,
    norm_gain,
    w_gate,
    w_value,
    w_bc,
    w_step,
    conv_value,
    conv_bc,
    dt_bias,
    a_log,
    d_skip,
    out_gain,
    w_out,
    cotangent,
):
    x = hidden_in[0].astype(jnp.float32)
    doc_row = doc_ids[0]
    tokens = x.shape[0]
    inner_loc = w_gate.shape[1]
    heads_loc = w_step.shape[1]
    head_dim = inner_loc // heads_loc
    state_dim = w_bc.shape[1] // 2
    n_taps = conv_value.shape[0] - 1
    n_edge = n_taps - 1
    inner_all = inner_loc * lax.axis_size("head")
    r = lax.rsqrt(jnp.mean(x * x, axis=1, keepdims=True) + eps)
    normed = (x * r * norm_gain).astype(jnp.bfloat16)
    z = jnp.dot(normed, w_gate, preferred_element_type=jnp.float32)
    x_val = jnp.dot(normed, w_value, preferred_element_type=jnp.float32)
    b_c = jnp.dot(normed, w_bc, preferred_element_type=jnp.float32)
    step_raw = jnp.dot(normed, w_step, preferred_element_type=jnp.float32)
    conv_in = jnp.concatenate([x_val, b_c], axis=1)
    edge_in, doc_edge = from_behind(
        (conv_in[tokens - n_edge :], (doc_row[tokens - 1 :] + 1).astype(jnp.float32)), "seq", 1
    )
    doc_before = doc_edge[0].astype(jnp.int32) - 1
    conv_ext = jnp.concatenate([edge_in, conv_in], axis=0)
    keep_dev = (doc_row == doc_before).astype(jnp.float32)

    def local_mix(ext_in, conv_v, conv_b, raw_step, bias_dt, log_rate, skip_gain):
        taps_all = jnp.concatenate([conv_v, conv_b], axis=1)
        conv_pre = taps_all[n_taps][None, :] + taps_all[0] * ext_in[n_edge : n_edge + tokens]
        for offset in range(1, n_taps):
            conv_pre = (
                conv_pre + taps_all[offset] * ext_in[n_edge - offset : n_edge - offset + tokens]
            )
        u = jax.nn.silu(conv_pre)
        x_heads = u[:, :inner_loc].reshape(tokens, heads_loc, head_dim)
        b_mat = u[:, inner_loc : inner_loc + state_dim]
        c_mat = u[:, inner_loc + state_dim :]
        step_size = jax.nn.softplus(raw_step + bias_dt)
        log_decay = -jnp.exp(log_rate) * step_size
        n_blocks = tokens // BLOCK
        blocks = (
            x_heads.reshape(n_blocks, BLOCK, heads_loc, head_dim),
            b_mat.reshape(n_blocks, BLOCK, state_dim),
            c_mat.reshape(n_blocks, BLOCK, state_dim),
            step_size.reshape(n_blocks, BLOCK, heads_loc),
            log_decay.reshape(n_blocks, BLOCK, heads_loc),
            doc_row.reshape(n_blocks, BLOCK),
        )
        init_carry = (jnp.zeros((heads_loc, head_dim, state_dim), jnp.float32), doc_before)
        final_carry, block_ys = lax.scan(ssd_block, init_carry, blocks)
        y_local = block_ys.reshape(tokens, heads_loc, head_dim) + skip_gain[None, :, None] * x_heads
        cum_dev = jnp.cumsum(log_decay, axis=0)
        carry_all = jnp.exp(cum_dev[tokens - 1]) * (doc_row[tokens - 1] == doc_before).astype(
            jnp.float32
        )
        return (y_local, final_carry[0], carry_all, c_mat, cum_dev)

    def correct(c_mat, cum_dev, state_in):
        return (
            jnp.einsum("tn,hpn->thp", c_mat, state_in, precision=HIGHEST)
            * (jnp.exp(cum_dev) * keep_dev[:, None])[:, :, None]
        )

    (y_local, state_end, carry_all, c_mat, cum_dev), local_pull = jax.vjp(
        local_mix, conv_ext, conv_value, conv_bc, step_raw, dt_bias, a_log, d_skip
    )
    carry_in, state_in = prefix(
        (carry_all, state_end),
        "seq",
        chain_combine,
        (jnp.ones_like(carry_all), jnp.zeros_like(state_end)),
    )
    y_corr, correct_pull = jax.vjp(correct, c_mat, cum_dev, state_in)
    y = (y_local + y_corr).reshape(tokens, inner_loc)
    gate_sig = jax.nn.sigmoid(z)
    gate_act = z * gate_sig
    g = y * gate_act
    sq_sum = lax.psum(jnp.sum(g * g, axis=1), "head")
    r_out = lax.rsqrt(sq_sum / inner_all + eps)[:, None]
    gated = (g * r_out * out_gain).astype(jnp.bfloat16)
    out_terms = jnp.dot(gated, w_out, preferred_element_type=jnp.float32)
    out_cols = lax.psum_scatter(
        out_terms.astype(jnp.bfloat16), "head", scatter_dimension=1, tiled=True
    ).astype(jnp.float32)
    width = out_cols.shape[1]
    residual = lax.dynamic_slice_in_dim(x, lax.axis_index("head") * width, width, 1)
    block_out = (residual + out_cols).astype(jnp.bfloat16)[None]
    cot_full = lax.all_gather(cotangent[0], "head", axis=1, tiled=True)
    g_w_out = jnp.einsum("ti,td->id", gated, cot_full, preferred_element_type=jnp.float32)
    d_gated = jnp.einsum("td,id->ti", cot_full, w_out, preferred_element_type=jnp.float32)
    q = d_gated * out_gain
    g_out_gain = jnp.sum(d_gated * g * r_out, axis=0)
    dot_sum = lax.psum(jnp.sum(q * g, axis=1), "head")
    d_g = r_out * q - g * r_out**3 * dot_sum[:, None] / inner_all
    d_y = (d_g * gate_act).reshape(tokens, heads_loc, head_dim)
    d_z = (d_g * y * gate_sig * (1.0 + z * (1.0 - gate_sig))).astype(jnp.bfloat16)
    d_cmat, d_cum, g_state = correct_pull(d_y)
    carry_back, state_grad = prefix_2(
        (carry_all, g_state),
        "seq",
        chain_combine,
        (jnp.ones_like(carry_all), jnp.zeros_like(g_state)),
    )
    d_carry = jnp.sum(state_grad * state_in, axis=(1, 2))
    d_ext, g_conv_value, g_conv_bc, d_step_f, g_dt_bias, g_a_log, g_d_skip = local_pull(
        (d_y, state_grad, d_carry, d_cmat, d_cum)
    )
    d_bc_ext, g_conv_bc = lax.psum((d_ext[:, inner_loc:], g_conv_bc), "head")
    d_ext = jnp.concatenate([d_ext[:, :inner_loc], d_bc_ext], axis=1)
    edge_back = from_behind(d_ext[:n_edge], "seq", -1)
    d_conv = d_ext[n_edge:]
    d_conv = jnp.concatenate(
        [d_conv[: tokens - n_edge], d_conv[tokens - n_edge :] + edge_back], axis=0
    )
    d_val = d_conv[:, :inner_loc].astype(jnp.bfloat16)
    d_bcm = d_conv[:, inner_loc:].astype(jnp.bfloat16)
    d_step = d_step_f.astype(jnp.bfloat16)
    g_w_gate = jnp.einsum("td,tc->dc", normed, d_z, preferred_element_type=jnp.float32)
    g_w_value = jnp.einsum("td,tc->dc", normed, d_val, preferred_element_type=jnp.float32)
    g_w_bc = jnp.einsum("td,tc->dc", normed, d_bcm, preferred_element_type=jnp.float32)
    g_w_step = jnp.einsum("td,tc->dc", normed, d_step, preferred_element_type=jnp.float32)
    d_part = jnp.einsum("tc,dc->td", d_z, w_gate, preferred_element_type=jnp.float32)
    d_part = d_part + jnp.einsum("tc,dc->td", d_val, w_value, preferred_element_type=jnp.float32)
    d_part = d_part + jnp.einsum("tc,dc->td", d_step, w_step, preferred_element_type=jnp.float32)
    d_normed = lax.psum(d_part.astype(jnp.bfloat16), "head").astype(jnp.float32) + jnp.einsum(
        "tc,dc->td", d_bcm, w_bc, preferred_element_type=jnp.float32
    )
    g_norm_gain = jnp.sum(d_normed * x * r, axis=0)
    q_norm = d_normed * norm_gain
    d_x = r * q_norm - x * r**3 * jnp.mean(q_norm * x, axis=1, keepdims=True)
    grad_in = (d_x + cot_full.astype(jnp.float32)).astype(jnp.bfloat16)[None]
    (
        g_norm_gain,
        g_w_gate,
        g_w_value,
        g_w_bc,
        g_w_step,
        g_conv_value,
        g_conv_bc,
        g_dt_bias,
        g_a_log,
        g_d_skip,
        g_out_gain,
        g_w_out,
    ) = lax.psum(
        (
            g_norm_gain,
            g_w_gate,
            g_w_value,
            g_w_bc,
            g_w_step,
            g_conv_value,
            g_conv_bc,
            g_dt_bias,
            g_a_log,
            g_d_skip,
            g_out_gain,
            g_w_out,
        ),
        ("seq", "dp"),
    )
    return (
        block_out,
        grad_in,
        g_norm_gain,
        g_w_gate,
        g_w_value,
        g_w_bc,
        g_w_step,
        g_conv_value,
        g_conv_bc,
        g_dt_bias,
        g_a_log,
        g_d_skip,
        g_out_gain,
        g_w_out,
    )


def solution(mesh):
    return jax.shard_map(
        on_device,
        mesh=mesh,
        in_specs=(
            P("dp", "seq", None),
            P("dp", "seq"),
            P(),
            P(None, "head"),
            P(None, "head"),
            P(),
            P(None, "head"),
            P(None, "head"),
            P(),
            P("head"),
            P("head"),
            P("head"),
            P("head"),
            P("head", None),
            P("dp", "seq", "head"),
        ),
        out_specs=(
            P("dp", "seq", "head"),
            P("dp", "seq", None),
            P(),
            P(None, "head"),
            P(None, "head"),
            P(),
            P(None, "head"),
            P(None, "head"),
            P(),
            P("head"),
            P("head"),
            P("head"),
            P("head"),
            P("head", None),
        ),
        check_vma=False,
    )
```

profile of v0, /device:TPU:0, one launch (start us, length us, event | category | flops | bytes accessed | tf_op | source)
XLA Modules:
  0.0 1185.3 jit_solution(17180875239085954251)
XLA Ops:
  16.4 5.7 collective-permute-start.1
  23.3 6.7 collective-permute-start
  39.1 9.1 all-gather.3
  52.3 6.5 fusion.131
  77.0 242.0 %while.114 = (s32[]{:T(128)}, f32[8,64,128]{2,1,0:T(8,128)S(1)}, s32[]{:T(128)}, f32[6,256,8,64]{1,0,3,2:T(8,128)}, pred[6,256,256,8]{2,3,1,0:T(8,128)(4,1)}, /*...) while((s32[]{:T(128)}, f32[8,64,128]{2,1,0:T(8,128)S(1)}, ...), condition=%wide.region_4.5_spmd.clone, body=%wide.region_1.4_spmd.clone.sunk | while | flops 912533568 | bytes 18610864 | solution.py:165
  96.6 12.7 %dynamic_update_slice.292 = f32[6,256,8,64]{1,0,3,2:T(8,128)} dynamic-update-slice(f32[6,256,8,64]{1,0,3,2:T(8,128)} %get-tuple-element.2538, f32[1,256,8,64]{1,0,3,2:T(1,128)S(1)} %copy.343, s32[]{:T(128)} %get-tuple-element.2535, s32[]{:T(128)} %constant.267.clone.1..sunk.2, s32[]{:T(128)} %constant.267.clone.1..sunk.2, s32[]{:T(128)} %constant.267.clone.1..sunk.2) | dynamic-update-slice | bytes 1048580 | tf_op jit(solution)/shard_map/jvp()/while/body/jit(dynamic_update_index_in_dim)/dynamic_update_slice | solution.py:165
  136.9 12.7 %dynamic_update_slice.292 = f32[6,256,8,64]{1,0,3,2:T(8,128)} dynamic-update-slice(f32[6,256,8,64]{1,0,3,2:T(8,128)} %get-tuple-element.2538, f32[1,256,8,64]{1,0,3,2:T(1,128)S(1)} %copy.343, s32[]{:T(128)} %get-tuple-element.2535, s32[]{:T(128)} %constant.267.clone.1..sunk.2, s32[]{:T(128)} %constant.267.clone.1..sunk.2, s32[]{:T(128)} %constant.267.clone.1..sunk.2) | dynamic-update-slice | bytes 1048580 | tf_op jit(solution)/shard_map/jvp()/while/body/jit(dynamic_update_index_in_dim)/dynamic_update_slice | solution.py:165
  177.1 12.7 %dynamic_update_slice.292 = f32[6,256,8,64]{1,0,3,2:T(8,128)} dynamic-update-slice(f32[6,256,8,64]{1,0,3,2:T(8,128)} %get-tuple-element.2538, f32[1,256,8,64]{1,0,3,2:T(1,128)S(1)} %copy.343, s32[]{:T(128)} %get-tuple-element.2535, s32[]{:T(128)} %constant.267.clone.1..sunk.2, s32[]{:T(128)} %constant.267.clone.1..sunk.2, s32[]{:T(128)} %constant.267.clone.1..sunk.2) | dynamic-update-slice | bytes 1048580 | tf_op jit(solution)/shard_map/jvp()/while/body/jit(dynamic_update_index_in_dim)/dynamic_update_slice | solution.py:165
  217.4 12.7 %dynamic_update_slice.292 = f32[6,256,8,64]{1,0,3,2:T(8,128)} dynamic-update-slice(f32[6,256,8,64]{1,0,3,2:T(8,128)} %get-tuple-element.2538, f32[1,256,8,64]{1,0,3,2:T(1,128)S(1)} %copy.343, s32[]{:T(128)} %get-tuple-element.2535, s32[]{:T(128)} %constant.267.clone.1..sunk.2, s32[]{:T(128)} %constant.267.clone.1..sunk.2, s32[]{:T(128)} %constant.267.clone.1..sunk.2) | dynamic-update-slice | bytes 1048580 | tf_op jit(solution)/shard_map/jvp()/while/body/jit(dynamic_update_index_in_dim)/dynamic_update_slice | solution.py:165
  257.7 12.7 %dynamic_update_slice.292 = f32[6,256,8,64]{1,0,3,2:T(8,128)} dynamic-update-slice(f32[6,256,8,64]{1,0,3,2:T(8,128)} %get-tuple-element.2538, f32[1,256,8,64]{1,0,3,2:T(1,128)S(1)} %copy.343, s32[]{:T(128)} %get-tuple-element.2535, s32[]{:T(128)} %constant.267.clone.1..sunk.2, s32[]{:T(128)} %constant.267.clone.1..sunk.2, s32[]{:T(128)} %constant.267.clone.1..sunk.2) | dynamic-update-slice | bytes 1048580 | tf_op jit(solution)/shard_map/jvp()/while/body/jit(dynamic_update_index_in_dim)/dynamic_update_slice | solution.py:165
  298.3 12.7 %dynamic_update_slice.292 = f32[6,256,8,64]{1,0,3,2:T(8,128)} dynamic-update-slice(f32[6,256,8,64]{1,0,3,2:T(8,128)} %get-tuple-element.2538, f32[1,256,8,64]{1,0,3,2:T(1,128)S(1)} %copy.343, s32[]{:T(128)} %get-tuple-element.2535, s32[]{:T(128)} %constant.267.clone.1..sunk.2, s32[]{:T(128)} %constant.267.clone.1..sunk.2, s32[]{:T(128)} %constant.267.clone.1..sunk.2) | dynamic-update-slice | bytes 1048580 | tf_op jit(solution)/shard_map/jvp()/while/body/jit(dynamic_update_index_in_dim)/dynamic_update_slice | solution.py:165
  320.2 5.0 reshape.503
  325.2 14.7 %all-gather = bf16[32,64,128]{2,1,0:T(8,128)(2,1)S(1)} all-gather(bf16[8,64,128]{2,1,0:T(8,128)(2,1)S(1)} %convert_element_type.190), channel_id=2, replica_groups=mesh['seq'=4,'head'=4,'dp'=2] {'seq'}, dimensions={0}, use_global_device_ids=true | all-gather | bytes 655360 | tf_op jit(solution)/shard_map/all_gather | solution.py:22
  349.2 5.3 multiply_reduce_fusion.9
  354.5 10.0 psum.119
  364.6 7.1 multiply_reduce_fusion.5
  371.7 8.0 psum.120
  379.8 9.2 multiply_reduce_fusion.6
  398.5 14.7 %all-gather.2 = bf16[32,64,128]{2,1,0:T(8,128)(2,1)S(1)} all-gather(bf16[8,64,128]{2,1,0:T(8,128)(2,1)S(1)} %fusion.158), channel_id=4, replica_groups=mesh['seq'=4,'head'=4,'dp'=2] {'seq'}, dimensions={0}, use_global_device_ids=true | all-gather | bytes 655360 | tf_op jit(solution)/shard_map/all_gather | solution.py:47
  419.2 351.8 %while.113 = (s32[]{:T(128)}, f32[8,64,128]{2,1,0:T(8,128)S(1)}, f32[6,256,8,64]{1,0,3,2:T(8,128)}, f32[6,256,128]{2,1,0:T(8,128)}, f32[6,256,128]{2,1,0:T(8,128...) while((s32[]{:T(128)}, f32[8,64,128]{2,1,0:T(8,128)S(1)}, ...), condition=%wide.region_26.27_spmd, body=%wide.region_16.26_spmd.sunk | while | flops 1819299840 | bytes 41175448 | solution.py:165
  430.2 6.1 fusion.272
  463.0 12.7 %dynamic_update_slice.279 = f32[6,256,8,64]{1,0,3,2:T(8,128)} dynamic-update-slice(f32[6,256,8,64]{1,0,3,2:T(8,128)} %get-tuple-element.2689, f32[1,256,8,64]{1,0,3,2:T(1,128)S(1)} %copy.340, s32[]{:T(128)S(6)} %sub.231, s32[]{:T(128)} %constant.267.clone.1..sunk.1, s32[]{:T(128)} %constant.267.clone.1..sunk.1, s32[]{:T(128)} %constant.267.clone.1..sunk.1) | dynamic-update-slice | bytes 1048580 | tf_op jit(solution)/shard_map/transpose(jvp())/while/body/jit(dynamic_update_index_in_dim)/dynamic_update_slice | solution.py:165
  488.8 6.1 fusion.272
  521.6 12.7 %dynamic_update_slice.279 = f32[6,256,8,64]{1,0,3,2:T(8,128)} dynamic-update-slice(f32[6,256,8,64]{1,0,3,2:T(8,128)} %get-tuple-element.2689, f32[1,256,8,64]{1,0,3,2:T(1,128)S(1)} %copy.340, s32[]{:T(128)S(6)} %sub.231, s32[]{:T(128)} %constant.267.clone.1..sunk.1, s32[]{:T(128)} %constant.267.clone.1..sunk.1, s32[]{:T(128)} %constant.267.clone.1..sunk.1) | dynamic-update-slice | bytes 1048580 | tf_op jit(solution)/shard_map/transpose(jvp())/while/body/jit(dynamic_update_index_in_dim)/dynamic_update_slice | solution.py:165
  547.5 6.1 fusion.272
  580.2 12.7 %dynamic_update_slice.279 = f32[6,256,8,64]{1,0,3,2:T(8,128)} dynamic-update-slice(f32[6,256,8,64]{1,0,3,2:T(8,128)} %get-tuple-element.2689, f32[1,256,8,64]{1,0,3,2:T(1,128)S(1)} %copy.340, s32[]{:T(128)S(6)} %sub.231, s32[]{:T(128)} %constant.267.clone.1..sunk.1, s32[]{:T(128)} %constant.267.clone.1..sunk.1, s32[]{:T(128)} %constant.267.clone.1..sunk.1) | dynamic-update-slice | bytes 1048580 | tf_op jit(solution)/shard_map/transpose(jvp())/while/body/jit(dynamic_update_index_in_dim)/dynamic_update_slice | solution.py:165
  606.0 6.1 fusion.272
  638.8 12.7 %dynamic_update_slice.279 = f32[6,256,8,64]{1,0,3,2:T(8,128)} dynamic-update-slice(f32[6,256,8,64]{1,0,3,2:T(8,128)} %get-tuple-element.2689, f32[1,256,8,64]{1,0,3,2:T(1,128)S(1)} %copy.340, s32[]{:T(128)S(6)} %sub.231, s32[]{:T(128)} %constant.267.clone.1..sunk.1, s32[]{:T(128)} %constant.267.clone.1..sunk.1, s32[]{:T(128)} %constant.267.clone.1..sunk.1) | dynamic-update-slice | bytes 1048580 | tf_op jit(solution)/shard_map/transpose(jvp())/while/body/jit(dynamic_update_index_in_dim)/dynamic_update_slice | solution.py:165
  664.6 6.1 fusion.272
  697.3 12.7 %dynamic_update_slice.279 = f32[6,256,8,64]{1,0,3,2:T(8,128)} dynamic-update-slice(f32[6,256,8,64]{1,0,3,2:T(8,128)} %get-tuple-element.2689, f32[1,256,8,64]{1,0,3,2:T(1,128)S(1)} %copy.340, s32[]{:T(128)S(6)} %sub.231, s32[]{:T(128)} %constant.267.clone.1..sunk.1, s32[]{:T(128)} %constant.267.clone.1..sunk.1, s32[]{:T(128)} %constant.267.clone.1..sunk.1) | dynamic-update-slice | bytes 1048580 | tf_op jit(solution)/shard_map/transpose(jvp())/while/body/jit(dynamic_update_index_in_dim)/dynamic_update_slice | solution.py:165
  723.1 6.1 fusion.272
  755.9 12.7 %dynamic_update_slice.279 = f32[6,256,8,64]{1,0,3,2:T(8,128)} dynamic-update-slice(f32[6,256,8,64]{1,0,3,2:T(8,128)} %get-tuple-element.2689, f32[1,256,8,64]{1,0,3,2:T(1,128)S(1)} %copy.340, s32[]{:T(128)S(6)} %sub.231, s32[]{:T(128)} %constant.267.clone.1..sunk.1, s32[]{:T(128)} %constant.267.clone.1..sunk.1, s32[]{:T(128)} %constant.267.clone.1..sunk.1) | dynamic-update-slice | bytes 1048580 | tf_op jit(solution)/shard_map/transpose(jvp())/while/body/jit(dynamic_update_index_in_dim)/dynamic_update_slice | solution.py:165
  772.5 5.0 fusion.148
  781.8 5.1 multiply_add_fusion.1
  788.2 9.7 multiply_reduce_fusion.4
  810.0 5.5 convolution_convert_fusion
  815.6 9.0 pad_add_fusion
  830.7 9.9 reduce-window.62
  849.5 22.5 %all-reduce.21.cloned.1.call-done = f32[1539,256]{0,1:T(8,128)} async-done(((f32[1539,256]{0,1:T(8,128)}), f32[1539,256]{0,1:T(8,128)}) %all-reduce.21.cloned.1.call-update) | async-done | bytes 1575952 | tf_op jit(solution)/shard_map/psum | solution.py:223
  875.7 10.3 collective-permute-done.2
  892.5 5.9 fusion.196
  908.9 5.3 convert_element_type.182
  914.5 9.1 psum.129
  929.4 79.8 %all-reduce.23.cloned.1.call-done = bf16[1536,1024]{1,0:T(8,128)(2,1)} async-done(((bf16[1536,1024]{1,0:T(8,128)(2,1)}), bf16[1536,1024]{1,0:T(8,128)(2,1)}) %all-reduce.23.cloned.1.call-update) | async-done | bytes 3145744 | tf_op jit(solution)/shard_map/psum | solution.py:240
  1009.3 6.2 fusion.127
  1015.4 31.5 %all-reduce.15 = (f32[1024]{0:T(1024)}, f32[1024,8]{0,1:T(8,128)}, f32[5,512]{1,0:T(8,128)}, f32[5,256]{1,0:T(8,128)}, f32[8]{0:T(128)}, /*index=5*/f32[8]{0:T(128)}, f32[8]{0:T(128)}, f32[512]{0:T(512)}) all-reduce(f32[1024]{0:T(1024)S(1)} %get-tuple-element.1769, ...), channel_id=1, replica_groups=mesh['seq'=4,'head'=4,'dp'=2] {'seq','dp'}, use_global_device_ids=true, to_apply=%region_35.36 | all-reduce | flops 13592 | bytes 108736 | tf_op jit(solution)/shard_map/psum | solution.py:260
  1047.0 6.9 fusion.132
  1053.9 117.2 %all-reduce.25.cloned.1.call-done = (f32[1024,512]{1,0:T(8,128)}, f32[1024,512]{1,0:T(8,128)}, f32[1024,256]{1,0:T(8,128)}, f32[512,1024]{1,0:T(8,128)}) async-done(((f32[1024,512]{1,0:T(8,128)}, f32[1024,512]{1,0:T(8,128)}, f32[1024,256]{1,0:T(8,128)}, f32[512,1024]{1,0:T(8,128)}), (f32[1024,512]{1,0:T(8,128)}, f32[1024,512]{1,0:T(8,128)}, f32[1024,256]{1,0:T(8,128)}, ...) | async-done | bytes 7340048 | tf_op jit(solution)/shard_map/psum | solution.py:260
  (711 shorter events, 530.0 us)
Async XLA Ops:
  7.2 342.0 %copy-start = (bf16[1024,512]{1,0:T(8,128)(2,1)S(1)}, bf16[1024,512]{1,0:T(8,128)(2,1)}, u32[]{:S(2)}) copy-start(bf16[1024,512]{1,0:T(8,128)(2,1)} %param.26) | copy-start | bytes 3145732
  7.2 357.4 %all-gather.6.cloned.1.call-start = ((), (), s32[]{:S(2)}) async-start(), calls=%async_computation.4 | async-start | bytes 3932160 | tf_op jit(solution)/shard_map/all_gather | solution.py:203
  15.5 36.8 %copy-start.17 = (f32[1536,256]{0,1:T(8,128)}, f32[1536,256]{0,1:T(8,128)S(1)}, u32[]{:S(2)}) copy-start(f32[1536,256]{0,1:T(8,128)S(1)} %fusion.194) | copy-start | bytes 4718596
  15.5 6.6 copy-start.61
  15.5 14.9 %copy-start.62 = (f32[5,512]{1,0:T(8,128)S(1)}, f32[5,512]{1,0:T(8,128)}, u32[]{:S(2)}) copy-start(f32[5,512]{1,0:T(8,128)} %param.30) | copy-start | bytes 30724
  15.5 14.9 %copy-start.69 = (f32[5,256]{1,0:T(8,128)S(1)}, f32[5,256]{1,0:T(8,128)}, u32[]{:S(2)}) copy-start(f32[5,256]{1,0:T(8,128)} %param.31) | copy-start | bytes 15364
  15.5 14.9 %copy-start.81 = (f32[8]{0:T(128)S(1)}, f32[8]{0:T(128)}, u32[]{:S(2)}) copy-start(f32[8]{0:T(128)} %param.33) | copy-start | bytes 100
  15.5 15.6 %copy-start.52 = (bf16[1024,8]{0,1:T(8,128)(2,1)S(1)}, bf16[1024,8]{0,1:T(8,128)(2,1)}, u32[]{:S(2)}) copy-start(bf16[1024,8]{0,1:T(8,128)(2,1)} %param.29) | copy-start | bytes 49156
  15.5 15.6 %copy-start.72 = (f32[8]{0:T(128)S(1)}, f32[8]{0:T(128)}, u32[]{:S(2)}) copy-start(f32[8]{0:T(128)} %param.32) | copy-start | bytes 100
  16.4 32.4 %collective-permute-start.1 = (f32[3,768]{0,1:T(8,128)}, f32[3,768]{0,1:T(8,128)}, u32[]{:S(2)}, u32[]{:S(2)}) collective-permute-start(f32[3,768]{0,1:T(8,128)} %fusion.165), channel_id=1, source_target_pairs={{0,8},{8,16},{16,24},{1,9},{9,17},{17,25},{2,10},{10,18},{18,26},{... | collective-permute-start | bytes 27656 | tf_op jit(solution)/shard_map/ppermute | solution.py:16
  23.3 14.2 %collective-permute-start = (f32[1]{0:T(128)}, f32[1]{0:T(128)}, u32[]{:S(2)}, u32[]{:S(2)}) collective-permute-start(f32[1]{0:T(128)} %bitcast.47), channel_id=1, source_target_pairs={{0,8},{8,16},{16,24},{1,9},{9,17},{17,25},{2,10},{10,18},{18,26},{... | collective-permute-start | bytes 20 | tf_op jit(solution)/shard_map/ppermute | solution.py:16
  30.1 6.7 copy-start.73
  30.1 841.9 %all-reduce.21.cloned.1.call-start = ((), (), s32[]{:S(2)}) async-start(), calls=%async_computation.2 | async-start | bytes 3407872 | tf_op jit(solution)/shard_map/psum | solution.py:223
  30.4 21.9 %copy-start.54 = (f32[768]{0:T(1024)}, f32[768]{0:T(1024)S(1)}, u32[]{:S(2)}) copy-start(f32[768]{0:T(1024)S(1)} %get-tuple-element.1778) | copy-start | bytes 9220
  30.4 21.9 %copy-start.56 = (f32[768]{0:T(1024)}, f32[768]{0:T(1024)S(1)}, u32[]{:S(2)}) copy-start(f32[768]{0:T(1024)S(1)} %get-tuple-element.1779) | copy-start | bytes 9220
  33.9 18.4 %copy-start.38 = (f32[1536,8]{0,1:T(8,128)}, f32[1536,8]{0,1:T(8,128)S(1)}, u32[]{:S(2)}) copy-start(f32[1536,8]{0,1:T(8,128)S(1)} %get-tuple-element.1989) | copy-start | bytes 147460
  38.2 14.1 %copy-start.49 = (f32[1536]{0:T(1024)}, f32[1536]{0:T(1024)S(1)}, u32[]{:S(2)}) copy-start(f32[1536]{0:T(1024)S(1)} %fusion.182) | copy-start | bytes 18436
  38.9 13.4 %copy-start.40 = (f32[1536,8]{0,1:T(8,128)}, f32[1536,8]{0,1:T(8,128)S(1)}, u32[]{:S(2)}) copy-start(f32[1536,8]{0,1:T(8,128)S(1)} %get-tuple-element.1954) | copy-start | bytes 147460
  38.9 354.8 %copy-start.34 = (f32[1536,8]{0,1:T(8,128)}, f32[1536,8]{0,1:T(8,128)S(1)}, u32[]{:S(2)}) copy-start(f32[1536,8]{0,1:T(8,128)S(1)} %get-tuple-element.1953) | copy-start | bytes 147460
  52.3 6.5 copy-start.1
  320.2 19.7 %copy-start.76 = (bf16[4,1,8]{2,0,1:T(4,128)(2,1)S(1)}, bf16[4,1,8]{2,0,1:T(4,128)(2,1)}, u32[]{:S(2)}) copy-start(bf16[4,1,8]{2,0,1:T(4,128)(2,1)} %copy.318) | copy-start | bytes 196
  349.2 15.4 %copy-start.70 = (f32[512]{0:T(512)S(1)}, f32[512]{0:T(512)}, u32[]{:S(2)}) copy-start(f32[512]{0:T(512)} %param.35) | copy-start | bytes 6148
  349.2 15.4 %copy-start.77 = (bf16[512,1024]{1,0:T(8,128)(2,1)S(1)}, bf16[512,1024]{1,0:T(8,128)(2,1)}, u32[]{:S(2)}) copy-start(bf16[512,1024]{1,0:T(8,128)(2,1)} %param.36) | copy-start | bytes 3145732
  364.5 15.2 %copy-start.59 = (f32[1536]{0:T(1024)}, f32[1536]{0:T(1024)S(1)}, u32[]{:S(2)}) copy-start(f32[1536]{0:T(1024)S(1)} %get-tuple-element.1988) | copy-start | bytes 18436
  419.2 353.3 %copy-start.35 = (f32[1536,8]{0,1:T(8,128)S(1)}, f32[1536,8]{0,1:T(8,128)}, u32[]{:S(2)}) copy-start(f32[1536,8]{0,1:T(8,128)} %copy-done.34) | copy-start | bytes 147460
  788.2 9.7 copy-start.55
  788.2 9.7 copy-start.57
  810.0 116.2 %reduce-scatter.2.cloned.1.call-start = ((), (), s32[]{:S(2)}) async-start(), calls=%async_computation.1 | async-start | bytes 3932160 | tf_op jit(solution)/shard_map/reduce_scatter | solution.py:197
  815.6 193.7 %all-reduce.23.cloned.1.call-start = ((), (), s32[]{:S(2)}) async-start(), calls=%async_computation.3 | async-start | bytes 6291456 | tf_op jit(solution)/shard_map/psum | solution.py:240
  827.0 14.1 %copy-start.39 = (f32[1536,8]{0,1:T(8,128)S(1)}, f32[1536,8]{0,1:T(8,128)}, u32[]{:S(2)}) copy-start(f32[1536,8]{0,1:T(8,128)} %copy-done.38) | copy-start | bytes 147460
  827.0 14.1 %copy-start.42 = (f32[6,256,8]{1,2,0:T(8,128)S(1)}, f32[6,256,8]{1,2,0:T(8,128)}, u32[]{:S(2)}) copy-start(f32[6,256,8]{1,2,0:T(8,128)} %get-tuple-element.1335) | copy-start | bytes 147460
  827.0 14.1 %copy-start.43 = (f32[6,256,8]{1,2,0:T(8,128)S(1)}, f32[6,256,8]{1,2,0:T(8,128)}, u32[]{:S(2)}) copy-start(f32[6,256,8]{1,2,0:T(8,128)} %get-tuple-element.1336) | copy-start | bytes 147460
  827.0 14.1 %copy-start.66 = (f32[8]{0:T(128)S(1)}, f32[8]{0:T(128)}, u32[]{:S(2)}) copy-start(f32[8]{0:T(128)} %copy-done.65) | copy-start | bytes 100
  827.0 14.3 %copy-start.53 = (bf16[1024,8]{0,1:T(8,128)(2,1)S(1)}, bf16[1024,8]{0,1:T(8,128)(2,1)}, u32[]{:S(2)}) copy-start(bf16[1024,8]{0,1:T(8,128)(2,1)} %param.29) | copy-start | bytes 49156
  873.2 12.9 %collective-permute-start.2 = (f32[3,768]{0,1:T(8,128)S(1)}, f32[3,768]{0,1:T(8,128)S(1)}, u32[]{:S(2)}, u32[]{:S(2)}) collective-permute-start(f32[3,768]{0,1:T(8,128)S(1)} %pad_maximum_fusion.1), channel_id=1, source_target_pairs={{8,0},{16,8},{24,16},{9,1},{17,9},{25,17},{10,2},{18,10},{26,18},{... | collective-permute-start | bytes 27656 | tf_op jit(solution)/shard_map/ppermute | solution.py:16
  874.6 13.9 %slice-start.2 = ((s8[6291456]{0:T(1024)(128)(4,1)}), s8[4194304]{0:T(1024)(128)(4,1)S(1)}, s32[]{:S(2)}) async-start(s8[6291456]{0:T(1024)(128)(4,1)} %bitcast.589), calls=%async_computation.8 | async-start | bytes 8388608
  874.6 13.8 %slice-start.4 = ((s8[6291456]{0:T(1024)(128)(4,1)}), s8[4194304]{0:T(1024)(128)(4,1)S(1)}, s32[]{:S(2)}) async-start(s8[6291456]{0:T(1024)(128)(4,1)} %bitcast.593), calls=%async_computation.10 | async-start | bytes 8388608
  875.7 12.8 %slice-start.3 = ((s8[6291456]{0:T(1024)(128)(4,1)}), s8[2097152]{0:T(1024)(128)(4,1)S(1)}, s32[]{:S(2)}) async-start(s8[6291456]{0:T(1024)(128)(4,1)} %bitcast.589), calls=%async_computation.9 | async-start | bytes 4194304
  875.7 12.8 %slice-start.5 = ((s8[6291456]{0:T(1024)(128)(4,1)}), s8[2097152]{0:T(1024)(128)(4,1)S(1)}, s32[]{:S(2)}) async-start(s8[6291456]{0:T(1024)(128)(4,1)} %bitcast.593), calls=%async_computation.11 | async-start | bytes 4194304
  892.2 278.9 %all-reduce.25.cloned.1.call-start = ((), (), s32[]{:S(2)}) async-start(), calls=%async_computation.5 | async-start | bytes 14680064 | tf_op jit(solution)/shard_map/psum | solution.py:260
  908.9 14.7 %copy-start.82 = (f32[8]{0:T(128)S(1)}, f32[8]{0:T(128)}, u32[]{:S(2)}) copy-start(f32[8]{0:T(128)} %param.33) | copy-start | bytes 100
  914.3 15.2 %copy-start.51 = (f32[5,768]{1,0:T(8,128)}, f32[5,768]{1,0:T(8,128)S(1)}, u32[]{:S(2)}) copy-start(f32[5,768]{1,0:T(8,128)S(1)} %pad_add_fusion.2) | copy-start | bytes 46084
  923.6 85.6 %copy-start.37 = (bf16[1536,256]{0,1:T(8,128)(2,1)S(1)}, bf16[1536,256]{0,1:T(8,128)(2,1)}, u32[]{:S(2)}) copy-start(bf16[1536,256]{0,1:T(8,128)(2,1)} %copy-done.36) | copy-start | bytes 2359300
  923.7 85.6 %copy-start.48 = (f32[1536]{0:T(1024)S(1)}, f32[1536]{0:T(1024)}, u32[]{:S(2)}) copy-start(f32[1536]{0:T(1024)} %copy-done.47) | copy-start | bytes 18436
  923.7 85.6 %copy-start.64 = (f32[1024]{0:T(1024)S(1)}, f32[1024]{0:T(1024)}, u32[]{:S(2)}) copy-start(f32[1024]{0:T(1024)} %param.25) | copy-start | bytes 12292
  923.7 85.6 %copy-start.80 = (bf16[1024,256]{1,0:T(8,128)(2,1)S(1)}, bf16[1024,256]{1,0:T(8,128)(2,1)}, u32[]{:S(2)}) copy-start(bf16[1024,256]{1,0:T(8,128)(2,1)} %param.28) | copy-start | bytes 1572868
  929.4 86.0 %copy-start.75 = (f32[512]{0:T(512)S(1)}, f32[512]{0:T(512)}, u32[]{:S(2)}) copy-start(f32[512]{0:T(512)} %get-tuple-element.1771) | copy-start | bytes 6148
  929.4 117.5 %copy-start.58 = (f32[1536]{0:T(1024)S(1)}, f32[1536]{0:T(1024)}, u32[]{:S(2)}) copy-start(f32[1536]{0:T(1024)} %get-tuple-element.1985) | copy-start | bytes 18436
  (52 other events, 177.7 us)
Sparse Core Ops, SparseCore 0:
  30.2 44.0 all-gather.5
  810.1 61.8 all-reduce.20
  875.0 43.9 reduce-scatter.1
  921.9 87.3 all-reduce.22
  1013.0 157.9 all-reduce.24
where the time goes:
time: 1200 us; the launch traced here: 1190 us
  local copies, waits for them, and re-layouts  354 us (30%)
  matrix products  246 us (20%)
  waiting for transfers between devices  230 us (19%)
  other arithmetic  217 us (18%)
  blocking collectives  97.2 us (8%)
  between operations  17.3 us (1%)
  starting transfers between devices  14.2 us (1%)
    dynamic_update_slice x54, local copies, waits for them, and re-layouts, local_mix(): final_carry, block_ys = lax.scan(ssd_block, init_carry, blocks)  173 us
    psum x1, waiting for transfers between devices, on_device(): lax.psum((g_norm_gain, g_w_gate, g_w_value, g_w_bc, g_w_step, g_conv_valu...  117 us
    dynamic_slice x54, local copies, waits for them, and re-layouts, local_mix(): final_carry, block_ys = lax.scan(ssd_block, init_carry, blocks)  80.7 us
    psum x1, waiting for transfers between devices, on_device(): lax.psum(d_part.astype(jnp.bfloat16), 'head').astype(jnp.float32)  79.8 us
    dynamic_update_slice x48, other arithmetic, local_mix(): final_carry, block_ys = lax.scan(ssd_block, init_carry, blocks)  70.9 us
    dot_general x18, matrix products, ssd_block(): y_intra = jnp.einsum('tsh,shp->thp', mixing, x_heads, precision=HIGHEST)  69.8 us
    dot_general x18, matrix products, ssd_block(): scores = jnp.einsum('tn,sn->ts', c_mat, b_mat, precision=HIGHEST)  36.9 us
    another operation x47, other arithmetic  36.5 us
  transfers between devices with their start and end apart: 8, of which 4 were waited for; matrix products, arithmetic and copies ran while one was open for 31% of the time, Pallas kernels for 0%

commit v1 on v0

v1 whole, which is shorter than its diff:
```python
import functools

import jax
import jax.numpy as jnp
from jax import lax
from jax.experimental import pallas as pl
from jax.experimental.pallas import tpu as pltpu
from jax.sharding import PartitionSpec as P

BLOCK = 256
EDGE = 8
EPS = 1e-05
NEG = -1e30
F32 = jnp.float32
BF16 = jnp.bfloat16
NN = (((1,), (0,)), ((), ()))
NT = (((1,), (1,)), ((), ()))
TN = (((0,), (0,)), ((), ()))
VMEM_LIMIT = 56 * 1024 * 1024


def dot(a, b, dims=NN):
    return lax.dot_general(a, b, dims, preferred_element_type=F32)


def halves(v):
    hi = v.astype(BF16)
    return hi, (v - hi.astype(F32)).astype(BF16)


def dot_left(v, m, dims=NN):
    hi, lo = halves(v)
    return dot(hi, m, dims) + dot(lo, m, dims)


def dot_right(m, v, dims=NN):
    hi, lo = halves(v)
    return dot(m, hi, dims) + dot(m, lo, dims)


def dot3(a, b, dims=NN):
    (ah, al), (bh, bl) = halves(a), halves(b)
    return dot(ah, bh, dims) + (dot(al, bh, dims) + dot(ah, bl, dims))


def score_pair(c, b, first):
    hi, lo = halves(c)
    cc, bb = jnp.concatenate([hi, lo], axis=1), jnp.concatenate([b, b], axis=1)
    return dot(cc, bb, NT) if first else dot(bb, cc, NT)


def sigmoid(v):
    return 1.0 / (1.0 + jnp.exp(-v))


def softplus(v):
    return jnp.maximum(v, 0.0) + jnp.log1p(jnp.exp(-jnp.abs(v)))


def iota(shape, axis):
    return lax.broadcasted_iota(jnp.int32, shape, axis)


def spread_matrix(heads, inner):
    return (iota((heads, inner), 1) // (inner // heads) == iota((heads, inner), 0)).astype(BF16)


def gather_matrix(heads, inner):
    return (iota((inner, heads), 0) // (inner // heads) == iota((inner, heads), 1)).astype(BF16)


def in_norm(x, gain):
    r = lax.rsqrt(jnp.mean(x * x, axis=1, keepdims=True) + EPS)
    return (x * r * gain).astype(BF16)


def conv_forward(ext_ref, start, size, taps):
    n_taps = taps.shape[0] - 1
    pre = taps[n_taps : n_taps + 1, :] + taps[0:1, :] * ext_ref[pl.ds(start + EDGE, size), :]
    for k in range(1, n_taps):
        pre = pre + taps[k : k + 1, :] * ext_ref[pl.ds(start + EDGE - k, size), :]
    return pre


def front_kernel(
    x_ref, halo_ref, gain_ref, wg_ref, wv_ref, wbc_ref, ws_ref, wst_ref, taps_ref, dtb_ref, dtbt_ref,
    rate_ref, ratet_ref, skip_ref, aux_ref, docr_ref,
    normed_ref, z_ref, cin_ref, head_ref, y_ref, c_ref, v_ref, cum_ref, vt_ref, cumt_ref, inc_ref,
    kept_ref, end_ref, carry_ref, ext,
):
    step_id = pl.program_id(0)
    size = x_ref.shape[0]
    inner = wv_ref.shape[1]
    heads = ws_ref.shape[1]
    state = wbc_ref.shape[1] // 2
    gain = gain_ref[...]

    @pl.when(step_id == 0)
    def _():
        edge = in_norm(halo_ref[...].astype(F32), gain)
        rows = edge.shape[0]
        ext[0:EDGE, :inner] = dot(edge, wv_ref[...])[rows - EDGE :]
        ext[0:EDGE, inner:] = dot(edge, wbc_ref[...])[rows - EDGE :]
        head_ref[...] = ext[0:EDGE, :]
        end_ref[...] = jnp.zeros_like(end_ref)
        carry_ref[...] = jnp.ones_like(carry_ref)

    @pl.when(step_id > 0)
    def _():
        ext[0:EDGE, :] = ext[size : size + EDGE, :]

    normed = in_norm(x_ref[...].astype(F32), gain)
    normed_ref[...] = normed
    z_ref[...] = dot(normed, wg_ref[...])
    ext[EDGE:, :inner] = dot(normed, wv_ref[...])
    ext[EDGE:, inner:] = dot(normed, wbc_ref[...])
    cin_ref[...] = ext[EDGE:, :]
    v = dot(normed, ws_ref[...]) + dtb_ref[...]
    vt = dot(wst_ref[...], normed, NT) + dtbt_ref[...]
    pre = conv_forward(ext, 0, size, taps_ref[...])
    u = pre * sigmoid(pre)
    xh = u[:, :inner]
    b_mat, c_full = u[:, inner : inner + state].astype(BF16), u[:, inner + state :]
    step = softplus(v)
    where_t, where_s = iota((size, size), 0), iota((size, size), 1)
    lower = (where_t >= where_s).astype(BF16)
    cum = dot_right(lower, rate_ref[...] * step)
    cumt = dot_left(ratet_ref[...] * softplus(vt), lower, NT)
    doc, last = aux_ref[:, 0:1], aux_ref[:, 2:3]
    mask = jnp.where((where_t >= where_s) & (doc == docr_ref[...]), 0.0, NEG)
    scores = score_pair(c_full, b_mat, True)
    spread = spread_matrix(heads, inner)
    xs = xh * dot_left(step, spread)
    total = cum[size - 1 : size, :]
    to_end = dot_left(jnp.exp(total - cum) * last, spread)
    inc = dot(b_mat, (xs * to_end).astype(BF16), TN)
    kept = dot_left(jnp.exp(total) * aux_ref[0:1, 3:4], spread)
    lanes = 2 * (inner // heads)
    first = iota((size, lanes), 1) < lanes // 2
    xs = xs.astype(BF16)
    parts = []
    for pair in range(heads // 2):
        xp = xs[:, pair * lanes : (pair + 1) * lanes]
        mixed = []
        for h in (2 * pair, 2 * pair + 1):
            decay = jnp.exp(cum[:, h : h + 1] - cumt[h : h + 1, :] + mask)
            mixed.append((scores * decay).astype(BF16))
        both = jnp.concatenate(mixed, axis=1)
        zero = jnp.zeros_like(xp)
        xx = jnp.concatenate([jnp.where(first, xp, zero), jnp.where(first, zero, xp)], axis=0)
        parts.append(dot(both, xx))
    y_ref[...] = jnp.concatenate(parts, axis=1) + skip_ref[...] * xh
    c_ref[...] = c_full
    v_ref[...] = v
    cum_ref[...] = cum
    vt_ref[...] = vt
    cumt_ref[...] = cumt
    inc_ref[0] = inc
    kept_ref[0] = kept
    end_ref[...] = kept * end_ref[...] + inc
    carry_ref[...] = carry_ref[...] * kept


def mid_kernel(
    yi_ref, z_ref, c_ref, cum_ref, aux_ref, cot_ref, w_out_ref, gain_ref, inc_ref, kept_ref, all_ref, weight_ref,
    y_ref, si_ref, dgn_ref, sums_ref, state,
):
    step_id = pl.program_id(0)
    inner = z_ref.shape[1]
    heads = cum_ref.shape[1]

    @pl.when(step_id == 0)
    def _():
        total = jnp.zeros_like(state)
        for k in range(all_ref.shape[0]):
            total = total + weight_ref[k] * all_ref[k].astype(F32)
        state[...] = total

    si = state[...]
    si_ref[0] = si
    state[...] = kept_ref[0] * si + inc_ref[0]
    into = dot_left(jnp.exp(cum_ref[...]) * aux_ref[:, 1:2], spread_matrix(heads, inner))
    y = yi_ref[...] + into * dot3(c_ref[...], si)
    y_ref[...] = y
    z = z_ref[...]
    g = y * (z * sigmoid(z))
    dgn = dot(cot_ref[...], w_out_ref[...], NT)
    dgn_ref[...] = dgn
    ones = jnp.ones((8, inner), BF16)
    sq = dot_right(ones, g * g, NT)
    inn = dot_right(ones, dgn * gain_ref[...] * g, NT)
    sums_ref[0:1, :] = sq[0:1]
    sums_ref[1:2, :] = inn[0:1]


def gate_kernel(
    inner_all, y_ref, z_ref, c_ref, cum_ref, aux_ref, cot_ref, w_out_ref, gain_ref, dgn_ref, sums_ref, kept_ref,
    normed_ref, dy_ref, dz_ref, out_ref, g_out_ref, g_gate_ref, g_gain_ref, g_state_ref, prod,
):
    step_id = pl.program_id(0)
    inner = z_ref.shape[1]
    heads = cum_ref.shape[1]

    @pl.when(step_id == 0)
    def _():
        for ref in (g_out_ref, g_gate_ref, g_gain_ref, g_state_ref):
            ref[...] = jnp.zeros_like(ref)
        prod[...] = jnp.ones_like(prod)

    y, z, dgn, gain = y_ref[...], z_ref[...], dgn_ref[...], gain_ref[...]
    sig = sigmoid(z)
    act = z * sig
    g = y * act
    r = lax.rsqrt(sums_ref[:, 0:1] / inner_all + EPS)
    gr = g * r
    gn = (gr * gain).astype(BF16)
    g_gain_ref[...] += jnp.sum(dgn * gr, axis=0, keepdims=True)
    dg = r * (dgn * gain) - g * (r * r * r * sums_ref[:, 1:2] / inner_all)
    dy = dg * act
    dz = (dg * y * (sig * (1.0 + z * (1.0 - sig)))).astype(BF16)
    dy_ref[...] = dy.astype(BF16)
    dz_ref[...] = dz
    out_ref[...] = dot(gn, w_out_ref[...]).astype(BF16)
    g_out_ref[...] += dot(gn, cot_ref[...], TN)
    g_gate_ref[...] += dot(normed_ref[...], dz, TN)
    into = dot_left(jnp.exp(cum_ref[...]) * aux_ref[:, 1:2], spread_matrix(heads, inner))
    g_state_ref[...] += prod[...] * dot(c_ref[...].astype(BF16), (dy * into).astype(BF16), TN)
    prod[...] = prod[...] * kept_ref[0]


def back_kernel(
    cin_ref, before_ref, dy_ref, y_ref, v_ref, cum_ref, vt_ref, cumt_ref, aux_ref, docr_ref, si_ref, kept_ref,
    taps_ref, rate_ref, skip_ref, all_ref, weight_ref,
    pre_ref, dstep_ref, g_dt_ref, g_log_ref, g_skip_ref, g_conv_ref, adj, ext,
):
    step_id = pl.program_id(0)
    size, inner = dy_ref.shape
    heads = cum_ref.shape[1]
    state = adj.shape[0]
    n_taps = taps_ref.shape[0] - 1

    @pl.when(step_id == 0)
    def _():
        total = jnp.zeros_like(adj)
        for k in range(all_ref.shape[0]):
            total = total + weight_ref[k] * all_ref[k].astype(F32)
        adj[...] = total
        for ref in (g_dt_ref, g_log_ref, g_skip_ref, g_conv_ref):
            ref[...] = jnp.zeros_like(ref)

    spread, collect = spread_matrix(heads, inner), gather_matrix(heads, inner)
    ext[0:EDGE, :] = before_ref[...]
    ext[EDGE:, :] = cin_ref[...]
    pre = conv_forward(ext, 0, size, taps_ref[...])
    sig = sigmoid(pre)
    u = pre * sig
    dsilu = sig * (1.0 + pre * (1.0 - sig))
    xh = u[:, :inner]
    b_mat, c_full = u[:, inner : inner + state].astype(BF16), u[:, inner + state :]
    c_mat = c_full.astype(BF16)
    v = v_ref[...]
    step = softplus(v)
    cum, cumt = cum_ref[...], cumt_ref[...]
    where_s, where_t = iota((size, size), 0), iota((size, size), 1)
    doc, carried, last = aux_ref[:, 0:1], aux_ref[:, 1:2], aux_ref[:, 2:3]
    mask = jnp.where((where_t >= where_s) & (doc == docr_ref[...]), 0.0, NEG)
    scores = score_pair(c_full, b_mat, False)
    step_e = dot_left(step, spread)
    total = cum[size - 1 : size, :]
    to_end = dot_left(jnp.exp(total - cum) * last, spread)
    into = dot_left(jnp.exp(cum) * carried, spread)
    xs = xh * step_e
    xsb = xs.astype(BF16)
    dyb = dy_ref[...]
    dy = dyb.astype(F32)
    si = si_ref[0]
    back = adj[...]
    backb = back.astype(BF16)
    dye = dy * into
    xse = xs * to_end
    d_c = dot3(dye, si, NT)
    d_b = dot3(xse, back, NT)
    dye, xse = dye.astype(BF16), xse.astype(BF16)
    d_xs_inter = to_end * dot(b_mat, backb)
    lanes = 2 * (inner // heads)
    first = iota((size, lanes), 1) < lanes // 2
    d_scores = jnp.zeros((size, size), F32)
    parts = []
    for pair in range(heads // 2):
        cols = slice(pair * lanes, (pair + 1) * lanes)
        xp, dp = xsb[:, cols], dyb[:, cols]
        zero = jnp.zeros_like(dp)
        d_two = (jnp.where(first, dp, zero), jnp.where(first, zero, dp))
        mixed = []
        for i, h in enumerate((2 * pair, 2 * pair + 1)):
            decay = jnp.exp(cumt[h : h + 1, :] - cum[:, h : h + 1] + mask)
            mixed.append((scores * decay).astype(BF16))
            d_scores = d_scores + dot(xp, d_two[i], NT) * decay
        parts.append(dot(jnp.concatenate(mixed, axis=1), jnp.concatenate(d_two, axis=0)))
    d_xs_intra = jnp.concatenate(parts, axis=1)
    d_sb = d_scores.astype(BF16)
    d_b = d_b + dot(d_sb, c_mat)
    d_c = d_c + dot(d_sb, b_mat, TN)
    skip = skip_ref[...]
    d_xs = d_xs_intra + d_xs_inter
    y_ssd = y_ref[...] - skip * xh
    d_step_dir = dot_left(xh * d_xs, collect)
    d_cum = dot_left(dy * y_ssd - (xsb.astype(F32) * d_xs_intra + xs * d_xs_inter), collect)
    inc = dot(b_mat, xse, TN)
    end_state = kept_ref[0] * si + inc
    through = dot_left(jnp.sum(back * end_state, axis=0, keepdims=True), collect)
    upper = (where_t >= where_s).astype(BF16)
    d_la = dot_right(upper, d_cum) + through
    d_la = d_la * aux_ref[:, 4:5]
    rate = rate_ref[...]
    g_log_ref[...] += jnp.sum(rate * step * d_la, axis=0, keepdims=True)
    d_v = (d_step_dir + rate * d_la) * sigmoid(v)
    g_dt_ref[...] += jnp.sum(d_v, axis=0, keepdims=True)
    dstep_ref[...] = d_v.astype(BF16)
    g_skip_ref[...] += jnp.sum(dy * xh, axis=0, keepdims=True)
    adj[...] = kept_ref[0] * back + dot(c_mat, dye, TN)
    pre_ref[:, :inner] = (skip * dy + step_e * d_xs) * dsilu[:, :inner]
    pre_ref[:, inner : inner + state] = d_b * dsilu[:, inner : inner + state]
    pre_ref[:, inner + state :] = d_c * dsilu[:, inner + state :]
    d_pre = pre_ref[...]
    for k in range(n_taps):
        g_conv_ref[k : k + 1, :] += jnp.sum(d_pre * ext[pl.ds(EDGE - k, size), :], axis=0, keepdims=True)
    g_conv_ref[n_taps : n_taps + 1, :] += jnp.sum(d_pre, axis=0, keepdims=True)


def proj_back_kernel(
    pre_ref, next_ref, taps_ref, normed_ref, dz_ref, dstep_ref, wg_ref, wv_ref, ws_ref,
    part_ref, g_value_ref, g_step_ref, ext,
):
    step_id = pl.program_id(0)
    size = pre_ref.shape[0]
    inner = wv_ref.shape[1]
    width = wg_ref.shape[0]

    @pl.when(step_id == 0)
    def _():
        g_value_ref[...] = jnp.zeros_like(g_value_ref)
        g_step_ref[...] = jnp.zeros_like(g_step_ref)

    ext[0:size, :] = pre_ref[...]
    ext[size:, :] = next_ref[...]
    taps = taps_ref[...]
    d_in = taps[0:1, :] * ext[0:size, :]
    for k in range(1, taps.shape[0] - 1):
        d_in = d_in + taps[k : k + 1, :] * ext[pl.ds(k, size), :]
    d_val = d_in[:, :inner].astype(BF16)
    dstep = dstep_ref[...]
    part = dot(dz_ref[...], wg_ref[...], NT) + dot(d_val, wv_ref[...], NT) + dot(dstep, ws_ref[...], NT)
    part_ref[:, :width] = part.astype(BF16)
    part_ref[:, width:] = d_in[:, inner:].astype(BF16)
    normed = normed_ref[...]
    g_value_ref[...] += dot(normed, d_val, TN)
    g_step_ref[...] += dot(normed, dstep, TN)


def last_kernel(
    part_ref, x_ref, cot_ref, gain_ref, wbc_ref, grad_ref, g_bc_ref, g_norm_ref,
):
    width = x_ref.shape[1]

    @pl.when(pl.program_id(0) == 0)
    def _():
        g_bc_ref[...] = jnp.zeros_like(g_bc_ref)
        g_norm_ref[...] = jnp.zeros_like(g_norm_ref)

    x = x_ref[...].astype(F32)
    gain = gain_ref[...]
    r = lax.rsqrt(jnp.mean(x * x, axis=1, keepdims=True) + EPS)
    xr = x * r
    normed = (xr * gain).astype(BF16)
    d_bc = part_ref[:, width:]
    d_normed = part_ref[:, :width].astype(F32) + dot(d_bc, wbc_ref[...], NT)
    g_bc_ref[...] += dot(normed, d_bc, TN)
    g_norm_ref[...] += jnp.sum(d_normed * xr, axis=0, keepdims=True)
    q = d_normed * gain
    d_x = r * q - xr * (r * r * jnp.mean(q * x, axis=1, keepdims=True))
    grad_ref[...] = (d_x + cot_ref[...].astype(F32)).astype(BF16)


def shift(block, axis, distance):
    devices = range(lax.axis_size(axis))
    return lax.ppermute(block, axis, [(i - distance, i) for i in devices if i - distance in devices])


def whole(a):
    return pl.BlockSpec(a.shape, lambda i: (0,) * len(a.shape))


def shape(dims, dtype=F32):
    return jax.ShapeDtypeStruct(dims, dtype)


def params():
    return pltpu.CompilerParams(vmem_limit_bytes=VMEM_LIMIT, dimension_semantics=("arbitrary",))


def chain_weights(carry, axis, reverse):
    n, here = lax.axis_size(axis), lax.axis_index(axis)
    rows = []
    for k in range(n):
        used = jnp.ones_like(carry[0])
        for j in range(n):
            between = ((here < j) & (j < k)) if reverse else ((k < j) & (j < here))
            used = used * jnp.where(between, carry[j], 1.0)
        reach = (k > here) if reverse else (k < here)
        rows.append(jnp.where(reach, used, 0.0))
    return jnp.stack(rows)


def on_device(
    hidden_in, doc_ids, norm_gain, w_gate, w_value, w_bc, w_step, conv_value, conv_bc, dt_bias, a_log, d_skip,
    out_gain, w_out, cotangent,
):
    x = hidden_in[0]
    docs = doc_ids[0]
    tokens, width = x.shape
    inner = w_gate.shape[1]
    heads = w_step.shape[1]
    head_dim = inner // heads
    bc_width = w_bc.shape[1]
    state = bc_width // 2
    channels = inner + bc_width
    blocks = tokens // BLOCK
    n_head = lax.axis_size("head")
    inner_all = inner * n_head
    n_taps = conv_value.shape[0] - 1

    edge_x, edge_doc = shift((x[tokens - 16 :], (docs[tokens - 1 :] + 1).astype(F32)), "seq", 1)
    doc_before = edge_doc[0] - 1.0
    docf = docs.astype(F32)
    by_block = docf.reshape(blocks, BLOCK)
    prev_doc = jnp.concatenate([doc_before[None], by_block[:-1, -1]])
    carried = (by_block == prev_doc[:, None]).astype(F32)
    last = (by_block == by_block[:, -1:]).astype(F32)
    kept_mask = jnp.broadcast_to((by_block[:, -1] == prev_doc).astype(F32)[:, None], by_block.shape)
    keep = (docf == jnp.concatenate([doc_before[None], docf[:-1]])).astype(F32).reshape(by_block.shape)
    none = jnp.zeros_like(keep)
    aux = jnp.stack([by_block, carried, last, kept_mask, keep, none, none, none], axis=-1).reshape(tokens, 8)
    docr = docf.reshape(1, tokens)

    taps = jnp.concatenate([conv_value, conv_bc], axis=1)
    gain = norm_gain[None]
    rate = -jnp.exp(a_log)[None]
    skip = jnp.repeat(d_skip, head_dim)[None]
    cot = lax.all_gather(cotangent[0], "head", axis=1, tiled=True)

    def rows(n, size=BLOCK):
        return pl.BlockSpec((size, n), lambda i: (i, 0))

    def cols(n):
        return pl.BlockSpec((n, BLOCK), lambda i: (0, i))

    def per_block(*dims):
        return pl.BlockSpec((1, *dims), lambda i: (i,) + (0,) * len(dims))

    def fixed(*dims):
        return pl.BlockSpec(dims, lambda i: (0,) * len(dims))

    w_step_t = w_step.T
    front = (x, edge_x, gain, w_gate, w_value, w_bc, w_step, w_step_t, taps, dt_bias[None], dt_bias[:, None],
             rate, rate.T, skip, aux, docr)
    (normed, z, cin, head_edge, y_intra, c_mat, v, cum, vt, cumt, inc, kept, end, carry) = pl.pallas_call(
        front_kernel,
        grid=(blocks,),
        in_specs=[rows(width)] + [whole(a) for a in front[1:14]] + [rows(8), cols(1)],
        out_specs=[rows(width), rows(inner), rows(channels), fixed(EDGE, channels), rows(inner), rows(state),
                   rows(heads), rows(heads), cols(heads), cols(heads), per_block(state, inner),
                   per_block(1, inner), fixed(state, inner), fixed(1, inner)],
        out_shape=[shape((tokens, width), BF16), shape((tokens, inner)), shape((tokens, channels)),
                   shape((EDGE, channels)), shape((tokens, inner)), shape((tokens, state)),
                   shape((tokens, heads)), shape((tokens, heads)), shape((heads, tokens)), shape((heads, tokens)),
                   shape((blocks, state, inner)), shape((blocks, 1, inner)), shape((state, inner)),
                   shape((1, inner))],
        scratch_shapes=[pltpu.VMEM((EDGE + BLOCK, channels), F32)],
        compiler_params=params(),
        name="front",
    )(*front)

    ends = lax.all_gather(end.astype(BF16), "seq")
    carries = lax.all_gather(carry, "seq")
    og = out_gain[None]
    mid = (y_intra, z, c_mat, cum, aux, cot, w_out, og, inc, kept, ends, chain_weights(carries, "seq", False))
    y, si, dgn, sums = pl.pallas_call(
        mid_kernel,
        grid=(blocks,),
        in_specs=[rows(inner), rows(inner), rows(state), rows(heads), rows(8), rows(width), whole(w_out), whole(og),
                  per_block(state, inner), per_block(1, inner), whole(ends), whole(mid[-1])],
        out_specs=[rows(inner), per_block(state, inner), rows(inner), cols(2)],
        out_shape=[shape((tokens, inner)), shape((blocks, state, inner)), shape((tokens, inner)), shape((2, tokens))],
        scratch_shapes=[pltpu.VMEM((state, inner), F32)],
        compiler_params=params(),
        name="mid",
    )(*mid)

    sums = lax.psum(sums, "head").T
    gate = (y, z, c_mat, cum, aux, cot, w_out, og, dgn, sums, kept, normed)
    dy, dz, out_part, g_w_out, g_w_gate, g_out_gain, g_state = pl.pallas_call(
        functools.partial(gate_kernel, inner_all),
        grid=(blocks,),
        in_specs=[rows(inner), rows(inner), rows(state), rows(heads), rows(8), rows(width), whole(w_out), whole(og),
                  rows(inner), rows(2), per_block(1, inner), rows(width)],
        out_specs=[rows(inner), rows(inner), rows(width), fixed(inner, width), fixed(width, inner), fixed(1, inner),
                   fixed(state, inner)],
        out_shape=[shape((tokens, inner), BF16), shape((tokens, inner), BF16), shape((tokens, width), BF16),
                   shape((inner, width)), shape((width, inner)), shape((1, inner)), shape((state, inner))],
        scratch_shapes=[pltpu.VMEM((1, inner), F32)],
        compiler_params=params(),
        name="gate",
    )(*gate)

    out_cols = lax.psum_scatter(out_part, "head", scatter_dimension=1, tiled=True).astype(F32)
    part_width = out_cols.shape[1]
    residual = lax.dynamic_slice_in_dim(x, lax.axis_index("head") * part_width, part_width, 1).astype(F32)
    block_out = (residual + out_cols).astype(BF16)[None]

    g_states = lax.all_gather(g_state.astype(BF16), "seq")
    before = jnp.concatenate([head_edge, cin.reshape(blocks, BLOCK, channels)[:-1, BLOCK - EDGE :].reshape(-1, channels)])

    def turn(spec_rows, n):
        return pl.BlockSpec((spec_rows, n), lambda i: (blocks - 1 - i, 0))

    def turn_cols(n):
        return pl.BlockSpec((n, BLOCK), lambda i: (0, blocks - 1 - i))

    def turn_block(*dims):
        return pl.BlockSpec((1, *dims), lambda i: (blocks - 1 - i,) + (0,) * len(dims))

    back = (cin, before, dy, y, v, cum, vt, cumt, aux, docr, si, kept, taps, rate, skip, g_states,
            chain_weights(carries, "seq", True))
    pre, dstep, g_dt, g_log, g_skip, g_conv = pl.pallas_call(
        back_kernel,
        grid=(blocks,),
        in_specs=[turn(BLOCK, channels), turn(EDGE, channels), turn(BLOCK, inner), turn(BLOCK, inner),
                  turn(BLOCK, heads), turn(BLOCK, heads), turn_cols(heads), turn_cols(heads), turn(BLOCK, 8),
                  turn_cols(1), turn_block(state, inner), turn_block(1, inner), whole(taps), whole(rate), whole(skip),
                  whole(g_states), whole(back[-1])],
        out_specs=[turn(BLOCK, channels), turn(BLOCK, heads), fixed(1, heads), fixed(1, heads), fixed(1, inner),
                   fixed(8, channels)],
        out_shape=[shape((tokens, channels)), shape((tokens, heads), BF16), shape((1, heads)), shape((1, heads)),
                   shape((1, inner)), shape((8, channels))],
        scratch_shapes=[pltpu.VMEM((state, inner), F32),
                        pltpu.VMEM((EDGE + BLOCK, channels), F32)],
        compiler_params=params(),
        name="back",
    )(*back)

    edge_back = shift(pre[:EDGE], "seq", -1)
    following = jnp.concatenate([pre.reshape(blocks, BLOCK, channels)[1:, :EDGE].reshape(-1, channels), edge_back])
    proj = (pre, following, taps, normed, dz, dstep, w_gate, w_value, w_step)
    part, g_w_value, g_w_step = pl.pallas_call(
        proj_back_kernel,
        grid=(blocks,),
        in_specs=[rows(channels), rows(channels, EDGE), whole(taps), rows(width), rows(inner), rows(heads),
                  whole(w_gate), whole(w_value), whole(w_step)],
        out_specs=[rows(width + bc_width), fixed(width, inner), fixed(width, heads)],
        out_shape=[shape((tokens, width + bc_width), BF16), shape((width, inner)), shape((width, heads))],
        scratch_shapes=[pltpu.VMEM((EDGE + BLOCK, channels), F32)],
        compiler_params=params(),
        name="proj_back",
    )(*proj)

    own = lax.psum_scatter(part, "head", scatter_dimension=0, tiled=True)
    slab = own.shape[0]
    start = lax.axis_index("head") * slab
    x_own = lax.dynamic_slice_in_dim(x, start, slab, 0)
    cot_own = lax.dynamic_slice_in_dim(cot, start, slab, 0)
    size = slab // 3
    fin = (own, x_own, cot_own, gain, w_bc)
    grad_own, g_w_bc, g_norm = pl.pallas_call(
        last_kernel,
        grid=(slab // size,),
        in_specs=[rows(width + bc_width, size), rows(width, size), rows(width, size), whole(gain), whole(w_bc)],
        out_specs=[rows(width, size), fixed(width, bc_width), fixed(1, width)],
        out_shape=[shape((slab, width), BF16), shape((width, bc_width)), shape((1, width))],
        compiler_params=params(),
        name="last",
    )(*fin)
    grad_in = lax.all_gather(grad_own, "head", axis=0, tiled=True)[None]

    g_w_gate, g_w_out = lax.psum((g_w_gate.astype(BF16), g_w_out.astype(BF16)), ("seq", "dp"))
    g_w_value = lax.psum(g_w_value.astype(BF16), ("seq", "dp"))
    g_w_bc = lax.psum(g_w_bc.astype(BF16), ("seq", "dp", "head"))
    g_norm, g_conv_bc = lax.psum((g_norm, g_conv[:, inner:]), ("seq", "dp", "head"))
    g_w_step, g_conv, g_dt, g_log, g_skip, g_out_gain = lax.psum(
        (g_w_step, g_conv[:, :inner], g_dt, g_log, g_skip, g_out_gain), ("seq", "dp")
    )
    return (
        block_out,
        grad_in,
        g_norm[0],
        g_w_gate.astype(F32),
        g_w_value.astype(F32),
        g_w_bc.astype(F32),
        g_w_step,
        g_conv[: n_taps + 1],
        g_conv_bc[: n_taps + 1],
        g_dt[0],
        g_log[0],
        g_skip.reshape(heads, head_dim).sum(axis=1),
        g_out_gain[0],
        g_w_out.astype(F32),
    )


def solution(mesh):
    return jax.shard_map(
        on_device,
        mesh=mesh,
        in_specs=(
            P("dp", "seq", None),
            P("dp", "seq"),
            P(),
            P(None, "head"),
            P(None, "head"),
            P(),
            P(None, "head"),
            P(None, "head"),
            P(),
            P("head"),
            P("head"),
            P("head"),
            P("head"),
            P("head", None),
            P("dp", "seq", "head"),
        ),
        out_specs=(
            P("dp", "seq", "head"),
            P("dp", "seq", None),
            P(),
            P(None, "head"),
            P(None, "head"),
            P(),
            P(None, "head"),
            P(None, "head"),
            P(),
            P("head"),
            P("head"),
            P("head"),
            P("head"),
            P("head", None),
        ),
        check_vma=False,
    )
```

time: 1200 us -> 583 us (0.49); the launches traced: 1190 us -> 581 us
  local copies, waits for them, and re-layouts: 354 us -> 24.9 us
  matrix products: 246 us -> 0 us
  other arithmetic: 217 us -> 27.8 us
  Pallas kernels: 0 us -> 91.1 us
  blocking collectives: 97.2 us -> 158 us
  waiting for transfers between devices: 230 us -> 252 us
    dot_general x90 -> x0, matrix products: 246 us -> none  [the longest x18 69.8 us: ssd_block(): y_intra = jnp.einsum('tsh,shp->thp', mixing, x_heads, precision=HIGHEST)]
    dynamic_update_slice x54 -> x0, local copies, waits for them, and re-layouts: 173 us -> none  [local_mix(): final_carry, block_ys = lax.scan(ssd_block, init_carry, blocks)]
    psum x3 -> x2, waiting for transfers between devices: 219 us -> 125 us  [the longest x1 91.2 us: on_device(): g_w_bc = lax.psum(g_w_bc.astype(BF16), ('seq', 'dp', 'head'))]
    pallas_call x0 -> x6, Pallas kernels: none -> 91.1 us  [the longest x1 25.9 us: on_device(): pl.pallas_call(back_kernel, grid=(blocks,), in_specs=[turn(BLOCK, channel...]
    reduce_scatter x1 -> x2, waiting for transfers between devices: 0.01 us -> 78.8 us  [the longest x1 40.7 us: on_device(): lax.psum_scatter(out_part, 'head', scatter_dimension=1, tiled=True)]
    dynamic_slice x54 -> x2, local copies, waits for them, and re-layouts: 80.7 us -> 2.99 us  [the longest x1 2.06 us: on_device(): cot_own = lax.dynamic_slice_in_dim(cot, start, slab, 0)]
    dynamic_update_slice x48 -> x0, other arithmetic: 70.9 us -> none  [local_mix(): final_carry, block_ys = lax.scan(ssd_block, init_carry, blocks)]
    psum x4 -> x3, blocking collectives: 58.7 us -> 115 us  [the longest x1 46.4 us: on_device(): lax.psum((g_w_step, g_conv[:, :inner], g_dt, g_log, g_skip, g_out_gain),...]
  transfers between devices with their start and end apart: 8 -> 9, of which waited for: 4 -> 6; matrix products, arithmetic and copies ran while one was open for 31% -> 7% of each run, Pallas kernels for 0% -> 4%
where the time goes in v1:
time: 583 us; the launch traced here: 581 us
  waiting for transfers between devices  252 us (43%)
  blocking collectives  158 us (27%)
  Pallas kernels  91.1 us (16%)
  other arithmetic  27.8 us (5%)
  local copies, waits for them, and re-layouts  24.9 us (4%)
  between operations  15.7 us (3%)
  starting transfers between devices  11.4 us (2%)
    psum x1, waiting for transfers between devices, on_device(): g_w_bc = lax.psum(g_w_bc.astype(BF16), ('seq', 'dp', 'head'))  91.2 us
    psum x1, blocking collectives, on_device(): lax.psum((g_w_step, g_conv[:, :inner], g_dt, g_log, g_skip, g_out_gain),...  46.4 us
    all_gather x1, waiting for transfers between devices, on_device(): grad_in = lax.all_gather(grad_own, 'head', axis=0, tiled=True)[None]  42.8 us
    reduce_scatter x1, waiting for transfers between devices, on_device(): lax.psum_scatter(out_part, 'head', scatter_dimension=1, tiled=True)  40.7 us
    psum x1, blocking collectives, on_device(): lax.psum((g_norm, g_conv[:, inner:]), ('seq', 'dp', 'head'))  39.5 us
    reduce_scatter x1, waiting for transfers between devices, on_device(): own = lax.psum_scatter(part, 'head', scatter_dimension=0, tiled=True)  38.1 us
    psum x1, waiting for transfers between devices, on_device(): lax.psum((g_w_gate.astype(BF16), g_w_out.astype(BF16)), ('seq', 'dp'))  33.8 us
    psum x1, blocking collectives, on_device(): sums = lax.psum(sums, 'head').T  29.4 us
  transfers between devices with their start and end apart: 9, of which 6 were waited for; matrix products, arithmetic and copies ran while one was open for 7% of the time, Pallas kernels for 4%

profile of v1, /device:TPU:0, one launch (start us, length us, event | category | flops | bytes accessed | tf_op | source)
XLA Modules:
  0.0 580.9 jit_solution(3344147633717551101)
XLA Ops:
  8.0 1.2 slice.39
  9.9 6.2 %collective-permute-start.1 = (f32[1]{0:T(128)}, f32[1]{0:T(128)}, u32[]{:S(2)}, u32[]{:S(2)}) collective-permute-start(f32[1]{0:T(128)} %bitcast.10), channel_id=1, source_target_pairs={{0,8},{8,16},{16,24},{1,9},{9,17},{17,25},{2,10},{10,18},{18,26},{... | collective-permute-start | bytes 20 | tf_op jit(solution)/shard_map/ppermute | solution.py:387
  16.1 0.8 slice_bitcast_fusion.2
  16.8 3.5 collective-permute-start
  21.4 1.5 copy.55.ws_ref
  24.4 1.2 fusion.8
  26.2 1.3 copy.56.dtbt_ref
  30.6 0.8 compare_convert_fusion
  31.5 1.2 copy.58.aux_ref
  33.3 20.4 %front.1 = (bf16[1536,1024]{1,0:T(8,128)(2,1)}, f32[1536,512]{1,0:T(8,128)}, f32[1536,768]{1,0:T(8,128)}, f32[8,768]{1,0:T(8,128)}, f32[1536,512]{1,0:T(8,128)},...) custom-call(bf16[1536,1024]{1,0:T(8,128)(2,1)} %bitcast.76, ...), custom_call_target="tpu_custom_call" | custom-call | tf_op jit(solution)/shard_map/front/pallas_call | solution.py:467
  53.7 1.0 convert_element_type.130
  54.7 11.9 %all-gather.4 = f32[4,1,512]{2,1,0:T(1,128)S(1)} all-gather(f32[1,1,512]{2,1,0:T(1,128)} %bitcast.96), channel_id=4, replica_groups=mesh['seq'=4,'head'=4,'dp'=2] {'seq'}, dimensions={0}, use_global_device_ids=true | all-gather | bytes 10240 | tf_op jit(solution)/shard_map/all_gather | solution.py:485
  66.6 0.9 slice_bitcast_fusion.1
  67.5 1.4 pad_maximum_fusion.before_ref
  68.9 15.5 %all-gather.1 = bf16[512,512]{1,0:T(8,128)(2,1)} all-gather(bf16[128,512]{1,0:T(8,128)(2,1)S(1)} %convert_element_type.130), channel_id=3, replica_groups=mesh['seq'=4,'head'=4,'dp'=2] {'seq'}, dimensions={0}, use_global_device_ids=true | all-gather | bytes 655360 | tf_op jit(solution)/shard_map/all_gather | solution.py:484
  85.8 11.1 %mid.1 = (f32[1536,512]{1,0:T(8,128)}, f32[6,128,512]{2,1,0:T(8,128)}, f32[1536,512]{1,0:T(8,128)}, f32[2,1536]{1,0:T(2,128)}) custom-call(f32[1536,512]{1,0:T(8,128)} %get-tuple-element.51.yi_ref, f32[1536,512]{1,0:T(8,128)} %get-tuple-element.52.z_ref, f32[1536,128]{1,0:T(8,128)} %get-tuple-element.53.c_ref, f32[1536,8]{1,0:T(8,128)} %get-tuple-element.54.cum_ref, ...), custom_call_target="tpu_custom_call" | custom-call | tf_op jit(solution)/shard_map/mid/pallas_call | solution.py:488
  96.9 1.0 copy.60
  97.9 29.4 %psum.91.sums_ref = f32[1536,2]{1,0:T(8,128)} all-reduce(f32[1536,2]{1,0:T(8,128)S(1)} %bitcast.80), channel_id=1, replica_groups=mesh['seq'=4,'head'=4,'dp'=2] {'head'}, use_global_device_ids=true, to_apply=%region_0.1 | all-reduce | flops 3072 | bytes 24576 | tf_op jit(solution)/shard_map/psum | solution.py:500
  127.4 15.4 %gate.1 = (bf16[1536,512]{1,0:T(8,128)(2,1)}, bf16[1536,512]{1,0:T(8,128)(2,1)}, bf16[1536,1024]{1,0:T(8,128)(2,1)}, f32[512,1024]{1,0:T(8,128)}, f32[1024,512]{...) custom-call(f32[1536,512]{1,0:T(8,128)} %get-tuple-element.59.y_ref, f32[1536,512]{1,0:T(8,128)} %get-tuple-element.52.z_ref, ...), custom_call_target="tpu_custom_call" | custom-call | tf_op jit(solution)/shard_map/gate/pallas_call | solution.py:502
  142.8 1.0 convert_element_type.133
  143.8 15.5 %all-gather.3 = bf16[512,512]{1,0:T(8,128)(2,1)} all-gather(bf16[128,512]{1,0:T(8,128)(2,1)S(1)} %convert_element_type.133), channel_id=5, replica_groups=mesh['seq'=4,'head'=4,'dp'=2] {'seq'}, dimensions={0}, use_global_device_ids=true | all-gather | bytes 655360 | tf_op jit(solution)/shard_map/all_gather | solution.py:521
  159.3 25.9 %back.1 = (f32[1536,768]{1,0:T(8,128)}, bf16[1536,8]{1,0:T(8,128)(2,1)}, f32[1,8]{1,0:T(1,128)}, f32[1,8]{1,0:T(1,128)}, f32[1,512]{1,0:T(1,128)}, /*index=5*/f32[8,768]{1,0:T(8,128)}) custom-call(f32[1536,768]{1,0:T(8,128)} %get-tuple-element.64.cin_ref, f32[48,768]{1,0:T(8,128)} %pad_maximum_fusion.before_ref, bf16[1536,512]{1,0:T(8,128)(2,1)} %get-tuple-element.66.dy_ref, ...), custom_call_target="tpu_custom_call" | custom-call | tf_op jit(solution)/shard_map/back/pallas_call | solution.py:535
  185.9 1.5 collective-permute-start.2
  187.4 0.9 slice_bitcast_fusion
  188.3 3.5 collective-permute-done.2
  192.5 13.4 %proj_back.1 = (bf16[1536,1280]{1,0:T(8,128)(2,1)}, f32[1024,512]{1,0:T(8,128)}, f32[1024,8]{1,0:T(8,128)}) custom-call(f32[1536,768]{1,0:T(8,128)} %get-tuple-element.72.pre_ref, f32[48,768]{1,0:T(8,128)} %pad_maximum_fusion.1.next_ref, f32[5,768]{1,0:T(8,128)} %copy-done.5, bf16[1536,1024]{1,0:T(8,128)(2,1)} %get-tuple-element.62.normed_ref, ...), custom_call_target="tpu_custom_call" | custom-call | tf_op jit(solution)/shard_map/proj_back/pallas_call | solution.py:555
  206.0 2.9 convert_element_type.134
  208.9 1.1 convert_element_type.140
  210.0 1.1 convert_element_type.136
  211.8 1.2 copy-done
  213.0 0.9 dynamic-slice_bitcast_fusion.1.x_ref
  213.9 2.1 dynamic-slice_bitcast_fusion.cot_ref
  216.0 38.1 %reduce-scatter.5.cloned.1.call-done.part_ref = bf16[384,1280]{1,0:T(8,128)(2,1)} async-done(((bf16[1536,1280]{1,0:T(8,128)(2,1)}), bf16[384,1280]{1,0:T(8,128)(2,1)}) %reduce-scatter.5.cloned.1.call-update) | async-done | bytes 983056 | tf_op jit(solution)/shard_map/reduce_scatter | solution.py:567
  254.1 4.8 last.1
  258.9 2.1 convert_element_type.138
  262.9 46.4 %all-reduce.1 = (f32[1024,8]{1,0:T(8,128)}, f32[8,512]{1,0:T(8,128)}, f32[8]{0:T(128)}, f32[8]{0:T(128)}, f32[8,64]{1,0:T(8,128)S(1)}, /*index=5*/f32[512]{0:T(512)}) all-reduce(f32[1024,8]{1,0:T(8,128)} %get-tuple-element.81, f32[8,512]{1,0:T(8,128)S(1)} %slice.95, ...), channel_id=1, replica_groups=mesh['seq'=4,'head'=4,'dp'=2] {'seq','dp'}, use_global_device_ids=true, to_apply=%region_7.8 | all-reduce | flops 13328 | bytes 106624 | tf_op jit(solution)/shard_map/psum | solution.py:589
  309.3 1.8 copy.64
  311.7 33.8 %all-reduce.8.cloned.1.call-done = (bf16[1024,512]{1,0:T(8,128)(2,1)}, bf16[1024,512]{1,0:T(8,128)(2,1)}, bf16[512,1024]{1,0:T(8,128)(2,1)}) async-done(((bf16[1024,512]{1,0:T(8,128)(2,1)}, bf16[1024,512]{1,0:T(8,128)(2,1)}, bf16[512,1024]{1,0:T(8,128)(2,1)}), (bf16[1024,512]{1,0:T(8,128)(2,1)}, bf16[1024,512]{1,0:T(8,128)(2,1)}, bf16[512,1024]{1,0:T(8,128)(2,1)})) %all-reduce.8.cloned.1.call-update) | async-done | bytes 3145744 | tf_op jit(solution)/shard_map/psum | solution.py:585
  345.5 3.0 convert_element_type.135
  348.5 1.6 convert_element_type.137
  350.1 1.6 convert_element_type.141
  351.7 40.7 %reduce-scatter.3.cloned.1.call-done = bf16[1536,256]{1,0:T(8,128)(2,1)} async-done(((bf16[1536,1024]{1,0:T(8,128)(2,1)}), bf16[1536,256]{1,0:T(8,128)(2,1)}) %reduce-scatter.3.cloned.1.call-update) | async-done | bytes 786448 | tf_op jit(solution)/shard_map/reduce_scatter | solution.py:516
  392.4 2.3 fusion.1
  394.6 39.5 %all-reduce = (f32[1024]{0:T(1024)}, f32[8,256]{1,0:T(8,128)}) all-reduce(f32[1024]{0:T(1024)S(1)} %bitcast.92, f32[8,256]{1,0:T(8,128)S(1)} %slice.97), channel_id=1, replica_groups=mesh['seq'=4,'head'=4,'dp'=2] {'seq','dp','head'}, use_global_device_ids=true, to_apply=%region_3.4 | all-reduce | flops 3072 | bytes 24576 | tf_op jit(solution)/shard_map/psum | solution.py:588
  434.1 91.2 %all-reduce.6.cloned.1.call-done = bf16[1024,256]{1,0:T(8,128)(2,1)} async-done(((bf16[1024,256]{1,0:T(8,128)(2,1)}), bf16[1024,256]{1,0:T(8,128)(2,1)}) %all-reduce.6.cloned.1.call-update) | async-done | bytes 524304 | tf_op jit(solution)/shard_map/psum | solution.py:587
  525.3 2.1 convert_element_type.139
  527.4 42.8 %all-gather.8.cloned.1.call-done = bf16[1536,1024]{1,0:T(8,128)(2,1)} async-done(((bf16[384,1024]{1,0:T(8,128)(2,1)}), bf16[1536,1024]{1,0:T(8,128)(2,1)}) %all-gather.8.cloned.1.call-update) | async-done | bytes 3145744 | tf_op jit(solution)/shard_map/all_gather | solution.py:583
  570.2 3.9 copy.76
  (78 shorter events, 13.0 us)
Async XLA Ops:
  7.2 78.6 %all-gather.10.cloned.1.call-start = ((), (), s32[]{:S(2)}) async-start(), calls=%async_computation.6 | async-start | bytes 3932160 | tf_op jit(solution)/shard_map/all_gather | solution.py:450
  7.9 246.2 %reduce-scatter.5.cloned.1.call-start = ((), (), s32[]{:S(2)}) async-start(), calls=%async_computation.3 | async-start | bytes 4915200 | tf_op jit(solution)/shard_map/reduce_scatter | solution.py:567
  9.9 19.9 %collective-permute-start.1 = (f32[1]{0:T(128)}, f32[1]{0:T(128)}, u32[]{:S(2)}, u32[]{:S(2)}) collective-permute-start(f32[1]{0:T(128)} %bitcast.10), channel_id=1, source_target_pairs={{0,8},{8,16},{16,24},{1,9},{9,17},{17,25},{2,10},{10,18},{18,26},{... | collective-permute-start | bytes 20 | tf_op jit(solution)/shard_map/ppermute | solution.py:387
  16.8 15.8 %collective-permute-start = (bf16[16,1024]{1,0:T(8,128)(2,1)S(1)}, bf16[16,1024]{1,0:T(8,128)(2,1)S(1)}, u32[]{:S(2)}, u32[]{:S(2)}) collective-permute-start(bf16[16,1024]{1,0:T(8,128)(2,1)S(1)} %slice_bitcast_fusion.2), channel_id=1, source_target_pairs={{0,8},{8,16},{16,24},{1,9},{9,17},{17,25},{2,10},{10,18},{18,26},{... | collective-permute-start | bytes 98312 | tf_op jit(solution)/shard_map/ppermute | solution.py:387
  29.0 3.6 copy-start.5
  29.7 2.9 copy-start.6
  32.7 0.6 copy-start.7
  185.9 5.9 %collective-permute-start.2 = (f32[8,768]{1,0:T(8,128)S(1)}, f32[8,768]{1,0:T(8,128)S(1)}, u32[]{:S(2)}, u32[]{:S(2)}) collective-permute-start(f32[8,768]{1,0:T(8,128)S(1)} %slice.94), channel_id=1, source_target_pairs={{8,0},{16,8},{24,16},{9,1},{17,9},{25,17},{10,2},{18,10},{26,18},{... | collective-permute-start | bytes 73736 | tf_op jit(solution)/shard_map/ppermute | solution.py:387
  205.9 2.9 copy-start.1
  205.9 139.5 %all-reduce.8.cloned.1.call-start = ((), (), s32[]{:S(2)}) async-start(), calls=%async_computation.7 | async-start | bytes 6291456 | tf_op jit(solution)/shard_map/psum | solution.py:585
  206.0 4.0 copy-start.2
  211.1 1.9 copy-start
  211.1 181.2 %reduce-scatter.3.cloned.1.call-start = ((), (), s32[]{:S(2)}) async-start(), calls=%async_computation.2 | async-start | bytes 3932160 | tf_op jit(solution)/shard_map/reduce_scatter | solution.py:516
  211.7 313.6 %all-reduce.6.cloned.1.call-start = ((), (), s32[]{:S(2)}) async-start(), calls=%async_computation.5 | async-start | bytes 1048576 | tf_op jit(solution)/shard_map/psum | solution.py:587
  216.0 45.6 %copy-start.8 = (f32[8,768]{1,0:T(8,128)S(1)}, f32[8,768]{1,0:T(8,128)}, u32[]{:S(2)}) copy-start(f32[8,768]{1,0:T(8,128)} %get-tuple-element.82) | copy-start | bytes 73732
  216.0 46.1 %copy-start.11 = (f32[1,512]{1,0:T(1,128)S(1)}, f32[1,512]{1,0:T(1,128)}, u32[]{:S(2)}) copy-start(f32[1,512]{1,0:T(1,128)} %get-tuple-element.85) | copy-start | bytes 6148
  216.0 46.9 %copy-start.10 = (f32[1,512]{1,0:T(1,128)S(1)}, f32[1,512]{1,0:T(1,128)}, u32[]{:S(2)}) copy-start(f32[1,512]{1,0:T(1,128)} %get-tuple-element.86) | copy-start | bytes 6148
  216.0 46.9 %copy-start.12 = (f32[1,8]{1,0:T(1,128)S(1)}, f32[1,8]{1,0:T(1,128)}, u32[]{:S(2)}) copy-start(f32[1,8]{1,0:T(1,128)} %get-tuple-element.83) | copy-start | bytes 100
  216.0 46.9 %copy-start.13 = (f32[1,8]{1,0:T(1,128)S(1)}, f32[1,8]{1,0:T(1,128)}, u32[]{:S(2)}) copy-start(f32[1,8]{1,0:T(1,128)} %get-tuple-element.84) | copy-start | bytes 100
  261.0 309.2 %all-gather.8.cloned.1.call-start = ((), (), s32[]{:S(2)}) async-start(), calls=%async_computation.4 | async-start | bytes 3932160 | tf_op jit(solution)/shard_map/all_gather | solution.py:583
  345.5 3.0 copy-start.4
  345.5 4.6 copy-start.3
  350.1 44.5 %copy-start.9 = (f32[1,1024]{1,0:T(1,128)S(1)}, f32[1,1024]{1,0:T(1,128)}, u32[]{:S(2)}) copy-start(f32[1,1024]{1,0:T(1,128)} %get-tuple-element.77) | copy-start | bytes 12292
Sparse Core Ops, SparseCore 0:
  9.8 46.5 all-gather.9
  206.1 47.9 reduce-scatter.4
  257.8 87.6 all-reduce.7
  348.3 43.9 reduce-scatter.2
  397.5 127.7 all-reduce.5
  527.1 42.9 all-gather.7

commit v2 on v0

v2 whole, which is shorter than its diff:
```python
import functools
import types

import jax
import jax.numpy as jnp
from jax import lax
from jax.experimental import pallas as pl
from jax.experimental.pallas import tpu as pltpu
from jax.sharding import PartitionSpec as P

BLOCK = 256
EDGE = 8
TAIL = 16
EPS = 1e-05
NEG = -1e30
F32 = jnp.float32
BF16 = jnp.bfloat16
NN = (((1,), (0,)), ((), ()))
NT = (((1,), (1,)), ((), ()))
TN = (((0,), (0,)), ((), ()))
MESH = pl.DeviceIdType.MESH
CUM, AUX, DYY, STEP, TO_END, INTO, RMS = 8, 16, 24, 32, 40, 48, 56
DIRECT = 8
LAG = 4
HEAD_AXIS, SEQ_AXIS, DP_AXIS = "head", "seq", "dp"
COT, HALO, ENDS, CARRY, BACK, SUM, OUT, PART, GRAD, EDGES, BC, BCG, PACK1, PACK2, PACK3 = (
    "cot", "halo", "ends", "carry", "back", "sum", "out", "part", "grad", "edge", "bc", "bcg", "pack1", "pack2", "pack3"
)
WO, WG, WV, WQ = "wo", "wg", "wv", "wq"
VMEM_LIMIT = 63 * 1024 * 1024


def dot(a, b, dims=NN):
    return lax.dot_general(a, b, dims, preferred_element_type=F32)


def halves(v):
    hi = v.astype(BF16)
    return hi, (v - hi.astype(F32)).astype(BF16)


def dot_left(v, m, dims=NN):
    hi, lo = halves(v)
    return dot(hi, m, dims) + dot(lo, m, dims)


def dot_right(m, v, dims=NN):
    hi, lo = halves(v)
    return dot(m, hi, dims) + dot(m, lo, dims)


def dot3(a, b, dims=NN):
    (ah, al), (bh, bl) = halves(a), halves(b)
    return dot(ah, bh, dims) + (dot(al, bh, dims) + dot(ah, bl, dims))


def score_pair(c, b, first):
    hi, lo = halves(c)
    cc, bb = jnp.concatenate([hi, lo], axis=1), jnp.concatenate([b, b], axis=1)
    return dot(cc, bb, NT) if first else dot(bb, cc, NT)


def sigmoid(v):
    return 1.0 / (1.0 + jnp.exp(-v))


def softplus(v):
    return jnp.maximum(v, 0.0) + jnp.log1p(jnp.exp(-jnp.abs(v)))


def iota(shape, axis):
    return lax.broadcasted_iota(jnp.int32, shape, axis)


def in_norm(x, gain):
    r = lax.rsqrt(jnp.mean(x * x, axis=1, keepdims=True) + EPS)
    return (x * r * gain).astype(BF16)


def repeat(n, body):
    def run(i, carry):
        body(i)
        return carry

    lax.fori_loop(0, n, run, 0)


def kernel(r):
    nh, ns = lax.axis_size(HEAD_AXIS), lax.axis_size(SEQ_AXIS)
    head, seq, dp = lax.axis_index(HEAD_AXIS), lax.axis_index(SEQ_AXIS), lax.axis_index(DP_AXIS)
    me = {HEAD_AXIS: head, SEQ_AXIS: seq, DP_AXIS: dp}
    count = {HEAD_AXIS: nh, SEQ_AXIS: ns, DP_AXIS: 2}
    tokens, width = r.x.shape
    inner, heads = r.wg.shape[1], r.ws.shape[0]
    state = r.wbc.shape[1] // 2
    channels = inner + 2 * state
    blocks, part, slab = tokens // BLOCK, width // nh, BLOCK // nh
    inner_all = inner * nh
    n_taps = r.cv.shape[0] - 1
    lanes = 2 * (inner // heads)

    def at(c):
        return pl.ds(pl.multiple_of(c * BLOCK, BLOCK), BLOCK)

    left, upper_half = lax.rem(head, 2), lax.div(head, 2)
    square = [head, 2 * upper_half + 1 - left, 2 * (1 - upper_half) + left, nh - 1 - head]

    def other(axis, o):
        if axis == HEAD_AXIS:
            return square[abs(o)]
        return lax.rem(me[axis] + o + count[axis], count[axis])

    def link(name, index, axis, o, src, dst):
        return pltpu.make_async_remote_copy(
            src_ref=src,
            dst_ref=dst,
            send_sem=getattr(r, name + "_s").at[index],
            recv_sem=getattr(r, name + "_r").at[index],
            device_id={axis: other(axis, o)},
            device_id_type=MESH,
        )

    def sent(name, index, axis, o, src):
        link(name, index, axis, o, src, src).wait_send()

    def came(name, index, axis, o, dst):
        link(name, index, axis, o, dst, dst).wait_recv()

    def gather_1(name, base, view):
        for o in (1, 2):
            link(name, base + o - 1, HEAD_AXIS, o, view(head), view(head)).start()

    def gather_2(name, base, view, half):
        for o in (1, 2):
            came(name, base + o - 1, HEAD_AXIS, o, view(square[o]))
            piece = half(square[o], o - 1)
            link(name, base + 1 + o, HEAD_AXIS, 3 - o, piece, piece).start()

    def gather_3(name, base, view, half):
        for o in (1, 2):
            came(name, base + 1 + o, HEAD_AXIS, 3 - o, half(square[3], o - 1))
            sent(name, base + o - 1, HEAD_AXIS, o, view(head))
            sent(name, base + 1 + o, HEAD_AXIS, 3 - o, half(square[o], o - 1))

    def scatter_1(name, base, block, inbox):
        for o in (1, 2):
            link(name, base + 2 * o - 2, HEAD_AXIS, o, block(square[o], o - 1), inbox.at[base + 2 * o - 2]).start()
            link(name, base + 2 * o - 1, HEAD_AXIS, o, block(square[3], o - 1), inbox.at[base + 2 * o - 1]).start()

    def scatter_2(name, base, block, inbox):
        for o in (1, 2):
            index = base + 2 * o - 1
            came(name, index, HEAD_AXIS, o, inbox.at[index])
            mine = block(square[3 - o], o - 1)
            mine[...] = (mine[...].astype(F32) + inbox[index].astype(F32)).astype(BF16)
            link(name, base + 3 + o, HEAD_AXIS, 3 - o, mine, inbox.at[base + 3 + o]).start()

    def scatter_3(name, base, block, inbox):
        totals = []
        for o in (1, 2):
            total = block(head, o - 1)[...].astype(F32)
            for index, by in ((base + 2 * o - 2, o), (base + 3 + o, 3 - o)):
                came(name, index, HEAD_AXIS, by, inbox.at[index])
                total = total + inbox[index].astype(F32)
            totals.append(total)
        return totals

    def scatter_sent(name, base, block):
        for o in (1, 2):
            sent(name, base + 2 * o - 2, HEAD_AXIS, o, block(square[o], o - 1))
            sent(name, base + 2 * o - 1, HEAD_AXIS, o, block(square[3], o - 1))
            sent(name, base + 3 + o, HEAD_AXIS, 3 - o, block(square[3 - o], o - 1))

    own = pltpu.make_async_copy(r.cot, r.cot_all.at[head], r.load.at[0])
    own.start()
    row, col = iota((BLOCK, BLOCK), 0), iota((BLOCK, BLOCK), 1)
    r.upper[...] = (row <= col).astype(BF16)
    r.eye[...] = (row == col).astype(BF16)
    dim = inner // heads
    r.spread[...] = (iota((heads, inner), 1) // dim == iota((heads, inner), 0)).astype(BF16)
    r.collect[...] = (iota((inner, heads), 0) // dim == iota((inner, heads), 1)).astype(BF16)
    for sel, lane in ((r.sel_step, STEP), (r.sel_end, TO_END), (r.sel_into, INTO)):
        sel[...] = (iota((128, inner), 1) // dim + lane == iota((128, inner), 0)).astype(BF16)
    r.tok[...] = jnp.zeros_like(r.tok)
    r.doc_out[...] = jnp.broadcast_to(r.docs[0:1, tokens - 1 : tokens].astype(F32), r.doc_out.shape)
    barrier = pltpu.get_barrier_semaphore()
    for axis in (HEAD_AXIS, SEQ_AXIS, DP_AXIS):
        for o in range(1, count[axis]):
            pl.semaphore_signal(barrier, inc=1, device_id={axis: other(axis, o)}, device_id_type=MESH)
    pl.semaphore_wait(barrier, nh + ns + 2 - 3)
    own.wait()

    def cot_of(h):
        return r.cot_all.at[h]

    def cot_half(h, i):
        return r.cot_all.at[h, pl.ds(i * (tokens // 2), tokens // 2)]

    gather_1(COT, 0, cot_of)
    x_tail = r.x.at[pl.ds(tokens - TAIL, TAIL)]
    link(HALO, 0, SEQ_AXIS, 1, x_tail, r.halo_x).start()
    link(HALO, 1, SEQ_AXIS, 1, r.doc_out, r.doc_in).start()

    taps = jnp.concatenate([r.cv[...], r.cb[...]], axis=1)
    rate = -jnp.exp(r.alog[...])
    skip = dot_left(r.dskip[...], r.spread[...])
    gain, out_gain = r.gain[...], r.og[...]

    def conv_pre(window, taps):
        pre = taps[n_taps : n_taps + 1, :] + taps[0:1, :] * window[EDGE:]
        for k in range(1, n_taps):
            pre = pre + taps[k : k + 1, :] * window[EDGE - k : EDGE - k + BLOCK]
        return pre

    def doc_row(c):
        return r.docs[0:1, at(c)].astype(F32)

    def expand(v):
        return dot_left(v, r.spread[...])

    def expand_tok(rows, sel, cols=slice(None)):
        return dot_left(r.tok[rows, :], sel[:, cols])

    def project(c):
        rows = at(c)
        normed = in_norm(r.x[rows, :].astype(F32), gain)
        r.normed[rows, :] = normed
        r.z[rows, :] = dot(normed, r.wg[...])
        inside = pl.ds(pl.multiple_of(c * BLOCK + EDGE, EDGE), BLOCK)
        r.cin[inside, :inner] = dot(normed, r.wv[...])
        r.cin[inside, inner:] = dot(normed, r.wbc[...])
        r.tok[rows, 0:heads] = dot(normed, r.ws[...], NT) + r.dtb[...]

    repeat(blocks, project)

    came(HALO, 0, SEQ_AXIS, -1, r.halo_x)
    came(HALO, 1, SEQ_AXIS, -1, r.doc_in)
    opened = jnp.where(seq == 0, 0.0, 1.0)
    edge = in_norm(r.halo_x[...].astype(F32), gain)
    r.cin[0:EDGE, :inner] = dot(edge, r.wv[...])[TAIL - EDGE :] * opened
    r.cin[0:EDGE, inner:] = dot(edge, r.wbc[...])[TAIL - EDGE :] * opened
    r.doc_prev[...] = jnp.where(seq == 0, -1.0, r.doc_in[...])

    r.carry[...] = jnp.ones_like(r.carry)

    def steps(c):
        rows = at(c)
        around = pl.ds(pl.multiple_of(c * BLOCK, BLOCK), BLOCK + EDGE)
        pre = conv_pre(r.cin[around, inner:], taps[:, inner:])
        u = pre * sigmoid(pre)
        r.b[rows, :] = u[:, :state].astype(BF16)
        r.c[rows, :] = u[:, state:]
        docs = doc_row(c)
        prev = r.doc_prev[0:1, 0:1]
        before = jnp.concatenate([prev, docs[:, : BLOCK - 1]], axis=1)
        ends = docs[:, BLOCK - 1 :]
        marks = [docs, (docs == prev).astype(F32), (docs == before).astype(F32), (docs == ends).astype(F32)]
        marks = jnp.concatenate(marks + [jnp.zeros((4, BLOCK), F32)], axis=0).astype(BF16)
        aux = dot(r.eye[...], marks, NT)
        r.tok[rows, AUX : AUX + 8] = aux
        step = softplus(r.tok[rows, 0:heads])
        la = rate * step
        la_hi, la_lo = halves(la)
        cum = dot(r.upper[...], la_hi, TN) + dot(r.upper[...], la_lo, TN)
        r.cumt[:, at(c)] = dot(la_hi, r.upper[...], TN) + dot(la_lo, r.upper[...], TN)
        total = cum[BLOCK - 1 :, :]
        r.tok[rows, CUM : CUM + heads] = cum
        r.tok[rows, STEP : STEP + heads] = step
        r.tok[rows, TO_END : TO_END + heads] = jnp.exp(total - cum) * aux[:, 3:4]
        r.tok[rows, INTO : INTO + heads] = jnp.exp(cum) * aux[:, 1:2]
        kept = expand(jnp.exp(total) * (ends == prev).astype(F32))
        r.kept[c] = kept
        r.carry[...] = r.carry[...] * kept
        r.doc_prev[...] = jnp.broadcast_to(ends, r.doc_prev.shape)

    repeat(blocks, steps)

    pairs = heads // 2
    direct = ns <= DIRECT
    if direct:
        for o in range(1, ns):
            link(CARRY, o - 1, SEQ_AXIS, o, r.carry, r.carry_in.at[o - 1]).start()
    for pair in range(pairs):
        r.carry_part[pair] = r.carry[:, pair * lanes : (pair + 1) * lanes]
    r.own[...] = jnp.zeros_like(r.own)

    def relay(turn):
        pair = turn - seq

        @pl.when(jnp.logical_and(pair >= 0, pair < pairs))
        def _():
            @pl.when(seq > 0)
            def _():
                came(ENDS, pair, SEQ_AXIS, -1, r.end_in.at[pair])

            into = jnp.where(seq > 0, r.end_in[pair], 0.0)
            r.end_out[pair] = r.carry_part[pair] * into + r.own[pair]
            r.own[pair] = into

            @pl.when(seq < ns - 1)
            def _():
                link(ENDS, pair, SEQ_AXIS, 1, r.end_out.at[pair], r.end_in.at[pair]).start()

    for pair in range(pairs):
        cols = slice(pair * lanes, (pair + 1) * lanes)

        def own_states(c, pair=pair, cols=cols):
            rows = at(c)
            around = pl.ds(pl.multiple_of(c * BLOCK, BLOCK), BLOCK + EDGE)
            pre = conv_pre(r.cin[around, cols], taps[:, cols])
            xh = pre * sigmoid(pre)
            xs = xh * expand_tok(rows, r.sel_step, cols)
            r.xs[rows, cols] = xs.astype(BF16)
            r.y[rows, cols] = skip[:, cols] * xh
            inc = dot(r.b[rows, :], (xs * expand_tok(rows, r.sel_end, cols)).astype(BF16), TN)
            r.inc[c, :, cols] = inc
            r.own[pair] = r.kept[c, :, cols] * r.own[pair] + inc

        repeat(blocks, own_states)
        relay(pair)

    gather_2(COT, 0, cot_of, cot_half)

    def pass_back():
        @pl.when(seq < ns - 1)
        def _():
            came(BACK, 0, SEQ_AXIS, 1, r.back_in.at[0])

        into = jnp.where(seq < ns - 1, r.back_in[0].astype(F32), 0.0)
        r.back_out[...] = (r.carry[...] * into + r.end[...]).astype(BF16)
        r.end[...] = into

        @pl.when(seq > 0)
        def _():
            link(BACK, 0, SEQ_AXIS, -1, r.back_out, r.back_in.at[0]).start()
            sent(BACK, 0, SEQ_AXIS, -1, r.back_out)

    first = iota((BLOCK, lanes), 1) < lanes // 2

    def split(pair):
        zero = jnp.zeros_like(pair)
        return jnp.where(first, pair, zero), jnp.where(first, zero, pair)

    def intra(c):
        rows = at(c)
        cum, cumt = r.tok[rows, CUM : CUM + heads], r.cumt[:, at(c)]
        mask = jnp.where((row >= col) & (r.tok[rows, AUX : AUX + 1] == doc_row(c)), 0.0, NEG)
        scores = score_pair(r.c[rows, :], r.b[rows, :], True)
        for pair in range(heads // 2):
            cols = slice(pair * lanes, (pair + 1) * lanes)
            mixed = []
            for h in (2 * pair, 2 * pair + 1):
                decay = jnp.exp(cum[:, h : h + 1] - cumt[h : h + 1, :] + mask)
                mixed.append((scores * decay).astype(BF16))
            two = jnp.concatenate(split(r.xs[rows, cols]), axis=0)
            r.y[rows, cols] += dot(jnp.concatenate(mixed, axis=1), two)
        relay(pairs + c)

    repeat(blocks, intra)

    if ns - 1 > blocks:
        repeat(ns - 1 - blocks, lambda i: relay(pairs + blocks + i))
    for pair in range(pairs):
        r.end[:, pair * lanes : (pair + 1) * lanes] = r.own[pair]
    gather_3(COT, 0, cot_of, cot_half)

    def dgn_of(rows):
        total = dot(r.cot_all[0, rows, :], r.wo[:, :part], NT)
        for k in range(1, nh):
            total = total + dot(r.cot_all[k, rows, :], r.wo[:, k * part : (k + 1) * part], NT)
        return total

    ones = jnp.ones((8, inner), BF16)

    def sums(c):
        rows = at(c)
        si = r.end[...]
        r.end[...] = r.kept[c] * si + r.inc[c]
        r.inc[c] = si
        into = expand_tok(rows, r.sel_into)
        y = r.y[rows, :] + into * dot3(r.c[rows, :], si)
        r.y[rows, :] = y
        z = r.z[rows, :]
        g = y * (z * sigmoid(z))
        squares = dot_right(ones, g * g, NT)
        products = dot_right(ones, dgn_of(rows) * out_gain * g, NT)
        r.sum_out[c] = jnp.concatenate([squares[0:1], products[0:1], jnp.zeros((6, BLOCK), F32)], axis=0)
        for o in range(1, nh):
            index = c * (nh - 1) + o - 1
            link(SUM, index, HEAD_AXIS, o, r.sum_out.at[c], r.sum_in.at[index]).start()
        r.parts[c, :, :width] = dot((g * out_gain).astype(BF16), r.wo[...]).astype(BF16)
        scatter_1(OUT, 6 * c, out_block(c), r.out_in)

    def out_block(c):
        half = BLOCK // 2
        return lambda h, i: r.parts.at[c, pl.ds(i * half, half), pl.ds(pl.multiple_of(h * part, part), part)]

    repeat(blocks, sums)
    r.inc[blocks] = r.end[...]

    r.end[...] = jnp.zeros_like(r.end)
    r.prod[...] = jnp.ones_like(r.prod)
    r.pack[...] = jnp.zeros_like(r.pack)
    r.g_gain[...] = jnp.zeros_like(r.g_gain)

    def gate(c):
        rows = at(c)
        scatter_2(OUT, 6 * c, out_block(c), r.out_in)
        total = r.sum_out[c]
        for o in range(1, nh):
            index = c * (nh - 1) + o - 1
            came(SUM, index, HEAD_AXIS, -o, r.sum_in.at[index])
            total = total + r.sum_in[index]
        both = dot_right(r.eye[...], total, NT)
        y, z = r.y[rows, :], r.z[rows, :]
        dgn = dgn_of(rows)
        sig = sigmoid(z)
        act = z * sig
        g = y * act
        rms = lax.rsqrt(both[:, 0:1] / inner_all + EPS)
        r.tok[rows, RMS : RMS + 1] = rms
        gr = g * rms
        r.xs[rows, :] = (gr * out_gain).astype(BF16)
        r.g_gain[...] += jnp.sum(dgn * gr, axis=0, keepdims=True)
        dg = rms * (dgn * out_gain) - g * (rms * rms * rms * both[:, 1:2] / inner_all)
        dy = dg * act
        dyb = dy.astype(BF16)
        r.dy[rows, :] = dyb
        r.tok[rows, DYY : DYY + heads] = dot_left(dyb.astype(F32) * y, r.collect[...])
        r.dz[rows, :] = (dg * y * (sig * (1.0 + z * (1.0 - sig)))).astype(BF16)
        into = expand_tok(rows, r.sel_into)
        r.end[...] += r.prod[...] * dot(r.c[rows, :].astype(BF16), (dy * into).astype(BF16), TN)
        r.prod[...] = r.prod[...] * r.kept[c]

    repeat(blocks, gate)

    if direct:
        r.back_out[...] = r.end[...].astype(BF16)
        for o in range(1, ns):
            link(BACK, o - 1, SEQ_AXIS, o, r.back_out, r.back_in.at[o - 1]).start()

    r.gw_out[...] = jnp.zeros_like(r.gw_out)
    r.gw_gate[...] = jnp.zeros_like(r.gw_gate)

    def weight_grads(c):
        rows = at(c)
        gn = r.xs[rows, :]
        for k in range(nh):
            r.gw_out[:, k * part : (k + 1) * part] += dot(gn, r.cot_all[k, rows, :], TN)
        r.gw_gate[...] += dot(r.normed[rows, :], r.dz[rows, :], TN)

    repeat(blocks, weight_grads)

    def ref(name, kind):
        return getattr(r, name + kind)

    def half_of(name, source, core):
        if name in (WO, WQ):
            half = source.shape[1] // 2
            return source.at[:, pl.ds(pl.multiple_of(core * half, half), half)]
        half = source.shape[0] // 2
        return source.at[pl.ds(pl.multiple_of(core * half, half), half)]

    def piece_of(name, half, place):
        piece = half.shape[0] // ns
        return half.at[pl.ds(pl.multiple_of(place * piece, piece), piece)]

    def total_a(name, source):
        return link(name + "a", 0, DP_AXIS, 1, half_of(name, source, 1 - dp), ref(name, "_pair"))

    def total_b(name, source):
        total_a(name, source).wait_send()
        came(name + "a", 0, DP_AXIS, 1, ref(name, "_pair"))
        mine = ref(name, "_mine")
        mine[...] = (half_of(name, source, dp)[...] + ref(name, "_pair")[...]).astype(mine.dtype)
        for o in range(1, ns):
            theirs = piece_of(name, mine, other(SEQ_AXIS, o))
            link(name + "b", o - 1, SEQ_AXIS, o, theirs, ref(name, "_in").at[o - 1]).start()

    def result(name, core, place):
        return piece_of(name, half_of(name, ref(name, "_sum"), core), place)

    def total_c(name):
        total = piece_of(name, ref(name, "_mine"), seq)[...].astype(F32)
        for o in range(1, ns):
            came(name + "b", o - 1, SEQ_AXIS, -o, ref(name, "_in").at[o - 1])
            total = total + ref(name, "_in")[o - 1].astype(F32)
        mine = result(name, dp, seq)
        mine[...] = total.astype(mine.dtype)
        for o in range(1, ns):
            link(name + "c", o - 1, SEQ_AXIS, o, mine, mine).start()
        link(name + "d", 0, DP_AXIS, 1, mine, mine).start()

    def total_d(name):
        for o in range(1, ns):
            piece = result(name, dp, other(SEQ_AXIS, -o))
            came(name + "c", o - 1, SEQ_AXIS, -o, piece)
            link(name + "d", o, DP_AXIS, 1, piece, piece).start()

    def total_e(name):
        for o in range(ns):
            came(name + "d", o, DP_AXIS, 1, result(name, 1 - dp, other(SEQ_AXIS, -o)))
            sent(name + "d", o, DP_AXIS, 1, result(name, dp, other(SEQ_AXIS, -o)))
        for o in range(1, ns):
            sent(name + "b", o - 1, SEQ_AXIS, o, piece_of(name, ref(name, "_mine"), other(SEQ_AXIS, o)))
            sent(name + "c", o - 1, SEQ_AXIS, o, result(name, dp, seq))

    total_a(WO, r.gw_out).start()
    total_a(WG, r.gw_gate).start()

    def chain_back(i):
        k = ns - 1 - i
        slot = jnp.maximum(lax.rem(seq - k + ns, ns) - 1, 0)

        @pl.when(k > seq)
        def _():
            r.end[...] = r.carry_in[slot] * r.end[...] + r.back_in[slot].astype(F32)

    if direct:
        for o in range(1, ns):
            came(BACK, o - 1, SEQ_AXIS, -o, r.back_in.at[o - 1])
            came(CARRY, o - 1, SEQ_AXIS, -o, r.carry_in.at[o - 1])
        r.end[...] = jnp.zeros_like(r.end)
        repeat(ns, chain_back)
    else:
        pass_back()
    r.g_dt[...] = jnp.zeros_like(r.g_dt)
    r.g_log[...] = jnp.zeros_like(r.g_log)
    r.g_skip[...] = jnp.zeros_like(r.g_skip)
    r.g_conv[...] = jnp.zeros_like(r.g_conv)
    r.gw_bc[...] = jnp.zeros_like(r.gw_bc)
    r.g_norm[...] = jnp.zeros_like(r.g_norm)

    def back(c):
        rows = at(c)
        around = pl.ds(pl.multiple_of(c * BLOCK, BLOCK), BLOCK + EDGE)
        inside = pl.ds(pl.multiple_of(c * BLOCK + EDGE, EDGE), BLOCK)
        b_mat, c_full = r.b[rows, :], r.c[rows, :]
        c_mat = c_full.astype(BF16)
        v = r.tok[rows, 0:heads]
        step = r.tok[rows, STEP : STEP + heads]
        cum, cumt, aux = r.tok[rows, CUM : CUM + heads], r.cumt[:, at(c)], r.tok[rows, AUX : AUX + 8]
        mask = jnp.where((row <= col) & (aux[:, 0:1] == doc_row(c)), 0.0, NEG)
        scores = score_pair(c_full, b_mat, False)
        d_scores = jnp.zeros((BLOCK, BLOCK), F32)
        d_b = jnp.zeros((BLOCK, state), F32)
        d_c = jnp.zeros((BLOCK, state), F32)
        d_step_own = jnp.zeros((BLOCK, heads), F32)
        d_cum = r.tok[rows, DYY : DYY + heads]
        through = jnp.zeros((1, heads), F32)

        def conv_grad(d_u, window, pre, sig, cols):
            d_pre = d_u * (sig * (1.0 + pre * (1.0 - sig)))
            for k in range(n_taps):
                shifted = window[EDGE - k : EDGE - k + BLOCK]
                r.g_conv[k : k + 1, cols] += jnp.sum(d_pre * shifted, axis=0, keepdims=True)
            r.g_conv[n_taps : n_taps + 1, cols] += jnp.sum(d_pre, axis=0, keepdims=True)
            r.cin[inside, cols] = d_pre

        for pair in range(heads // 2):
            cols = slice(pair * lanes, (pair + 1) * lanes)
            window = r.cin[around, cols]
            pre = conv_pre(window, taps[:, cols])
            sig = sigmoid(pre)
            xh = pre * sig
            step_e, to_end_e, into_e = (expand_tok(rows, sel, cols) for sel in (r.sel_step, r.sel_end, r.sel_into))
            xs = xh * step_e
            xsb = xs.astype(BF16)
            dyb = r.dy[rows, cols]
            dy = dyb.astype(F32)
            adj = r.end[:, cols]
            dye = dy * into_e
            d_c = d_c + dot3(dye, r.inc[c, :, cols], NT)
            d_b = d_b + dot3(xs * to_end_e, adj, NT)
            d_xs_inter = to_end_e * dot(b_mat, adj.astype(BF16))
            two = split(dyb)
            mixed = []
            for i, h in enumerate((2 * pair, 2 * pair + 1)):
                decay = jnp.exp(cumt[h : h + 1, :] - cum[:, h : h + 1] + mask)
                mixed.append((scores * decay).astype(BF16))
                d_scores = d_scores + dot(xsb, two[i], NT) * decay
            d_xs_intra = dot(jnp.concatenate(mixed, axis=1), jnp.concatenate(two, axis=0))
            d_xs = d_xs_intra + d_xs_inter
            collect = r.collect[cols, :]
            d_step_own = d_step_own + dot_left(xh * d_xs, collect)
            lost = skip[:, cols] * (dy * xh) + (xsb.astype(F32) * d_xs_intra + xs * d_xs_inter)
            d_cum = d_cum - dot_left(lost, collect)
            ended = jnp.sum(adj * r.inc[c + 1, :, cols], axis=0, keepdims=True)
            through = through + dot_left(ended, collect)
            r.g_skip[:, cols] += jnp.sum(dy * xh, axis=0, keepdims=True)
            r.end[:, cols] = r.kept[c, :, cols] * adj + dot(c_mat, dye.astype(BF16), TN)
            conv_grad(skip[:, cols] * dy + step_e * d_xs, window, pre, sig, cols)
        d_sb = d_scores.astype(BF16)
        d_b = d_b + dot(d_sb, c_mat)
        d_c = d_c + dot(d_sb, b_mat, TN)
        cols = slice(inner, channels)
        window = r.cin[around, cols]
        pre = conv_pre(window, taps[:, cols])
        conv_grad(jnp.concatenate([d_b, d_c], axis=1), window, pre, sigmoid(pre), cols)
        d_la = (dot_right(r.upper[...], d_cum) + through) * aux[:, 2:3]
        r.g_log[...] += jnp.sum(rate * step * d_la, axis=0, keepdims=True)
        d_v = (d_step_own + rate * d_la) * sigmoid(v)
        r.g_dt[...] += jnp.sum(d_v, axis=0, keepdims=True)
        r.dstep[rows, :] = d_v.astype(BF16)

    def project_back(c):
        rows = at(c)
        window = r.cin[pl.ds(pl.multiple_of(c * BLOCK + EDGE, EDGE), BLOCK + EDGE), :]
        d_in = taps[0:1, :] * window[:BLOCK]
        for k in range(1, n_taps):
            d_in = d_in + taps[k : k + 1, :] * window[k : k + BLOCK]
        d_val = d_in[:, :inner].astype(BF16)
        dstep = r.dstep[rows, :]
        normed = r.normed[rows, :]
        r.gw_value[...] += dot(normed, d_val, TN)
        r.pack[0:heads, :] += dot(dstep, normed, TN)
        d_part = dot(r.dz[rows, :], r.wg[...], NT) + dot(d_val, r.wv[...], NT) + dot(dstep, r.ws[...])
        scatter_sent(OUT, 6 * c, out_block(c))
        r.parts[c, :, :width] = d_part.astype(BF16)
        r.parts[c, :, width:] = d_in[:, inner:].astype(BF16)
        scatter_1(PART, 6 * c, part_block(c), r.part_in)

    def part_block(c):
        half = slab // 2
        return lambda h, i: r.parts.at[c, pl.ds(pl.multiple_of(h * slab + i * half, half), half)]

    def combine(c):
        scatter_2(PART, 6 * c, part_block(c), r.part_in)

    def slab_of(c):
        return lambda h: r.normed.at[pl.ds(pl.multiple_of(c * BLOCK + h * slab, slab), slab)]

    def slab_half(c):
        half = slab // 2
        return lambda h, i: r.normed.at[pl.ds(pl.multiple_of(c * BLOCK + h * slab + i * half, half), half)]

    def forward(c):
        gather_2(GRAD, 4 * c, slab_of(c), slab_half(c))

    def own_slab(c):
        return pl.ds(pl.multiple_of(c * BLOCK + head * slab, slab), slab)

    def finish(c):
        rows = own_slab(c)
        total = jnp.concatenate(scatter_3(PART, 6 * c, part_block(c), r.part_in), axis=0)
        x = r.x[rows, :].astype(F32)
        norm = lax.rsqrt(jnp.mean(x * x, axis=1, keepdims=True) + EPS)
        xr = x * norm
        d_bc = total[:, width:].astype(BF16)
        d_normed = total[:, :width] + dot(d_bc, r.wbc[...], NT)
        r.gw_bc[...] += dot(r.normed[rows, :], d_bc, TN)
        r.g_norm[...] += jnp.sum(d_normed * xr, axis=0, keepdims=True)
        q = d_normed * gain
        d_x = norm * q - xr * (norm * norm * jnp.mean(q * x, axis=1, keepdims=True))
        cot = jnp.concatenate([r.cot_all[k, rows, :] for k in range(nh)], axis=1)
        r.normed[rows, :] = (d_x + cot.astype(F32)).astype(BF16)
        gather_1(GRAD, 4 * c, slab_of(c))

    def add_residual(c):
        cols = pl.ds(pl.multiple_of(head * part, part), part)
        half = BLOCK // 2
        for i, total in enumerate(scatter_3(OUT, 6 * c, out_block(c), r.out_in)):
            rows = pl.ds(pl.multiple_of(c * BLOCK + i * half, half), half)
            scaled = r.tok[rows, RMS : RMS + 1] * total
            r.block_out[rows, :] = (scaled + r.x[rows, cols].astype(F32)).astype(BF16)

    def reverse(t):
        c = blocks - 1 - t
        back(c)

        @pl.when(t == 0)
        def _():
            total_b(WO, r.gw_out)
            total_b(WG, r.gw_gate)
            r.gw_value[...] = jnp.zeros_like(r.gw_value)

        @pl.when(t >= 1)
        def _():
            add_residual(c)
            project_back(c)

        @pl.when(t >= 2)
        def _():
            combine(c + 1)

        @pl.when(t == 2)
        def _():
            total_c(WO)
            total_c(WG)

        @pl.when(t >= LAG)
        def _():
            finish(c + LAG - 1)

        @pl.when(t == 4)
        def _():
            total_d(WO)
            total_d(WG)

    repeat(blocks, reverse)

    first_rows = r.cin.at[pl.ds(EDGE, EDGE)]
    last_rows = r.cin.at[pl.ds(EDGE + tokens, EDGE)]
    link(EDGES, 0, SEQ_AXIS, -1, first_rows, last_rows).start()
    order = [*range(blocks - 2, -1, -1), blocks - 1]
    waiting = order[max(blocks - LAG, 0) :]
    add_residual(blocks - 1)
    combine(0)
    came(EDGES, 0, SEQ_AXIS, 1, last_rows)

    @pl.when(seq == ns - 1)
    def _():
        r.cin[EDGE + tokens :, :] = jnp.zeros((EDGE, channels), F32)

    project_back(blocks - 1)
    total_a(WV, r.gw_value).start()
    r.pack[9 : 9 + n_taps + 1, :channels] = r.g_conv[: n_taps + 1, :]
    r.pack[14:15, :inner] = r.g_gain[...]
    r.pack[15:16, 0:heads] = r.g_dt[...]
    r.pack[15:16, 128 : 128 + heads] = r.g_log[...]
    r.pack[15:16, 256 : 256 + heads] = dot_left(r.g_skip[...], r.collect[...])
    for c in waiting[:-2]:
        finish(c)
    total_b(WV, r.gw_value)
    finish(0)
    combine(blocks - 1)
    for c in order[:-2]:
        forward(c)
    finish(blocks - 1)

    r.pack[8:9, :] = r.g_norm[...]
    quarter = width // nh
    r.bc_out[...] = r.gw_bc[...].astype(BF16)
    r.pack_out[...] = r.pack[8:16, :]
    for o in range(1, nh):
        rows = pl.ds(pl.multiple_of(other(HEAD_AXIS, o) * quarter, quarter), quarter)
        link(BC, o - 1, HEAD_AXIS, o, r.bc_out.at[rows], r.bc_in[o - 1]).start()
        link(PACK1, o - 1, HEAD_AXIS, o, r.pack_out, r.pack1_in.at[o - 1]).start()
    for o in range(1, nh):
        came(PACK1, o - 1, HEAD_AXIS, -o, r.pack1_in.at[o - 1])
        r.pack[8:9, :] += r.pack1_in[o - 1, 0:1, :]
        r.pack[9 : 9 + n_taps + 1, inner:channels] += r.pack1_in[o - 1, 1 : 2 + n_taps, inner:channels]
    link(PACK2, 0, DP_AXIS, 1, r.pack, r.pack2_in).start()
    rows = pl.ds(pl.multiple_of(head * quarter, quarter), quarter)
    mine = r.gw_bc[rows, :]
    for o in range(1, nh):
        came(BC, o - 1, HEAD_AXIS, -o, r.bc_in[o - 1])
        mine = mine + r.bc_in[o - 1][...].astype(F32)
    r.gw_q[...] = mine
    total_a(WQ, r.gw_q).start()
    came(PACK2, 0, DP_AXIS, 1, r.pack2_in)
    link(PACK2, 0, DP_AXIS, 1, r.pack, r.pack2_in).wait_send()
    r.pack[...] += r.pack2_in[...]
    for o in range(1, ns):
        link(PACK3, o - 1, SEQ_AXIS, o, r.pack, r.pack3_in.at[o - 1]).start()
    for c in order[-2:]:
        forward(c)
    total_b(WQ, r.gw_q)
    total_c(WV)
    total_c(WQ)
    total_d(WV)
    total_d(WQ)
    total_e(WQ)
    for o in range(nh):
        rows = pl.ds(pl.multiple_of(other(HEAD_AXIS, o) * quarter, quarter), quarter)
        if o == 0:
            r.bc_sum[rows, :] = r.wq_sum[...].astype(BF16)
            mine = r.bc_sum.at[rows]
        else:
            link(BCG, o - 1, HEAD_AXIS, o, mine, mine).start()
    total = r.pack[...]
    for o in range(1, ns):
        came(PACK3, o - 1, SEQ_AXIS, -o, r.pack3_in.at[o - 1])
        total = total + r.pack3_in[o - 1]
    r.small[...] = total
    total_e(WO)
    total_e(WG)
    total_e(WV)
    for o in range(1, nh):
        rows = pl.ds(pl.multiple_of(other(HEAD_AXIS, -o) * quarter, quarter), quarter)
        came(BCG, o - 1, HEAD_AXIS, -o, r.bc_sum.at[rows])
        sent(BCG, o - 1, HEAD_AXIS, o, mine)
        rows = pl.ds(pl.multiple_of(other(HEAD_AXIS, o) * quarter, quarter), quarter)
        sent(BC, o - 1, HEAD_AXIS, o, r.bc_out.at[rows])
        sent(PACK1, o - 1, HEAD_AXIS, o, r.pack_out)
    for o in range(1, ns):
        sent(PACK3, o - 1, SEQ_AXIS, o, r.pack)
        if direct:
            sent(BACK, o - 1, SEQ_AXIS, o, r.back_out)
            sent(CARRY, o - 1, SEQ_AXIS, o, r.carry)
    sent(HALO, 0, SEQ_AXIS, 1, x_tail)
    sent(HALO, 1, SEQ_AXIS, 1, r.doc_out)
    sent(EDGES, 0, SEQ_AXIS, -1, first_rows)

    @pl.when(seq < ns - 1)
    def _():
        for pair in range(pairs):
            sent(ENDS, pair, SEQ_AXIS, 1, r.end_out.at[pair])

    def drain(c):
        for o in range(1, nh):
            sent(SUM, c * (nh - 1) + o - 1, HEAD_AXIS, o, r.sum_out.at[c])
        scatter_sent(PART, 6 * c, part_block(c))
        gather_3(GRAD, 4 * c, slab_of(c), slab_half(c))

    repeat(blocks, drain)
    done = pltpu.make_async_copy(r.normed, r.grad_in, r.load.at[0])
    done.start()
    done.wait()


def write_kernel(n, *refs):
    small = refs[n]
    for source, target in zip(refs[:n], refs[n + 1 :]):
        target[...] = source[...].astype(target.dtype)
    norm, step, conv_v, conv_b, dt, log, skip, gain = refs[2 * n + 1 :]
    inner, heads, taps = conv_v.shape[1], dt.shape[1], conv_v.shape[0]

    @pl.when(pl.program_id(0) == 0)
    def _():
        norm[...] = small[8:9, :]
        step[...] = small[0:heads, :]
        conv_v[...] = small[9 : 9 + taps, :inner]
        conv_b[...] = small[9 : 9 + taps, inner : inner + conv_b.shape[1]]
        dt[...] = small[15:16, 0:heads]
        log[...] = small[15:16, 128 : 128 + heads]
        skip[...] = small[15:16, 256 : 256 + heads]
        gain[...] = small[14:15, :inner]


def on_device(
    hidden_in, doc_ids, norm_gain, w_gate, w_value, w_bc, w_step, conv_value, conv_bc, dt_bias, a_log, d_skip,
    out_gain, w_out, cotangent,
):
    x, cot = hidden_in[0], cotangent[0]
    tokens, width = x.shape
    inner, heads = w_gate.shape[1], w_step.shape[1]
    bc_width, head_dim = w_bc.shape[1], inner // heads
    state = bc_width // 2
    channels = inner + bc_width
    blocks = tokens // BLOCK
    nh, ns = lax.axis_size(HEAD_AXIS), lax.axis_size(SEQ_AXIS)
    part, slab = width // nh, BLOCK // nh
    n_taps = conv_value.shape[0] - 1
    vmem, hbm = pltpu.VMEM, pl.ANY
    inbox = ns - 1 if ns <= DIRECT else 1
    inputs = dict(
        x=x, cot=cot, docs=doc_ids, gain=norm_gain[None], wg=w_gate, wv=w_value, wbc=w_bc,
        ws=w_step.T, wo=w_out, cv=conv_value, cb=conv_bc, dtb=dt_bias[None], alog=a_log[None],
        dskip=d_skip[None], og=out_gain[None],
    )
    outputs = dict(
        block_out=((tokens, part), BF16),
        grad_in=((tokens, width), BF16),
        wg_sum=(w_gate.shape, BF16),
        wv_sum=(w_value.shape, BF16),
        wo_sum=(w_out.shape, BF16),
        bc_sum=(w_bc.shape, BF16),
        small=((16, width), F32),
    )
    scratch = dict(
        cot_all=vmem((nh, tokens, part), BF16),
        halo_x=vmem((TAIL, width), BF16),
        doc_out=vmem((8, 128), F32),
        doc_in=vmem((8, 128), F32),
        doc_prev=vmem((8, 128), F32),
        upper=vmem((BLOCK, BLOCK), BF16),
        eye=vmem((BLOCK, BLOCK), BF16),
        spread=vmem((heads, inner), BF16),
        collect=vmem((inner, heads), BF16),
        normed=vmem((tokens, width), BF16),
        z=vmem((tokens, inner), F32),
        cin=vmem((EDGE + tokens + EDGE, channels), F32),
        y=vmem((tokens, inner), F32),
        xs=vmem((tokens, inner), BF16),
        dy=vmem((tokens, inner), BF16),
        b=vmem((tokens, state), BF16),
        c=vmem((tokens, state), F32),
        tok=vmem((tokens, 128), F32),
        cumt=vmem((heads, tokens), F32),
        dstep=vmem((tokens, heads), BF16),
        inc=vmem((blocks + 1, state, inner), F32),
        kept=vmem((blocks, 1, inner), F32),
        end=vmem((state, inner), F32),
        own=vmem((heads // 2, state, 2 * head_dim), F32),
        end_out=vmem((heads // 2, state, 2 * head_dim), F32),
        end_in=vmem((heads // 2, state, 2 * head_dim), F32),
        carry_part=vmem((heads // 2, 1, 2 * head_dim), F32),
        sel_step=vmem((128, inner), BF16),
        sel_end=vmem((128, inner), BF16),
        sel_into=vmem((128, inner), BF16),
        back_out=vmem((state, inner), BF16),
        back_in=vmem((inbox, state, inner), BF16),
        carry=vmem((1, inner), F32),
        carry_in=vmem((inbox, 1, inner), F32),
        prod=vmem((1, inner), F32),
        sum_out=vmem((blocks, 8, BLOCK), F32),
        sum_in=vmem((blocks * (nh - 1), 8, BLOCK), F32),
        parts=vmem((blocks, BLOCK, width + bc_width), BF16),
        out_in=vmem((blocks * 6, BLOCK // 2, part), BF16),
        part_in=vmem((blocks * 6, slab // 2, width + bc_width), BF16),
        gw_out=vmem(w_out.shape, F32),
        wq_sum=vmem((width // nh, bc_width), F32),
        dz=vmem((tokens, inner), BF16),
        g_gain=vmem((1, inner), F32),
        g_dt=vmem((1, heads), F32),
        g_log=vmem((1, heads), F32),
        g_skip=vmem((1, inner), F32),
        g_conv=vmem((8, channels), F32),
        g_norm=vmem((1, width), F32),
        pack=vmem((16, width), F32),
        pack_out=vmem((8, width), F32),
        pack1_in=vmem((nh - 1, 8, width), F32),
        pack2_in=vmem((16, width), F32),
        pack3_in=vmem((ns - 1, 16, width), F32),
        load=pltpu.SemaphoreType.DMA((1,)),
    )
    for name, (rows, cols), kind in (
        (WO, (inner, width // 2), BF16), (WG, (width // 2, inner), BF16), (WV, (width // 2, inner), BF16),
        (WQ, (width // nh, state), F32),
    ):
        if name != WV:
            scratch[name + "_pair"] = vmem((rows, cols), F32)
            scratch[name + "_mine"] = vmem((rows, cols), kind)
        scratch[name + "_in"] = vmem((ns - 1, rows // ns, cols), kind)
    counts = dict(
        cot=4, halo=2, ends=heads // 2, carry=ns - 1, back=ns - 1, sum=blocks * (nh - 1), out=blocks * 6,
        part=blocks * 6, grad=blocks * 4, edge=1, bc=nh - 1, bcg=nh - 1, pack1=nh - 1, pack2=1, pack3=ns - 1,
    )
    for name in (WO, WG, WV, WQ):
        counts |= {name + "a": 1, name + "b": ns - 1, name + "c": ns - 1, name + "d": ns}
    for name, n in counts.items():
        scratch[name + "_s"] = pltpu.SemaphoreType.DMA((n,))
        scratch[name + "_r"] = pltpu.SemaphoreType.DMA((n,))
    names = [*inputs, *outputs, *scratch]

    def run(*refs):
        r = types.SimpleNamespace(**dict(zip(names, refs)))
        quarter = width // nh
        r.gw_gate = r.gw_value = r.z.at[pl.ds(0, width)]
        r.wv_pair = r.z.at[pl.ds(width, width // 2)]
        r.gw_bc = r.y.at[pl.ds(0, width), pl.ds(0, bc_width)]
        r.gw_q = r.y.at[pl.ds(width, quarter), pl.ds(0, bc_width)]
        r.bc_out = r.xs.at[pl.ds(0, width), pl.ds(0, bc_width)]
        r.wv_mine = r.xs.at[pl.ds(width, width // 2)]
        r.bc_in = [r.dz.at[pl.ds(o * quarter, quarter), pl.ds(0, bc_width)] for o in range(nh - 1)]
        kernel(r)

    block_out, grad_in, g_gate, g_value, g_out, g_bc, small = pl.pallas_call(
        run,
        out_shape=[jax.ShapeDtypeStruct(*o) for o in outputs.values()],
        in_specs=[pl.BlockSpec(memory_space=hbm if name == "cot" else vmem) for name in inputs],
        out_specs=[pl.BlockSpec(memory_space=hbm if name == "grad_in" else vmem) for name in outputs],
        scratch_shapes=list(scratch.values()),
        compiler_params=pltpu.CompilerParams(
            collective_id=0, has_side_effects=True, vmem_limit_bytes=VMEM_LIMIT
        ),
        name="block",
    )(*inputs.values())
    steps = 8
    grads = (block_out, grad_in, g_gate, g_value, g_out, g_bc)
    kinds = (BF16, BF16, F32, F32, F32, F32)
    tiny = ((1, width), (heads, width), (n_taps + 1, inner), (n_taps + 1, bc_width), (1, heads), (1, heads), (1, heads),
            (1, inner))

    def split_rows(a):
        return pl.BlockSpec((a.shape[0] // steps, a.shape[1]), lambda i: (i, 0))

    def whole(dims):
        return pl.BlockSpec(dims, lambda i: (0, 0))

    outs = pl.pallas_call(
        functools.partial(write_kernel, len(grads)),
        grid=(steps,),
        in_specs=[*map(split_rows, grads), whole(small.shape)],
        out_specs=[*map(split_rows, grads), *map(whole, tiny)],
        out_shape=[jax.ShapeDtypeStruct(a.shape, k) for a, k in zip(grads, kinds)]
        + [jax.ShapeDtypeStruct(dims, F32) for dims in tiny],
        compiler_params=pltpu.CompilerParams(vmem_limit_bytes=VMEM_LIMIT),
        name="write",
    )(*grads, small)
    block_out, grad_in, g_gate, g_value, g_out, g_bc, g_norm, g_step, g_cv, g_cb, g_dt, g_log, g_skip, g_gain = outs
    return (
        block_out[None], grad_in[None], g_norm[0], g_gate, g_value, g_bc, g_step.T, g_cv, g_cb, g_dt[0], g_log[0],
        g_skip[0], g_gain[0], g_out,
    )


def solution(mesh):
    return jax.shard_map(
        on_device,
        mesh=mesh,
        in_specs=(
            P(DP_AXIS, SEQ_AXIS, None),
            P(DP_AXIS, SEQ_AXIS),
            P(),
            P(None, HEAD_AXIS),
            P(None, HEAD_AXIS),
            P(),
            P(None, HEAD_AXIS),
            P(None, HEAD_AXIS),
            P(),
            P(HEAD_AXIS),
            P(HEAD_AXIS),
            P(HEAD_AXIS),
            P(HEAD_AXIS),
            P(HEAD_AXIS, None),
            P(DP_AXIS, SEQ_AXIS, HEAD_AXIS),
        ),
        out_specs=(
            P(DP_AXIS, SEQ_AXIS, HEAD_AXIS),
            P(DP_AXIS, SEQ_AXIS, None),
            P(),
            P(None, HEAD_AXIS),
            P(None, HEAD_AXIS),
            P(),
            P(None, HEAD_AXIS),
            P(None, HEAD_AXIS),
            P(),
            P(HEAD_AXIS),
            P(HEAD_AXIS),
            P(HEAD_AXIS),
            P(HEAD_AXIS),
            P(HEAD_AXIS, None),
        ),
        check_vma=False,
    )
```

time: 1200 us -> 219 us (0.18); the launches traced: 1190 us -> 219 us
  local copies, waits for them, and re-layouts: 354 us -> 0 us
  matrix products: 246 us -> 0 us
  waiting for transfers between devices: 230 us -> 0 us
  Pallas kernels: 0 us -> 218 us
  other arithmetic: 217 us -> 0 us
  blocking collectives: 97.2 us -> 0 us
  between operations: 17.3 us -> 0.84 us
  starting transfers between devices: 14.2 us -> 0 us
    dot_general x90 -> x0, matrix products: 246 us -> none  [the longest x18 69.8 us: ssd_block(): y_intra = jnp.einsum('tsh,shp->thp', mixing, x_heads, precision=HIGHEST)]
    psum x3 -> x0, waiting for transfers between devices: 219 us -> none  [the longest x1 117 us: on_device(): lax.psum((g_norm_gain, g_w_gate, g_w_value, g_w_bc, g_w_step, g_conv_valu...]
    pallas_call x0 -> x2, Pallas kernels: none -> 218 us  [the longest x1 209 us: on_device(): pl.pallas_call(run, out_shape=[jax.ShapeDtypeStruct(*o) for o in outputs....]
    dynamic_update_slice x54 -> x0, local copies, waits for them, and re-layouts: 173 us -> none  [local_mix(): final_carry, block_ys = lax.scan(ssd_block, init_carry, blocks)]
    dynamic_slice x54 -> x0, local copies, waits for them, and re-layouts: 80.7 us -> none  [local_mix(): final_carry, block_ys = lax.scan(ssd_block, init_carry, blocks)]
    dynamic_update_slice x48 -> x0, other arithmetic: 70.9 us -> none  [local_mix(): final_carry, block_ys = lax.scan(ssd_block, init_carry, blocks)]
    psum x4 -> x0, blocking collectives: 58.7 us -> none  [the longest x1 31.5 us: on_device(): lax.psum((g_norm_gain, g_w_gate, g_w_value, g_w_bc, g_w_step, g_conv_valu...]
    reduce_sum x25 -> x0, other arithmetic: 43.9 us -> none  [the longest x1 9.69 us: local_mix(): taps_all[offset] * ext_in[n_edge - offset:n_edge - offset + tokens]]
  transfers between devices with their start and end apart: 8 -> 0, of which waited for: 4 -> 0; matrix products, arithmetic and copies ran while one was open for 31% -> 0% of each run, Pallas kernels for 0% -> 0%
where the time goes in v2:
time: 219 us
  Pallas kernels  218 us (100%)
    pallas_call x1, Pallas kernels, on_device(): pl.pallas_call(run, out_shape=[jax.ShapeDtypeStruct(*o) for o in outputs....  209 us
    pallas_call x1, Pallas kernels, on_device(): pl.pallas_call(functools.partial(write_kernel, len(grads)), grid=(steps,)...  9.16 us

profile of v2, /device:TPU:0, one launch (start us, length us, event | category | flops | bytes accessed | tf_op | source)
XLA Modules:
  0.0 218.9 jit_solution(9079596880504148000)
XLA Ops:
  0.7 208.9 %block.1 = (bf16[1536,256]{1,0:T(8,128)(2,1)}, bf16[1536,1024]{1,0:T(8,128)(2,1)}, bf16[1024,512]{1,0:T(8,128)(2,1)}, bf16[1024,512]{1,0:T(8,128)(2,1)}, bf16[51...) custom-call(bf16[1536,1024]{1,0:T(8,128)(2,1)} %bitcast.16, bf16[1536,256]{1,0:T(8,128)(2,1)} %bitcast.17, ...), custom_call_target="tpu_custom_call" | custom-call | tf_op jit(solution)/shard_map/block/pallas_call | solution.py:949
  209.5 9.2 %write.1 = (bf16[1536,256]{1,0:T(8,128)(2,1)}, bf16[1536,1024]{1,0:T(8,128)(2,1)}, f32[1024,512]{1,0:T(8,128)}, f32[1024,512]{1,0:T(8,128)}, f32[512,1024]{1,0:T...) custom-call(bf16[1536,256]{1,0:T(8,128)(2,1)} %get-tuple-element.35., ...), custom_call_target="tpu_custom_call" | custom-call | tf_op jit(solution)/shard_map/write/pallas_call | solution.py:972

commit v3 on v2

--- a/solution.py
+++ b/solution.py
@@ -20,13 +20,13 @@
 TN = (((0,), (0,)), ((), ()))
 MESH = pl.DeviceIdType.MESH
 CUM, AUX, DYY, STEP, TO_END, INTO, RMS = 8, 16, 24, 32, 40, 48, 56
-DIRECT = 8
 LAG = 4
 HEAD_AXIS, SEQ_AXIS, DP_AXIS = "head", "seq", "dp"
-COT, HALO, ENDS, CARRY, BACK, SUM, OUT, PART, GRAD, EDGES, BC, BCG, PACK1, PACK2, PACK3 = (
-    "cot", "halo", "ends", "carry", "back", "sum", "out", "part", "grad", "edge", "bc", "bcg", "pack1", "pack2", "pack3"
+COT, HALO, ENDS, NORM, BACK, SUM, OUT, PART, GRAD, EDGES, BC, BCG, PACK1 = (
+    "cot", "halo", "ends", "norm", "back", "sum", "out", "part", "grad", "edge", "bc", "bcg", "pack1"
 )
-WO, WG, WV, WQ = "wo", "wg", "wv", "wq"
+WO, WG, WV, WQ, WP = "wo", "wg", "wv", "wq", "wp"
+PIECES = {WO: 4, WG: 4, WV: 4, WQ: 1, WP: 1}
 VMEM_LIMIT = 63 * 1024 * 1024
 
 
@@ -61,7 +61,7 @@
 
 
 def sigmoid(v):
-    return 1.0 / (1.0 + jnp.exp(-v))
+    return 0.5 * jnp.tanh(0.5 * v) + 0.5
 
 
 def softplus(v):
@@ -225,7 +225,6 @@
         rows = at(c)
         normed = in_norm(r.x[rows, :].astype(F32), gain)
         r.normed[rows, :] = normed
-        r.z[rows, :] = dot(normed, r.wg[...])
         inside = pl.ds(pl.multiple_of(c * BLOCK + EDGE, EDGE), BLOCK)
         r.cin[inside, :inner] = dot(normed, r.wv[...])
         r.cin[inside, inner:] = dot(normed, r.wbc[...])
@@ -276,16 +275,12 @@
     repeat(blocks, steps)
 
     pairs = heads // 2
-    direct = ns <= DIRECT
-    if direct:
-        for o in range(1, ns):
-            link(CARRY, o - 1, SEQ_AXIS, o, r.carry, r.carry_in.at[o - 1]).start()
     for pair in range(pairs):
         r.carry_part[pair] = r.carry[:, pair * lanes : (pair + 1) * lanes]
     r.own[...] = jnp.zeros_like(r.own)
 
     def relay(turn):
-        pair = turn - seq
+        pair = turn - 2 * seq
 
         @pl.when(jnp.logical_and(pair >= 0, pair < pairs))
         def _():
@@ -321,19 +316,20 @@
 
     gather_2(COT, 0, cot_of, cot_half)
 
-    def pass_back():
-        @pl.when(seq < ns - 1)
+    def relay_back(turn):
+        distance = ns - 1 - seq
+        pair = turn - 2 * distance
+
+        @pl.when(jnp.logical_and(distance > 0, jnp.logical_and(pair >= 0, pair < pairs)))
         def _():
-            came(BACK, 0, SEQ_AXIS, 1, r.back_in.at[0])
-
-        into = jnp.where(seq < ns - 1, r.back_in[0].astype(F32), 0.0)
-        r.back_out[...] = (r.carry[...] * into + r.end[...]).astype(BF16)
-        r.end[...] = into
-
-        @pl.when(seq > 0)
-        def _():
-            link(BACK, 0, SEQ_AXIS, -1, r.back_out, r.back_in.at[0]).start()
-            sent(BACK, 0, SEQ_AXIS, -1, r.back_out)
+            came(BACK, pair, SEQ_AXIS, 1, r.back_in.at[pair])
+            into = r.back_in[pair].astype(F32)
+            r.back_out[pair] = (r.carry_part[pair] * into + r.own[pair]).astype(BF16)
+            r.own[pair] = into
+
+            @pl.when(seq > 0)
+            def _():
+                link(BACK, pair, SEQ_AXIS, -1, r.back_out.at[pair], r.back_in.at[pair]).start()
 
     first = iota((BLOCK, lanes), 1) < lanes // 2
 
@@ -354,12 +350,13 @@
                 mixed.append((scores * decay).astype(BF16))
             two = jnp.concatenate(split(r.xs[rows, cols]), axis=0)
             r.y[rows, cols] += dot(jnp.concatenate(mixed, axis=1), two)
+        r.z[rows, :] = dot(r.normed[rows, :], r.wg[...])
         relay(pairs + c)
 
     repeat(blocks, intra)
 
-    if ns - 1 > blocks:
-        repeat(ns - 1 - blocks, lambda i: relay(pairs + blocks + i))
+    if 2 * (ns - 1) > blocks:
+        repeat(2 * (ns - 1) - blocks, lambda i: relay(pairs + blocks + i))
     for pair in range(pairs):
         r.end[:, pair * lanes : (pair + 1) * lanes] = r.own[pair]
     gather_3(COT, 0, cot_of, cot_half)
@@ -434,10 +431,15 @@
 
     repeat(blocks, gate)
 
-    if direct:
-        r.back_out[...] = r.end[...].astype(BF16)
-        for o in range(1, ns):
-            link(BACK, o - 1, SEQ_AXIS, o, r.back_out, r.back_in.at[o - 1]).start()
+    for pair in range(pairs):
+        r.own[pair] = r.end[:, pair * lanes : (pair + 1) * lanes]
+
+    @pl.when(seq == ns - 1)
+    def _():
+        for pair in range(pairs):
+            r.back_out[pair] = r.own[pair].astype(BF16)
+            link(BACK, pair, SEQ_AXIS, -1, r.back_out.at[pair], r.back_in.at[pair]).start()
+        r.own[...] = jnp.zeros_like(r.own)
 
     r.gw_out[...] = jnp.zeros_like(r.gw_out)
     r.gw_gate[...] = jnp.zeros_like(r.gw_gate)
@@ -448,6 +450,7 @@
         for k in range(nh):
             r.gw_out[:, k * part : (k + 1) * part] += dot(gn, r.cot_all[k, rows, :], TN)
         r.gw_gate[...] += dot(r.normed[rows, :], r.dz[rows, :], TN)
+        relay_back(c)
 
     repeat(blocks, weight_grads)
 
@@ -461,9 +464,16 @@
         half = source.shape[0] // 2
         return source.at[pl.ds(pl.multiple_of(core * half, half), half)]
 
-    def piece_of(name, half, place):
-        piece = half.shape[0] // ns
-        return half.at[pl.ds(pl.multiple_of(place * piece, piece), piece)]
+    near = seq < ns // 2
+    depth, last = jnp.where(near, seq, ns - 1 - seq), ns // 2 - 1
+    inward = jnp.where(near, 1, -1)
+
+    def piece_of(name, half, j):
+        rows = half.shape[0] // PIECES[name]
+        return half.at[pl.ds(j * rows, rows)]
+
+    def result(name, core, j):
+        return piece_of(name, half_of(name, ref(name, "_sum"), core), j)
 
     def total_a(name, source):
         return link(name + "a", 0, DP_AXIS, 1, half_of(name, source, 1 - dp), ref(name, "_pair"))
@@ -473,57 +483,73 @@
         came(name + "a", 0, DP_AXIS, 1, ref(name, "_pair"))
         mine = ref(name, "_mine")
         mine[...] = (half_of(name, source, dp)[...] + ref(name, "_pair")[...]).astype(mine.dtype)
-        for o in range(1, ns):
-            theirs = piece_of(name, mine, other(SEQ_AXIS, o))
-            link(name + "b", o - 1, SEQ_AXIS, o, theirs, ref(name, "_in").at[o - 1]).start()
-
-    def result(name, core, place):
-        return piece_of(name, half_of(name, ref(name, "_sum"), core), place)
+
+        @pl.when(depth == 0)
+        def _():
+            for j in range(PIECES[name]):
+                link(name + "b", j, SEQ_AXIS, inward, piece_of(name, mine, j), ref(name, "_in").at[j]).start()
 
     def total_c(name):
-        total = piece_of(name, ref(name, "_mine"), seq)[...].astype(F32)
-        for o in range(1, ns):
-            came(name + "b", o - 1, SEQ_AXIS, -o, ref(name, "_in").at[o - 1])
-            total = total + ref(name, "_in")[o - 1].astype(F32)
-        mine = result(name, dp, seq)
-        mine[...] = total.astype(mine.dtype)
-        for o in range(1, ns):
-            link(name + "c", o - 1, SEQ_AXIS, o, mine, mine).start()
-        link(name + "d", 0, DP_AXIS, 1, mine, mine).start()
+        @pl.when(depth > 0)
+        def _():
+            for j in range(PIECES[name]):
+                came(name + "b", j, SEQ_AXIS, -inward, ref(name, "_in").at[j])
+                mine = piece_of(name, ref(name, "_mine"), j)
+                mine[...] = (mine[...].astype(F32) + ref(name, "_in")[j].astype(F32)).astype(mine.dtype)
+
+                @pl.when(depth < last)
+                def _():
+                    link(name + "b", j, SEQ_AXIS, inward, mine, ref(name, "_in").at[j]).start()
+
+                @pl.when(depth == last)
+                def _():
+                    link(name + "c", j, SEQ_AXIS, inward, mine, result(name, dp, j)).start()
 
     def total_d(name):
-        for o in range(1, ns):
-            piece = result(name, dp, other(SEQ_AXIS, -o))
-            came(name + "c", o - 1, SEQ_AXIS, -o, piece)
-            link(name + "d", o, DP_AXIS, 1, piece, piece).start()
+        for j in range(PIECES[name]):
+            total = result(name, dp, j)
+
+            @pl.when(depth == last)
+            def _():
+                came(name + "c", j, SEQ_AXIS, inward, total)
+                mine = piece_of(name, ref(name, "_mine"), j)
+                total[...] = (mine[...].astype(F32) + total[...].astype(F32)).astype(mine.dtype)
+
+            @pl.when(depth < last)
+            def _():
+                came(name + "f", j, SEQ_AXIS, inward, total)
+
+            @pl.when(depth > 0)
+            def _():
+                link(name + "f", j, SEQ_AXIS, -inward, total, total).start()
+
+            link(name + "d", j, DP_AXIS, 1, total, total).start()
 
     def total_e(name):
-        for o in range(ns):
-            came(name + "d", o, DP_AXIS, 1, result(name, 1 - dp, other(SEQ_AXIS, -o)))
-            sent(name + "d", o, DP_AXIS, 1, result(name, dp, other(SEQ_AXIS, -o)))
-        for o in range(1, ns):
-            sent(name + "b", o - 1, SEQ_AXIS, o, piece_of(name, ref(name, "_mine"), other(SEQ_AXIS, o)))
-            sent(name + "c", o - 1, SEQ_AXIS, o, result(name, dp, seq))
+        for j in range(PIECES[name]):
+            total, mine = result(name, dp, j), piece_of(name, ref(name, "_mine"), j)
+            came(name + "d", j, DP_AXIS, 1, result(name, 1 - dp, j))
+            sent(name + "d", j, DP_AXIS, 1, total)
+
+            @pl.when(depth < last)
+            def _():
+                sent(name + "b", j, SEQ_AXIS, inward, mine)
+
+            @pl.when(depth == last)
+            def _():
+                sent(name + "c", j, SEQ_AXIS, inward, mine)
+
+            @pl.when(depth > 0)
+            def _():
+                sent(name + "f", j, SEQ_AXIS, -inward, total)
 
     total_a(WO, r.gw_out).start()
     total_a(WG, r.gw_gate).start()
 
-    def chain_back(i):
-        k = ns - 1 - i
-        slot = jnp.maximum(lax.rem(seq - k + ns, ns) - 1, 0)
-
-        @pl.when(k > seq)
-        def _():
-            r.end[...] = r.carry_in[slot] * r.end[...] + r.back_in[slot].astype(F32)
-
-    if direct:
-        for o in range(1, ns):
-            came(BACK, o - 1, SEQ_AXIS, -o, r.back_in.at[o - 1])
-            came(CARRY, o - 1, SEQ_AXIS, -o, r.carry_in.at[o - 1])
-        r.end[...] = jnp.zeros_like(r.end)
-        repeat(ns, chain_back)
-    else:
-        pass_back()
+    if 2 * (ns - 1) + pairs > blocks:
+        repeat(2 * (ns - 1) + pairs - blocks, lambda i: relay_back(blocks + i))
+    for pair in range(pairs):
+        r.end[:, pair * lanes : (pair + 1) * lanes] = r.own[pair]
     r.g_dt[...] = jnp.zeros_like(r.g_dt)
     r.g_log[...] = jnp.zeros_like(r.g_log)
     r.g_skip[...] = jnp.zeros_like(r.g_skip)
@@ -609,15 +635,18 @@
         d_in = taps[0:1, :] * window[:BLOCK]
         for k in range(1, n_taps):
             d_in = d_in + taps[k : k + 1, :] * window[k : k + BLOCK]
-        d_val = d_in[:, :inner].astype(BF16)
+        d_inb = d_in.astype(BF16)
+        d_val = d_inb[:, :inner]
         dstep = r.dstep[rows, :]
         normed = r.normed[rows, :]
-        r.gw_value[...] += dot(normed, d_val, TN)
+        grads = dot(normed, d_inb, TN)
+        r.gw_value[...] += grads[:, :inner]
+        r.gw_bc[...] += grads[:, inner:]
         r.pack[0:heads, :] += dot(dstep, normed, TN)
         d_part = dot(r.dz[rows, :], r.wg[...], NT) + dot(d_val, r.wv[...], NT) + dot(dstep, r.ws[...])
         scatter_sent(OUT, 6 * c, out_block(c))
         r.parts[c, :, :width] = d_part.astype(BF16)
-        r.parts[c, :, width:] = d_in[:, inner:].astype(BF16)
+        r.parts[c, :, width:] = d_inb[:, inner:]
         scatter_1(PART, 6 * c, part_block(c), r.part_in)
 
     def part_block(c):
@@ -648,7 +677,6 @@
         xr = x * norm
         d_bc = total[:, width:].astype(BF16)
         d_normed = total[:, :width] + dot(d_bc, r.wbc[...], NT)
-        r.gw_bc[...] += dot(r.normed[rows, :], d_bc, TN)
         r.g_norm[...] += jnp.sum(d_normed * xr, axis=0, keepdims=True)
         q = d_normed * gain
         d_x = norm * q - xr * (norm * norm * jnp.mean(q * x, axis=1, keepdims=True))
@@ -686,7 +714,6 @@
         @pl.when(t == 2)
         def _():
             total_c(WO)
-            total_c(WG)
 
         @pl.when(t >= LAG)
         def _():
@@ -694,8 +721,8 @@
 
         @pl.when(t == 4)
         def _():
+            total_c(WG)
             total_d(WO)
-            total_d(WG)
 
     repeat(blocks, reverse)
 
@@ -714,83 +741,99 @@
 
     project_back(blocks - 1)
     total_a(WV, r.gw_value).start()
+
+    quarter = width // nh
+
+    def quarter_of(whole, h):
+        return whole.at[pl.ds(pl.multiple_of(h * quarter, quarter), quarter)]
+
     r.pack[9 : 9 + n_taps + 1, :channels] = r.g_conv[: n_taps + 1, :]
     r.pack[14:15, :inner] = r.g_gain[...]
     r.pack[15:16, 0:heads] = r.g_dt[...]
     r.pack[15:16, 128 : 128 + heads] = r.g_log[...]
     r.pack[15:16, 256 : 256 + heads] = dot_left(r.g_skip[...], r.collect[...])
+    r.bc_out[...] = r.gw_bc[...].astype(BF16)
+    r.pack_out[...] = r.pack[8:16, :]
+    for o in range(1, nh):
+        link(PACK1, o - 1, HEAD_AXIS, o, r.pack_out, r.pack1_in.at[o - 1]).start()
+        link(BC, o - 1, HEAD_AXIS, o, quarter_of(r.bc_out, square[o]), r.bc_in[o - 1]).start()
     for c in waiting[:-2]:
         finish(c)
     total_b(WV, r.gw_value)
+    total_d(WG)
+    for o in range(1, nh):
+        came(PACK1, o - 1, HEAD_AXIS, -o, r.pack1_in.at[o - 1])
+        r.pack[9 : 9 + n_taps + 1, inner:channels] += r.pack1_in[o - 1, 1 : 2 + n_taps, inner:channels]
+    total_a(WP, r.pack).start()
     finish(0)
     combine(blocks - 1)
-    for c in order[:-2]:
-        forward(c)
-    finish(blocks - 1)
-
-    r.pack[8:9, :] = r.g_norm[...]
-    quarter = width // nh
-    r.bc_out[...] = r.gw_bc[...].astype(BF16)
-    r.pack_out[...] = r.pack[8:16, :]
-    for o in range(1, nh):
-        rows = pl.ds(pl.multiple_of(other(HEAD_AXIS, o) * quarter, quarter), quarter)
-        link(BC, o - 1, HEAD_AXIS, o, r.bc_out.at[rows], r.bc_in[o - 1]).start()
-        link(PACK1, o - 1, HEAD_AXIS, o, r.pack_out, r.pack1_in.at[o - 1]).start()
-    for o in range(1, nh):
-        came(PACK1, o - 1, HEAD_AXIS, -o, r.pack1_in.at[o - 1])
-        r.pack[8:9, :] += r.pack1_in[o - 1, 0:1, :]
-        r.pack[9 : 9 + n_taps + 1, inner:channels] += r.pack1_in[o - 1, 1 : 2 + n_taps, inner:channels]
-    link(PACK2, 0, DP_AXIS, 1, r.pack, r.pack2_in).start()
-    rows = pl.ds(pl.multiple_of(head * quarter, quarter), quarter)
-    mine = r.gw_bc[rows, :]
+    mine = quarter_of(r.gw_bc, head)[...]
     for o in range(1, nh):
         came(BC, o - 1, HEAD_AXIS, -o, r.bc_in[o - 1])
         mine = mine + r.bc_in[o - 1][...].astype(F32)
     r.gw_q[...] = mine
     total_a(WQ, r.gw_q).start()
-    came(PACK2, 0, DP_AXIS, 1, r.pack2_in)
-    link(PACK2, 0, DP_AXIS, 1, r.pack, r.pack2_in).wait_send()
-    r.pack[...] += r.pack2_in[...]
+    total_c(WV)
+    total_b(WP, r.pack)
+    total_b(WQ, r.gw_q)
+    for c in order[:2]:
+        forward(c)
+    total_c(WP)
+    total_c(WQ)
+    finish(blocks - 1)
+    for o in range(1, nh):
+        link(NORM, o - 1, HEAD_AXIS, o, r.g_norm, r.norm_in.at[o - 1]).start()
+    for c in order[2:-2]:
+        forward(c)
+    total_d(WV)
+    total_d(WP)
+    total_d(WQ)
+    total = r.g_norm[...]
+    for o in range(1, nh):
+        came(NORM, o - 1, HEAD_AXIS, -o, r.norm_in.at[o - 1])
+        total = total + r.norm_in[o - 1]
+    r.norm_out[0] = total
+    link(NORM, nh - 1, DP_AXIS, 1, r.norm_out.at[0], r.norm_in.at[nh - 1]).start()
+    forward(0)
+    total_e(WQ)
+    mine = quarter_of(r.bc_sum, head)
+    mine[...] = r.wq_sum[...].astype(BF16)
+    for o in range(1, nh):
+        link(BCG, o - 1, HEAD_AXIS, o, mine, mine).start()
+    came(NORM, nh - 1, DP_AXIS, 1, r.norm_in.at[nh - 1])
+    total = r.norm_out[0] + r.norm_in[nh - 1]
+    r.norm_out[1] = total
     for o in range(1, ns):
-        link(PACK3, o - 1, SEQ_AXIS, o, r.pack, r.pack3_in.at[o - 1]).start()
-    for c in order[-2:]:
-        forward(c)
-    total_b(WQ, r.gw_q)
-    total_c(WV)
-    total_c(WQ)
-    total_d(WV)
-    total_d(WQ)
-    total_e(WQ)
-    for o in range(nh):
-        rows = pl.ds(pl.multiple_of(other(HEAD_AXIS, o) * quarter, quarter), quarter)
-        if o == 0:
-            r.bc_sum[rows, :] = r.wq_sum[...].astype(BF16)
-            mine = r.bc_sum.at[rows]
-        else:
-            link(BCG, o - 1, HEAD_AXIS, o, mine, mine).start()
-    total = r.pack[...]
+        link(NORM, nh + o - 1, SEQ_AXIS, o, r.norm_out.at[1], r.norm_in.at[nh + o - 1]).start()
+    forward(blocks - 1)
+    for name in (WO, WG, WV, WP):
+        total_e(name)
+
+    r.norm_all[seq] = total
     for o in range(1, ns):
-        came(PACK3, o - 1, SEQ_AXIS, -o, r.pack3_in.at[o - 1])
-        total = total + r.pack3_in[o - 1]
-    r.small[...] = total
-    total_e(WO)
-    total_e(WG)
-    total_e(WV)
+        came(NORM, nh + o - 1, SEQ_AXIS, -o, r.norm_in.at[nh + o - 1])
+        r.norm_all[other(SEQ_AXIS, -o)] = r.norm_in[nh + o - 1]
+    total = r.norm_all[0]
+    for k in range(1, ns):
+        total = total + r.norm_all[k]
+    r.norm_sum[...] = total
     for o in range(1, nh):
-        rows = pl.ds(pl.multiple_of(other(HEAD_AXIS, -o) * quarter, quarter), quarter)
-        came(BCG, o - 1, HEAD_AXIS, -o, r.bc_sum.at[rows])
+        came(BCG, o - 1, HEAD_AXIS, -o, quarter_of(r.bc_sum, square[o]))
         sent(BCG, o - 1, HEAD_AXIS, o, mine)
-        rows = pl.ds(pl.multiple_of(other(HEAD_AXIS, o) * quarter, quarter), quarter)
-        sent(BC, o - 1, HEAD_AXIS, o, r.bc_out.at[rows])
+        sent(BC, o - 1, HEAD_AXIS, o, quarter_of(r.bc_out, square[o]))
         sent(PACK1, o - 1, HEAD_AXIS, o, r.pack_out)
+        sent(NORM, o - 1, HEAD_AXIS, o, r.g_norm)
+    sent(NORM, nh - 1, DP_AXIS, 1, r.norm_out.at[0])
     for o in range(1, ns):
-        sent(PACK3, o - 1, SEQ_AXIS, o, r.pack)
-        if direct:
-            sent(BACK, o - 1, SEQ_AXIS, o, r.back_out)
-            sent(CARRY, o - 1, SEQ_AXIS, o, r.carry)
+        sent(NORM, nh + o - 1, SEQ_AXIS, o, r.norm_out.at[1])
     sent(HALO, 0, SEQ_AXIS, 1, x_tail)
     sent(HALO, 1, SEQ_AXIS, 1, r.doc_out)
     sent(EDGES, 0, SEQ_AXIS, -1, first_rows)
+
+    @pl.when(seq > 0)
+    def _():
+        for pair in range(pairs):
+            sent(BACK, pair, SEQ_AXIS, -1, r.back_out.at[pair])
 
     @pl.when(seq < ns - 1)
     def _():
@@ -810,15 +853,15 @@
 
 
 def write_kernel(n, *refs):
-    small = refs[n]
-    for source, target in zip(refs[:n], refs[n + 1 :]):
+    small, norm_sum = refs[n : n + 2]
+    for source, target in zip(refs[:n], refs[n + 2 :]):
         target[...] = source[...].astype(target.dtype)
-    norm, step, conv_v, conv_b, dt, log, skip, gain = refs[2 * n + 1 :]
+    norm, step, conv_v, conv_b, dt, log, skip, gain = refs[2 * n + 2 :]
     inner, heads, taps = conv_v.shape[1], dt.shape[1], conv_v.shape[0]
 
     @pl.when(pl.program_id(0) == 0)
     def _():
-        norm[...] = small[8:9, :]
+        norm[...] = norm_sum[...]
         step[...] = small[0:heads, :]
         conv_v[...] = small[9 : 9 + taps, :inner]
         conv_b[...] = small[9 : 9 + taps, inner : inner + conv_b.shape[1]]
@@ -843,7 +886,6 @@
     part, slab = width // nh, BLOCK // nh
     n_taps = conv_value.shape[0] - 1
     vmem, hbm = pltpu.VMEM, pl.ANY
-    inbox = ns - 1 if ns <= DIRECT else 1
     inputs = dict(
         x=x, cot=cot, docs=doc_ids, gain=norm_gain[None], wg=w_gate, wv=w_value, wbc=w_bc,
         ws=w_step.T, wo=w_out, cv=conv_value, cb=conv_bc, dtb=dt_bias[None], alog=a_log[None],
@@ -856,7 +898,8 @@
         wv_sum=(w_value.shape, BF16),
         wo_sum=(w_out.shape, BF16),
         bc_sum=(w_bc.shape, BF16),
-        small=((16, width), F32),
+        wp_sum=((16, width), F32),
+        norm_sum=((1, width), F32),
     )
     scratch = dict(
         cot_all=vmem((nh, tokens, part), BF16),
@@ -889,10 +932,12 @@
         sel_step=vmem((128, inner), BF16),
         sel_end=vmem((128, inner), BF16),
         sel_into=vmem((128, inner), BF16),
-        back_out=vmem((state, inner), BF16),
-        back_in=vmem((inbox, state, inner), BF16),
+        back_out=vmem((heads // 2, state, 2 * head_dim), BF16),
+        norm_in=vmem((nh + ns - 1, 1, width), F32),
+        norm_out=vmem((2, 1, width), F32),
+        norm_all=vmem((ns, 1, width), F32),
+        back_in=vmem((heads // 2, state, 2 * head_dim), BF16),
         carry=vmem((1, inner), F32),
-        carry_in=vmem((inbox, 1, inner), F32),
         prod=vmem((1, inner), F32),
         sum_out=vmem((blocks, 8, BLOCK), F32),
         sum_in=vmem((blocks * (nh - 1), 8, BLOCK), F32),
@@ -911,24 +956,22 @@
         pack=vmem((16, width), F32),
         pack_out=vmem((8, width), F32),
         pack1_in=vmem((nh - 1, 8, width), F32),
-        pack2_in=vmem((16, width), F32),
-        pack3_in=vmem((ns - 1, 16, width), F32),
         load=pltpu.SemaphoreType.DMA((1,)),
     )
     for name, (rows, cols), kind in (
         (WO, (inner, width // 2), BF16), (WG, (width // 2, inner), BF16), (WV, (width // 2, inner), BF16),
-        (WQ, (width // nh, state), F32),
+        (WQ, (width // nh, state), F32), (WP, (8, width), F32),
     ):
         if name != WV:
             scratch[name + "_pair"] = vmem((rows, cols), F32)
             scratch[name + "_mine"] = vmem((rows, cols), kind)
-        scratch[name + "_in"] = vmem((ns - 1, rows // ns, cols), kind)
+        scratch[name + "_in"] = vmem((PIECES[name], rows // PIECES[name], cols), kind)
     counts = dict(
-        cot=4, halo=2, ends=heads // 2, carry=ns - 1, back=ns - 1, sum=blocks * (nh - 1), out=blocks * 6,
-        part=blocks * 6, grad=blocks * 4, edge=1, bc=nh - 1, bcg=nh - 1, pack1=nh - 1, pack2=1, pack3=ns - 1,
+        cot=4, halo=2, ends=heads // 2, back=heads // 2, norm=nh + ns - 1, sum=blocks * (nh - 1), out=blocks * 6,
+        part=blocks * 6, grad=blocks * 4, edge=1, bc=nh - 1, bcg=nh - 1, pack1=nh - 1,
     )
-    for name in (WO, WG, WV, WQ):
-        counts |= {name + "a": 1, name + "b": ns - 1, name + "c": ns - 1, name + "d": ns}
+    for name, n in PIECES.items():
+        counts |= {name + "a": 1, name + "b": n, name + "c": n, name + "d": n, name + "f": n}
     for name, n in counts.items():
         scratch[name + "_s"] = pltpu.SemaphoreType.DMA((n,))
         scratch[name + "_r"] = pltpu.SemaphoreType.DMA((n,))
@@ -946,7 +989,7 @@
         r.bc_in = [r.dz.at[pl.ds(o * quarter, quarter), pl.ds(0, bc_width)] for o in range(nh - 1)]
         kernel(r)
 
-    block_out, grad_in, g_gate, g_value, g_out, g_bc, small = pl.pallas_call(
+    block_out, grad_in, g_gate, g_value, g_out, g_bc, small, norm = pl.pallas_call(
         run,
         out_shape=[jax.ShapeDtypeStruct(*o) for o in outputs.values()],
         in_specs=[pl.BlockSpec(memory_space=hbm if name == "cot" else vmem) for name in inputs],
@@ -972,13 +1015,13 @@
     outs = pl.pallas_call(
         functools.partial(write_kernel, len(grads)),
         grid=(steps,),
-        in_specs=[*map(split_rows, grads), whole(small.shape)],
+        in_specs=[*map(split_rows, grads), whole(small.shape), whole(norm.shape)],
         out_specs=[*map(split_rows, grads), *map(whole, tiny)],
         out_shape=[jax.ShapeDtypeStruct(a.shape, k) for a, k in zip(grads, kinds)]
         + [jax.ShapeDtypeStruct(dims, F32) for dims in tiny],
         compiler_params=pltpu.CompilerParams(vmem_limit_bytes=VMEM_LIMIT),
         name="write",
-    )(*grads, small)
+    )(*grads, small, norm)
     block_out, grad_in, g_gate, g_value, g_out, g_bc, g_norm, g_step, g_cv, g_cb, g_dt, g_log, g_skip, g_gain = outs
     return (
         block_out[None], grad_in[None], g_norm[0], g_gate, g_value, g_bc, g_step.T, g_cv, g_cb, g_dt[0], g_log[0],

time: 219 us -> 193 us (0.88)
  Pallas kernels: 218 us -> 192 us
    pallas_call x1, Pallas kernels: 209 us -> 183 us  [on_device(): pl.pallas_call(run, out_shape=[jax.ShapeDtypeStruct(*o) for o in outputs....]
where the time goes in v3:
time: 193 us
  Pallas kernels  192 us (99%)
    pallas_call x1, Pallas kernels, on_device(): pl.pallas_call(run, out_shape=[jax.ShapeDtypeStruct(*o) for o in outputs....  183 us
    pallas_call x1, Pallas kernels, on_device(): pl.pallas_call(functools.partial(write_kernel, len(grads)), grid=(steps,)...  9.17 us

profile of v3, /device:TPU:0, one launch (start us, length us, event | category | flops | bytes accessed | tf_op | source)
XLA Modules:
  0.0 192.6 jit_solution(4530612859208864507)
XLA Ops:
  0.7 182.7 %block.1 = (bf16[1536,256]{1,0:T(8,128)(2,1)}, bf16[1536,1024]{1,0:T(8,128)(2,1)}, bf16[1024,512]{1,0:T(8,128)(2,1)}, bf16[1024,512]{1,0:T(8,128)(2,1)}, bf16[51...) custom-call(bf16[1536,1024]{1,0:T(8,128)(2,1)} %bitcast.16, ...), custom_call_target="tpu_custom_call" | custom-call | tf_op jit(solution)/shard_map/block/pallas_call | solution.py:992
  183.3 9.2 %write.1 = (bf16[1536,256]{1,0:T(8,128)(2,1)}, bf16[1536,1024]{1,0:T(8,128)(2,1)}, f32[1024,512]{1,0:T(8,128)}, f32[1024,512]{1,0:T(8,128)}, f32[512,1024]{1,0:T...) custom-call(bf16[1536,256]{1,0:T(8,128)(2,1)} %get-tuple-element.36., ...), custom_call_target="tpu_custom_call" | custom-call | tf_op jit(solution)/shard_map/write/pallas_call | solution.py:1015

commit v4 on v3

--- a/solution.py
+++ b/solution.py
@@ -26,7 +26,8 @@
     "cot", "halo", "ends", "norm", "back", "sum", "out", "part", "grad", "edge", "bc", "bcg", "pack1"
 )
 WO, WG, WV, WQ, WP = "wo", "wg", "wv", "wq", "wp"
-PIECES = {WO: 4, WG: 4, WV: 4, WQ: 1, WP: 1}
+PIECES = {WO: 4, WG: 4, WV: 8, WQ: 1, WP: 1}
+LOADED = ("x_hbm", "cot", "wg_hbm", "wv_hbm", "wbc_hbm", "wo_hbm")
 VMEM_LIMIT = 63 * 1024 * 1024
 
 
@@ -49,9 +50,15 @@
     return dot(m, hi, dims) + dot(m, lo, dims)
 
 
+def both(v, axis=1):
+    return jnp.concatenate(halves(v), axis=axis)
+
+
 def dot3(a, b, dims=NN):
     (ah, al), (bh, bl) = halves(a), halves(b)
-    return dot(ah, bh, dims) + (dot(al, bh, dims) + dot(ah, bl, dims))
+    return dot(
+        jnp.concatenate([ah, al, ah], axis=1), jnp.concatenate([bh, bh, bl], axis=dims[0][1][0]), dims
+    )
 
 
 def score_pair(c, b, first):
@@ -171,8 +178,16 @@
             sent(name, base + 2 * o - 1, HEAD_AXIS, o, block(square[3], o - 1))
             sent(name, base + 3 + o, HEAD_AXIS, 3 - o, block(square[3 - o], o - 1))
 
-    own = pltpu.make_async_copy(r.cot, r.cot_all.at[head], r.load.at[0])
-    own.start()
+    def cot_of(h):
+        return r.cot_all.at[:, pl.ds(pl.multiple_of(h * part, part), part)]
+
+    def cot_half(h, i):
+        return r.cot_all.at[pl.ds(i * (tokens // 2), tokens // 2), pl.ds(pl.multiple_of(h * part, part), part)]
+
+    moves = ((r.x_hbm, r.x), (r.wv_hbm, r.wv), (r.wbc_hbm, r.wbc), (r.cot, cot_of(head)), (r.wg_hbm, r.wg), (r.wo_hbm, r.wo))
+    loads = [pltpu.make_async_copy(*move, r.load.at[i]) for i, move in enumerate(moves)]
+    for load in loads:
+        load.start()
     row, col = iota((BLOCK, BLOCK), 0), iota((BLOCK, BLOCK), 1)
     r.upper[...] = (row <= col).astype(BF16)
     r.eye[...] = (row == col).astype(BF16)
@@ -180,7 +195,7 @@
     r.spread[...] = (iota((heads, inner), 1) // dim == iota((heads, inner), 0)).astype(BF16)
     r.collect[...] = (iota((inner, heads), 0) // dim == iota((inner, heads), 1)).astype(BF16)
     for sel, lane in ((r.sel_step, STEP), (r.sel_end, TO_END), (r.sel_into, INTO)):
-        sel[...] = (iota((128, inner), 1) // dim + lane == iota((128, inner), 0)).astype(BF16)
+        sel[...] = (iota((256, inner), 1) // dim + lane == lax.rem(iota((256, inner), 0), 128)).astype(BF16)
     r.tok[...] = jnp.zeros_like(r.tok)
     r.doc_out[...] = jnp.broadcast_to(r.docs[0:1, tokens - 1 : tokens].astype(F32), r.doc_out.shape)
     barrier = pltpu.get_barrier_semaphore()
@@ -188,14 +203,8 @@
         for o in range(1, count[axis]):
             pl.semaphore_signal(barrier, inc=1, device_id={axis: other(axis, o)}, device_id_type=MESH)
     pl.semaphore_wait(barrier, nh + ns + 2 - 3)
-    own.wait()
-
-    def cot_of(h):
-        return r.cot_all.at[h]
-
-    def cot_half(h, i):
-        return r.cot_all.at[h, pl.ds(i * (tokens // 2), tokens // 2)]
-
+    for load in loads[:4]:
+        load.wait()
     gather_1(COT, 0, cot_of)
     x_tail = r.x.at[pl.ds(tokens - TAIL, TAIL)]
     link(HALO, 0, SEQ_AXIS, 1, x_tail, r.halo_x).start()
@@ -203,6 +212,8 @@
 
     taps = jnp.concatenate([r.cv[...], r.cb[...]], axis=1)
     rate = -jnp.exp(r.alog[...])
+    same = iota((heads, heads), 0) == iota((heads, heads), 1)
+    rate_col = jnp.sum(jnp.where(same, rate, 0.0), axis=1, keepdims=True)
     skip = dot_left(r.dskip[...], r.spread[...])
     gain, out_gain = r.gain[...], r.og[...]
 
@@ -215,11 +226,8 @@
     def doc_row(c):
         return r.docs[0:1, at(c)].astype(F32)
 
-    def expand(v):
-        return dot_left(v, r.spread[...])
-
-    def expand_tok(rows, sel, cols=slice(None)):
-        return dot_left(r.tok[rows, :], sel[:, cols])
+    def expand_tok(marks, sel, cols=slice(None)):
+        return dot(marks, sel[:, cols])
 
     def project(c):
         rows = at(c)
@@ -254,20 +262,17 @@
         before = jnp.concatenate([prev, docs[:, : BLOCK - 1]], axis=1)
         ends = docs[:, BLOCK - 1 :]
         marks = [docs, (docs == prev).astype(F32), (docs == before).astype(F32), (docs == ends).astype(F32)]
-        marks = jnp.concatenate(marks + [jnp.zeros((4, BLOCK), F32)], axis=0).astype(BF16)
-        aux = dot(r.eye[...], marks, NT)
-        r.tok[rows, AUX : AUX + 8] = aux
-        step = softplus(r.tok[rows, 0:heads])
-        la = rate * step
-        la_hi, la_lo = halves(la)
-        cum = dot(r.upper[...], la_hi, TN) + dot(r.upper[...], la_lo, TN)
-        r.cumt[:, at(c)] = dot(la_hi, r.upper[...], TN) + dot(la_lo, r.upper[...], TN)
-        total = cum[BLOCK - 1 :, :]
-        r.tok[rows, CUM : CUM + heads] = cum
-        r.tok[rows, STEP : STEP + heads] = step
-        r.tok[rows, TO_END : TO_END + heads] = jnp.exp(total - cum) * aux[:, 3:4]
-        r.tok[rows, INTO : INTO + heads] = jnp.exp(cum) * aux[:, 1:2]
-        kept = expand(jnp.exp(total) * (ends == prev).astype(F32))
+        vt = r.tok[rows, :].T[0:heads]
+        step = softplus(vt)
+        la_hi, la_lo = halves(rate_col * step)
+        cum = dot(la_hi, r.upper[...]) + dot(la_lo, r.upper[...])
+        r.cumt[:, at(c)] = cum
+        total = cum[:, BLOCK - 1 :]
+        columns = [vt, cum, *marks, jnp.zeros((12, BLOCK), F32), step, jnp.exp(total - cum) * marks[3]]
+        columns += [jnp.exp(cum) * marks[1], jnp.zeros((72, BLOCK), F32)]
+        r.tok[rows, :] = jnp.concatenate(columns, axis=0).T
+        held = jnp.exp(total) * (ends == prev).astype(F32)
+        kept = jnp.sum(r.spread[...].astype(F32) * held, axis=0, keepdims=True)
         r.kept[c] = kept
         r.carry[...] = r.carry[...] * kept
         r.doc_prev[...] = jnp.broadcast_to(ends, r.doc_prev.shape)
@@ -304,14 +309,15 @@
             around = pl.ds(pl.multiple_of(c * BLOCK, BLOCK), BLOCK + EDGE)
             pre = conv_pre(r.cin[around, cols], taps[:, cols])
             xh = pre * sigmoid(pre)
-            xs = xh * expand_tok(rows, r.sel_step, cols)
+            marks = both(r.tok[rows, :])
+            xs = xh * expand_tok(marks, r.sel_step, cols)
             r.xs[rows, cols] = xs.astype(BF16)
             r.y[rows, cols] = skip[:, cols] * xh
-            inc = dot(r.b[rows, :], (xs * expand_tok(rows, r.sel_end, cols)).astype(BF16), TN)
+            inc = dot(r.b[rows, :], (xs * expand_tok(marks, r.sel_end, cols)).astype(BF16), TN)
             r.inc[c, :, cols] = inc
             r.own[pair] = r.kept[c, :, cols] * r.own[pair] + inc
 
-        repeat(blocks, own_states)
+        repeat(blocks // 2, lambda i, body=own_states: (body(2 * i), body(2 * i + 1)))
         relay(pair)
 
     gather_2(COT, 0, cot_of, cot_half)
@@ -353,7 +359,9 @@
         r.z[rows, :] = dot(r.normed[rows, :], r.wg[...])
         relay(pairs + c)
 
+    loads[4].wait()
     repeat(blocks, intra)
+    loads[5].wait()
 
     if 2 * (ns - 1) > blocks:
         repeat(2 * (ns - 1) - blocks, lambda i: relay(pairs + blocks + i))
@@ -362,26 +370,24 @@
     gather_3(COT, 0, cot_of, cot_half)
 
     def dgn_of(rows):
-        total = dot(r.cot_all[0, rows, :], r.wo[:, :part], NT)
-        for k in range(1, nh):
-            total = total + dot(r.cot_all[k, rows, :], r.wo[:, k * part : (k + 1) * part], NT)
-        return total
-
-    ones = jnp.ones((8, inner), BF16)
+        return dot(r.cot_all[rows, :], r.wo[...], NT)
+
+    lane8 = iota((BLOCK, 8), 1)
 
     def sums(c):
         rows = at(c)
         si = r.end[...]
         r.end[...] = r.kept[c] * si + r.inc[c]
         r.inc[c] = si
-        into = expand_tok(rows, r.sel_into)
+        into = expand_tok(both(r.tok[rows, :]), r.sel_into)
         y = r.y[rows, :] + into * dot3(r.c[rows, :], si)
         r.y[rows, :] = y
         z = r.z[rows, :]
         g = y * (z * sigmoid(z))
-        squares = dot_right(ones, g * g, NT)
-        products = dot_right(ones, dgn_of(rows) * out_gain * g, NT)
-        r.sum_out[c] = jnp.concatenate([squares[0:1], products[0:1], jnp.zeros((6, BLOCK), F32)], axis=0)
+        squares = jnp.sum(g * g, axis=1, keepdims=True)
+        products = jnp.sum(dgn_of(rows) * out_gain * g, axis=1, keepdims=True)
+        cols_hi, cols_lo = halves(jnp.where(lane8 == 0, squares, jnp.where(lane8 == 1, products, 0.0)))
+        r.sum_out[c] = dot(cols_hi, r.eye[...], TN) + dot(cols_lo, r.eye[...], TN)
         for o in range(1, nh):
             index = c * (nh - 1) + o - 1
             link(SUM, index, HEAD_AXIS, o, r.sum_out.at[c], r.sum_in.at[index]).start()
@@ -402,30 +408,28 @@
 
     def gate(c):
         rows = at(c)
-        scatter_2(OUT, 6 * c, out_block(c), r.out_in)
         total = r.sum_out[c]
         for o in range(1, nh):
             index = c * (nh - 1) + o - 1
             came(SUM, index, HEAD_AXIS, -o, r.sum_in.at[index])
             total = total + r.sum_in[index]
-        both = dot_right(r.eye[...], total, NT)
+        shares = dot_right(r.eye[...], total, NT)
         y, z = r.y[rows, :], r.z[rows, :]
         dgn = dgn_of(rows)
         sig = sigmoid(z)
         act = z * sig
         g = y * act
-        rms = lax.rsqrt(both[:, 0:1] / inner_all + EPS)
+        rms = lax.rsqrt(shares[:, 0:1] / inner_all + EPS)
         r.tok[rows, RMS : RMS + 1] = rms
         gr = g * rms
         r.xs[rows, :] = (gr * out_gain).astype(BF16)
         r.g_gain[...] += jnp.sum(dgn * gr, axis=0, keepdims=True)
-        dg = rms * (dgn * out_gain) - g * (rms * rms * rms * both[:, 1:2] / inner_all)
+        dg = rms * (dgn * out_gain) - g * (rms * rms * rms * shares[:, 1:2] / inner_all)
         dy = dg * act
         dyb = dy.astype(BF16)
         r.dy[rows, :] = dyb
-        r.tok[rows, DYY : DYY + heads] = dot_left(dyb.astype(F32) * y, r.collect[...])
         r.dz[rows, :] = (dg * y * (sig * (1.0 + z * (1.0 - sig)))).astype(BF16)
-        into = expand_tok(rows, r.sel_into)
+        into = expand_tok(both(r.tok[rows, :]), r.sel_into)
         r.end[...] += r.prod[...] * dot(r.c[rows, :].astype(BF16), (dy * into).astype(BF16), TN)
         r.prod[...] = r.prod[...] * r.kept[c]
 
@@ -444,21 +448,31 @@
     r.gw_out[...] = jnp.zeros_like(r.gw_out)
     r.gw_gate[...] = jnp.zeros_like(r.gw_gate)
 
-    def weight_grads(c):
-        rows = at(c)
-        gn = r.xs[rows, :]
-        for k in range(nh):
-            r.gw_out[:, k * part : (k + 1) * part] += dot(gn, r.cot_all[k, rows, :], TN)
+    def weight_grads(i):
+        rows = pl.ds(pl.multiple_of(i * 2 * BLOCK, 2 * BLOCK), 2 * BLOCK)
+        r.gw_out[...] += dot(r.xs[rows, :], r.cot_all[rows, :], TN)
+        scatter_2(OUT, 12 * i, out_block(2 * i), r.out_in)
+        relay_back(2 * i)
         r.gw_gate[...] += dot(r.normed[rows, :], r.dz[rows, :], TN)
-        relay_back(c)
-
-    repeat(blocks, weight_grads)
+        r.tok[rows, DYY : DYY + heads] = dot_left(r.dy[rows, :].astype(F32) * r.y[rows, :], r.collect[...])
+        scatter_2(OUT, 12 * i + 6, out_block(2 * i + 1), r.out_in)
+        relay_back(2 * i + 1)
+
+    repeat(blocks // 2, weight_grads)
+
+    def add_residual(c):
+        cols = pl.ds(pl.multiple_of(head * part, part), part)
+        half = BLOCK // 2
+        for i, total in enumerate(scatter_3(OUT, 6 * c, out_block(c), r.out_in)):
+            rows = pl.ds(pl.multiple_of(c * BLOCK + i * half, half), half)
+            scaled = r.tok[rows, RMS : RMS + 1] * total
+            r.block_out[rows, :] = (scaled + r.x[rows, cols].astype(F32)).astype(BF16)
 
     def ref(name, kind):
         return getattr(r, name + kind)
 
     def half_of(name, source, core):
-        if name in (WO, WQ):
+        if name == WO:
             half = source.shape[1] // 2
             return source.at[:, pl.ds(pl.multiple_of(core * half, half), half)]
         half = source.shape[0] // 2
@@ -473,7 +487,8 @@
         return half.at[pl.ds(j * rows, rows)]
 
     def result(name, core, j):
-        return piece_of(name, half_of(name, ref(name, "_sum"), core), j)
+        whole = ref(name, "_sum")
+        return piece_of(name, whole if name == WQ else half_of(name, whole, core), j)
 
     def total_a(name, source):
         return link(name + "a", 0, DP_AXIS, 1, half_of(name, source, 1 - dp), ref(name, "_pair"))
@@ -484,15 +499,20 @@
         mine = ref(name, "_mine")
         mine[...] = (half_of(name, source, dp)[...] + ref(name, "_pair")[...]).astype(mine.dtype)
 
+        start_inward(name)
+
+    def start_inward(name):
+        mine = ref(name, "_mine")
+
         @pl.when(depth == 0)
         def _():
             for j in range(PIECES[name]):
                 link(name + "b", j, SEQ_AXIS, inward, piece_of(name, mine, j), ref(name, "_in").at[j]).start()
 
-    def total_c(name):
+    def total_c(name, pieces=None):
         @pl.when(depth > 0)
         def _():
-            for j in range(PIECES[name]):
+            for j in pieces or range(PIECES[name]):
                 came(name + "b", j, SEQ_AXIS, -inward, ref(name, "_in").at[j])
                 mine = piece_of(name, ref(name, "_mine"), j)
                 mine[...] = (mine[...].astype(F32) + ref(name, "_in")[j].astype(F32)).astype(mine.dtype)
@@ -505,31 +525,32 @@
                 def _():
                     link(name + "c", j, SEQ_AXIS, inward, mine, result(name, dp, j)).start()
 
-    def total_d(name):
-        for j in range(PIECES[name]):
+    def total_d(name, middle, pieces=None):
+        for j in pieces or range(PIECES[name]):
             total = result(name, dp, j)
 
-            @pl.when(depth == last)
+            @pl.when(depth == last if middle else depth < last)
             def _():
-                came(name + "c", j, SEQ_AXIS, inward, total)
-                mine = piece_of(name, ref(name, "_mine"), j)
-                total[...] = (mine[...].astype(F32) + total[...].astype(F32)).astype(mine.dtype)
-
-            @pl.when(depth < last)
-            def _():
-                came(name + "f", j, SEQ_AXIS, inward, total)
-
-            @pl.when(depth > 0)
-            def _():
-                link(name + "f", j, SEQ_AXIS, -inward, total, total).start()
-
-            link(name + "d", j, DP_AXIS, 1, total, total).start()
+                if middle:
+                    came(name + "c", j, SEQ_AXIS, inward, total)
+                    mine = piece_of(name, ref(name, "_mine"), j)
+                    total[...] = (mine[...].astype(F32) + total[...].astype(F32)).astype(mine.dtype)
+                else:
+                    came(name + "f", j, SEQ_AXIS, inward, total)
+
+                @pl.when(depth > 0)
+                def _():
+                    link(name + "f", j, SEQ_AXIS, -inward, total, total).start()
+
+                if name != WQ:
+                    link(name + "d", j, DP_AXIS, 1, total, total).start()
 
     def total_e(name):
         for j in range(PIECES[name]):
             total, mine = result(name, dp, j), piece_of(name, ref(name, "_mine"), j)
-            came(name + "d", j, DP_AXIS, 1, result(name, 1 - dp, j))
-            sent(name + "d", j, DP_AXIS, 1, total)
+            if name != WQ:
+                came(name + "d", j, DP_AXIS, 1, result(name, 1 - dp, j))
+                sent(name + "d", j, DP_AXIS, 1, total)
 
             @pl.when(depth < last)
             def _():
@@ -546,6 +567,7 @@
     total_a(WO, r.gw_out).start()
     total_a(WG, r.gw_gate).start()
 
+    repeat(blocks // 2, add_residual)
     if 2 * (ns - 1) + pairs > blocks:
         repeat(2 * (ns - 1) + pairs - blocks, lambda i: relay_back(blocks + i))
     for pair in range(pairs):
@@ -568,6 +590,7 @@
         cum, cumt, aux = r.tok[rows, CUM : CUM + heads], r.cumt[:, at(c)], r.tok[rows, AUX : AUX + 8]
         mask = jnp.where((row <= col) & (aux[:, 0:1] == doc_row(c)), 0.0, NEG)
         scores = score_pair(c_full, b_mat, False)
+        marks = both(r.tok[rows, :])
         d_scores = jnp.zeros((BLOCK, BLOCK), F32)
         d_b = jnp.zeros((BLOCK, state), F32)
         d_c = jnp.zeros((BLOCK, state), F32)
@@ -589,7 +612,7 @@
             pre = conv_pre(window, taps[:, cols])
             sig = sigmoid(pre)
             xh = pre * sig
-            step_e, to_end_e, into_e = (expand_tok(rows, sel, cols) for sel in (r.sel_step, r.sel_end, r.sel_into))
+            step_e, to_end_e, into_e = (expand_tok(marks, sel, cols) for sel in (r.sel_step, r.sel_end, r.sel_into))
             xs = xh * step_e
             xsb = xs.astype(BF16)
             dyb = r.dy[rows, cols]
@@ -607,12 +630,12 @@
                 d_scores = d_scores + dot(xsb, two[i], NT) * decay
             d_xs_intra = dot(jnp.concatenate(mixed, axis=1), jnp.concatenate(two, axis=0))
             d_xs = d_xs_intra + d_xs_inter
-            collect = r.collect[cols, :]
-            d_step_own = d_step_own + dot_left(xh * d_xs, collect)
+            collect = jnp.concatenate([r.collect[cols, :]] * 2, axis=0)
+            d_step_own = d_step_own + dot(both(xh * d_xs), collect)
             lost = skip[:, cols] * (dy * xh) + (xsb.astype(F32) * d_xs_intra + xs * d_xs_inter)
-            d_cum = d_cum - dot_left(lost, collect)
+            d_cum = d_cum - dot(both(lost), collect)
             ended = jnp.sum(adj * r.inc[c + 1, :, cols], axis=0, keepdims=True)
-            through = through + dot_left(ended, collect)
+            through = through + dot(both(ended), collect)
             r.g_skip[:, cols] += jnp.sum(dy * xh, axis=0, keepdims=True)
             r.end[:, cols] = r.kept[c, :, cols] * adj + dot(c_mat, dye.astype(BF16), TN)
             conv_grad(skip[:, cols] * dy + step_e * d_xs, window, pre, sig, cols)
@@ -680,17 +703,8 @@
         r.g_norm[...] += jnp.sum(d_normed * xr, axis=0, keepdims=True)
         q = d_normed * gain
         d_x = norm * q - xr * (norm * norm * jnp.mean(q * x, axis=1, keepdims=True))
-        cot = jnp.concatenate([r.cot_all[k, rows, :] for k in range(nh)], axis=1)
-        r.normed[rows, :] = (d_x + cot.astype(F32)).astype(BF16)
+        r.normed[rows, :] = (d_x + r.cot_all[rows, :].astype(F32)).astype(BF16)
         gather_1(GRAD, 4 * c, slab_of(c))
-
-    def add_residual(c):
-        cols = pl.ds(pl.multiple_of(head * part, part), part)
-        half = BLOCK // 2
-        for i, total in enumerate(scatter_3(OUT, 6 * c, out_block(c), r.out_in)):
-            rows = pl.ds(pl.multiple_of(c * BLOCK + i * half, half), half)
-            scaled = r.tok[rows, RMS : RMS + 1] * total
-            r.block_out[rows, :] = (scaled + r.x[rows, cols].astype(F32)).astype(BF16)
 
     def reverse(t):
         c = blocks - 1 - t
@@ -702,9 +716,12 @@
             total_b(WG, r.gw_gate)
             r.gw_value[...] = jnp.zeros_like(r.gw_value)
 
+        @pl.when(t < blocks - blocks // 2)
+        def _():
+            add_residual(c)
+
         @pl.when(t >= 1)
         def _():
-            add_residual(c)
             project_back(c)
 
         @pl.when(t >= 2)
@@ -719,10 +736,14 @@
         def _():
             finish(c + LAG - 1)
 
+        @pl.when(t >= LAG + 2)
+        def _():
+            forward(c + LAG + 1)
+
         @pl.when(t == 4)
         def _():
             total_c(WG)
-            total_d(WO)
+            total_d(WO, True)
 
     repeat(blocks, reverse)
 
@@ -730,9 +751,7 @@
     last_rows = r.cin.at[pl.ds(EDGE + tokens, EDGE)]
     link(EDGES, 0, SEQ_AXIS, -1, first_rows, last_rows).start()
     order = [*range(blocks - 2, -1, -1), blocks - 1]
-    waiting = order[max(blocks - LAG, 0) :]
-    add_residual(blocks - 1)
-    combine(0)
+    unfinished, unsent = order[blocks - LAG :], order[max(blocks - LAG - 2, 0) :]
     came(EDGES, 0, SEQ_AXIS, 1, last_rows)
 
     @pl.when(seq == ns - 1)
@@ -742,70 +761,88 @@
     project_back(blocks - 1)
     total_a(WV, r.gw_value).start()
 
-    quarter = width // nh
-
-    def quarter_of(whole, h):
-        return whole.at[pl.ds(pl.multiple_of(h * quarter, quarter), quarter)]
-
+    half_rows = width // 2
+    quarter = half_rows // nh
+
+    def bc_rows(whole, core, h):
+        return whole.at[pl.ds(pl.multiple_of(core * half_rows + h * quarter, quarter), quarter)]
+
+    def half_bc(core):
+        return r.gw_bc.at[pl.ds(pl.multiple_of(core * half_rows, half_rows), half_rows)]
+
+    link(BC, nh - 1, DP_AXIS, 1, half_bc(1 - dp), r.bc_pair).start()
     r.pack[9 : 9 + n_taps + 1, :channels] = r.g_conv[: n_taps + 1, :]
     r.pack[14:15, :inner] = r.g_gain[...]
     r.pack[15:16, 0:heads] = r.g_dt[...]
     r.pack[15:16, 128 : 128 + heads] = r.g_log[...]
     r.pack[15:16, 256 : 256 + heads] = dot_left(r.g_skip[...], r.collect[...])
-    r.bc_out[...] = r.gw_bc[...].astype(BF16)
     r.pack_out[...] = r.pack[8:16, :]
     for o in range(1, nh):
         link(PACK1, o - 1, HEAD_AXIS, o, r.pack_out, r.pack1_in.at[o - 1]).start()
-        link(BC, o - 1, HEAD_AXIS, o, quarter_of(r.bc_out, square[o]), r.bc_in[o - 1]).start()
-    for c in waiting[:-2]:
-        finish(c)
+    total_d(WG, True)
     total_b(WV, r.gw_value)
-    total_d(WG)
+    came(BC, nh - 1, DP_AXIS, 1, r.bc_pair)
+    r.bc_out[...] = (half_bc(dp)[...] + r.bc_pair[...]).astype(BF16)
+    for o in range(1, nh):
+        link(BC, o - 1, HEAD_AXIS, o, bc_rows(r.bc_out, 0, square[o]), r.bc_in.at[o - 1]).start()
+    combine(0)
+    forward(unsent[0])
+    finish(unfinished[0])
+    total_c(WV, (0, 1))
     for o in range(1, nh):
         came(PACK1, o - 1, HEAD_AXIS, -o, r.pack1_in.at[o - 1])
         r.pack[9 : 9 + n_taps + 1, inner:channels] += r.pack1_in[o - 1, 1 : 2 + n_taps, inner:channels]
     total_a(WP, r.pack).start()
-    finish(0)
     combine(blocks - 1)
-    mine = quarter_of(r.gw_bc, head)[...]
+    total_c(WV, (2, 3))
+    total_d(WV, True, (0, 1))
+    for c in unfinished[1:-1]:
+        finish(c)
+    forward(unsent[1])
+    total_c(WV, (4, 5))
+    total_d(WV, True, (2, 3))
+    mine = bc_rows(r.bc_out, 0, head)[...].astype(F32)
     for o in range(1, nh):
-        came(BC, o - 1, HEAD_AXIS, -o, r.bc_in[o - 1])
-        mine = mine + r.bc_in[o - 1][...].astype(F32)
-    r.gw_q[...] = mine
-    total_a(WQ, r.gw_q).start()
-    total_c(WV)
+        came(BC, o - 1, HEAD_AXIS, -o, r.bc_in.at[o - 1])
+        mine = mine + r.bc_in[o - 1].astype(F32)
+    r.wq_mine[...] = mine.astype(BF16)
+    start_inward(WQ)
     total_b(WP, r.pack)
-    total_b(WQ, r.gw_q)
-    for c in order[:2]:
-        forward(c)
-    total_c(WP)
-    total_c(WQ)
+    total_c(WV, (6, 7))
+    total_d(WV, True, (4, 5))
+    total_d(WO, False)
+    total_d(WG, False)
     finish(blocks - 1)
     for o in range(1, nh):
         link(NORM, o - 1, HEAD_AXIS, o, r.g_norm, r.norm_in.at[o - 1]).start()
-    for c in order[2:-2]:
+    total_d(WV, True, (6, 7))
+    total_c(WP)
+    total_c(WQ)
+    for c in unsent[2:-1]:
         forward(c)
-    total_d(WV)
-    total_d(WP)
-    total_d(WQ)
+    total_d(WP, True)
+    total_d(WQ, True)
+    total_d(WV, False)
     total = r.g_norm[...]
     for o in range(1, nh):
         came(NORM, o - 1, HEAD_AXIS, -o, r.norm_in.at[o - 1])
         total = total + r.norm_in[o - 1]
     r.norm_out[0] = total
     link(NORM, nh - 1, DP_AXIS, 1, r.norm_out.at[0], r.norm_in.at[nh - 1]).start()
-    forward(0)
+    forward(blocks - 1)
+    total_d(WP, False)
+    total_d(WQ, False)
     total_e(WQ)
-    mine = quarter_of(r.bc_sum, head)
-    mine[...] = r.wq_sum[...].astype(BF16)
+    mine = bc_rows(r.bc_sum, dp, head)
+    mine[...] = r.wq_sum[...]
     for o in range(1, nh):
         link(BCG, o - 1, HEAD_AXIS, o, mine, mine).start()
+    link(BCG, nh - 1, DP_AXIS, 1, mine, mine).start()
     came(NORM, nh - 1, DP_AXIS, 1, r.norm_in.at[nh - 1])
     total = r.norm_out[0] + r.norm_in[nh - 1]
     r.norm_out[1] = total
     for o in range(1, ns):
         link(NORM, nh + o - 1, SEQ_AXIS, o, r.norm_out.at[1], r.norm_in.at[nh + o - 1]).start()
-    forward(blocks - 1)
     for name in (WO, WG, WV, WP):
         total_e(name)
 
@@ -818,11 +855,17 @@
         total = total + r.norm_all[k]
     r.norm_sum[...] = total
     for o in range(1, nh):
-        came(BCG, o - 1, HEAD_AXIS, -o, quarter_of(r.bc_sum, square[o]))
+        theirs = bc_rows(r.bc_sum, dp, square[o])
+        came(BCG, o - 1, HEAD_AXIS, -o, theirs)
+        link(BCG, nh - 1 + o, DP_AXIS, 1, theirs, theirs).start()
         sent(BCG, o - 1, HEAD_AXIS, o, mine)
-        sent(BC, o - 1, HEAD_AXIS, o, quarter_of(r.bc_out, square[o]))
+        sent(BC, o - 1, HEAD_AXIS, o, bc_rows(r.bc_out, 0, square[o]))
         sent(PACK1, o - 1, HEAD_AXIS, o, r.pack_out)
         sent(NORM, o - 1, HEAD_AXIS, o, r.g_norm)
+    for o in range(nh):
+        came(BCG, nh - 1 + o, DP_AXIS, 1, bc_rows(r.bc_sum, 1 - dp, square[o]))
+        sent(BCG, nh - 1 + o, DP_AXIS, 1, bc_rows(r.bc_sum, dp, square[o]))
+    sent(BC, nh - 1, DP_AXIS, 1, half_bc(1 - dp))
     sent(NORM, nh - 1, DP_AXIS, 1, r.norm_out.at[0])
     for o in range(1, ns):
         sent(NORM, nh + o - 1, SEQ_AXIS, o, r.norm_out.at[1])
@@ -845,11 +888,13 @@
             sent(SUM, c * (nh - 1) + o - 1, HEAD_AXIS, o, r.sum_out.at[c])
         scatter_sent(PART, 6 * c, part_block(c))
         gather_3(GRAD, 4 * c, slab_of(c), slab_half(c))
+        store(c).start()
+
+    def store(c):
+        return pltpu.make_async_copy(r.normed.at[at(c)], r.grad_in.at[at(c)], r.stored.at[c])
 
     repeat(blocks, drain)
-    done = pltpu.make_async_copy(r.normed, r.grad_in, r.load.at[0])
-    done.start()
-    done.wait()
+    repeat(blocks, lambda c: store(c).wait())
 
 
 def write_kernel(n, *refs):
@@ -887,8 +932,8 @@
     n_taps = conv_value.shape[0] - 1
     vmem, hbm = pltpu.VMEM, pl.ANY
     inputs = dict(
-        x=x, cot=cot, docs=doc_ids, gain=norm_gain[None], wg=w_gate, wv=w_value, wbc=w_bc,
-        ws=w_step.T, wo=w_out, cv=conv_value, cb=conv_bc, dtb=dt_bias[None], alog=a_log[None],
+        x_hbm=x, cot=cot, docs=doc_ids, gain=norm_gain[None], wg_hbm=w_gate, wv_hbm=w_value, wbc_hbm=w_bc,
+        ws=w_step.T, wo_hbm=w_out, cv=conv_value, cb=conv_bc, dtb=dt_bias[None], alog=a_log[None],
         dskip=d_skip[None], og=out_gain[None],
     )
     outputs = dict(
@@ -902,7 +947,13 @@
         norm_sum=((1, width), F32),
     )
     scratch = dict(
-        cot_all=vmem((nh, tokens, part), BF16),
+        x=vmem((tokens, width), BF16),
+        wg=vmem(w_gate.shape, BF16),
+        wv=vmem(w_value.shape, BF16),
+        wbc=vmem(w_bc.shape, BF16),
+        wo=vmem(w_out.shape, BF16),
+        bc_in=vmem((nh - 1, width // 2 // nh, bc_width), BF16),
+        cot_all=vmem((tokens, width), BF16),
         halo_x=vmem((TAIL, width), BF16),
         doc_out=vmem((8, 128), F32),
         doc_in=vmem((8, 128), F32),
@@ -929,9 +980,9 @@
         end_out=vmem((heads // 2, state, 2 * head_dim), F32),
         end_in=vmem((heads // 2, state, 2 * head_dim), F32),
         carry_part=vmem((heads // 2, 1, 2 * head_dim), F32),
-        sel_step=vmem((128, inner), BF16),
-        sel_end=vmem((128, inner), BF16),
-        sel_into=vmem((128, inner), BF16),
+        sel_step=vmem((256, inner), BF16),
+        sel_end=vmem((256, inner), BF16),
+        sel_into=vmem((256, inner), BF16),
         back_out=vmem((heads // 2, state, 2 * head_dim), BF16),
         norm_in=vmem((nh + ns - 1, 1, width), F32),
         norm_out=vmem((2, 1, width), F32),
@@ -945,7 +996,7 @@
         out_in=vmem((blocks * 6, BLOCK // 2, part), BF16),
         part_in=vmem((blocks * 6, slab // 2, width + bc_width), BF16),
         gw_out=vmem(w_out.shape, F32),
-        wq_sum=vmem((width // nh, bc_width), F32),
+        wq_sum=vmem((width // 2 // nh, bc_width), BF16),
         dz=vmem((tokens, inner), BF16),
         g_gain=vmem((1, inner), F32),
         g_dt=vmem((1, heads), F32),
@@ -956,19 +1007,21 @@
         pack=vmem((16, width), F32),
         pack_out=vmem((8, width), F32),
         pack1_in=vmem((nh - 1, 8, width), F32),
-        load=pltpu.SemaphoreType.DMA((1,)),
+        load=pltpu.SemaphoreType.DMA((6,)),
+        stored=pltpu.SemaphoreType.DMA((blocks,)),
     )
     for name, (rows, cols), kind in (
         (WO, (inner, width // 2), BF16), (WG, (width // 2, inner), BF16), (WV, (width // 2, inner), BF16),
-        (WQ, (width // nh, state), F32), (WP, (8, width), F32),
+        (WQ, (width // 2 // nh, bc_width), BF16), (WP, (8, width), F32),
     ):
+        if name not in (WV, WQ):
+            scratch[name + "_pair"] = vmem((rows, cols), F32)
         if name != WV:
-            scratch[name + "_pair"] = vmem((rows, cols), F32)
             scratch[name + "_mine"] = vmem((rows, cols), kind)
         scratch[name + "_in"] = vmem((PIECES[name], rows // PIECES[name], cols), kind)
     counts = dict(
         cot=4, halo=2, ends=heads // 2, back=heads // 2, norm=nh + ns - 1, sum=blocks * (nh - 1), out=blocks * 6,
-        part=blocks * 6, grad=blocks * 4, edge=1, bc=nh - 1, bcg=nh - 1, pack1=nh - 1,
+        part=blocks * 6, grad=blocks * 4, edge=1, bc=nh, bcg=2 * nh - 1, pack1=nh - 1,
     )
     for name, n in PIECES.items():
         counts |= {name + "a": 1, name + "b": n, name + "c": n, name + "d": n, name + "f": n}
@@ -979,20 +1032,18 @@
 
     def run(*refs):
         r = types.SimpleNamespace(**dict(zip(names, refs)))
-        quarter = width // nh
         r.gw_gate = r.gw_value = r.z.at[pl.ds(0, width)]
         r.wv_pair = r.z.at[pl.ds(width, width // 2)]
         r.gw_bc = r.y.at[pl.ds(0, width), pl.ds(0, bc_width)]
-        r.gw_q = r.y.at[pl.ds(width, quarter), pl.ds(0, bc_width)]
-        r.bc_out = r.xs.at[pl.ds(0, width), pl.ds(0, bc_width)]
+        r.bc_pair = r.y.at[pl.ds(width, width // 2), pl.ds(0, bc_width)]
+        r.bc_out = r.xs.at[pl.ds(0, width // 2), pl.ds(0, bc_width)]
         r.wv_mine = r.xs.at[pl.ds(width, width // 2)]
-        r.bc_in = [r.dz.at[pl.ds(o * quarter, quarter), pl.ds(0, bc_width)] for o in range(nh - 1)]
         kernel(r)
 
     block_out, grad_in, g_gate, g_value, g_out, g_bc, small, norm = pl.pallas_call(
         run,
         out_shape=[jax.ShapeDtypeStruct(*o) for o in outputs.values()],
-        in_specs=[pl.BlockSpec(memory_space=hbm if name == "cot" else vmem) for name in inputs],
+        in_specs=[pl.BlockSpec(memory_space=hbm if name in LOADED else vmem) for name in inputs],
         out_specs=[pl.BlockSpec(memory_space=hbm if name == "grad_in" else vmem) for name in outputs],
         scratch_shapes=list(scratch.values()),
         compiler_params=pltpu.CompilerParams(

time: 193 us -> 166 us (0.86)
  Pallas kernels: 192 us -> 164 us
    pallas_call x1, Pallas kernels: 183 us -> 155 us  [on_device(): pl.pallas_call(run, out_shape=[jax.ShapeDtypeStruct(*o) for o in outputs....]
where the time goes in v4:
time: 166 us; the launch traced here: 165 us
  Pallas kernels  164 us (99%)
    pallas_call x1, Pallas kernels, on_device(): pl.pallas_call(run, out_shape=[jax.ShapeDtypeStruct(*o) for o in outputs....  155 us
    pallas_call x1, Pallas kernels, on_device(): pl.pallas_call(functools.partial(write_kernel, len(grads)), grid=(steps,)...  9.17 us

profile of v4, /device:TPU:0, one launch (start us, length us, event | category | flops | bytes accessed | tf_op | source)
XLA Modules:
  0.0 165.2 jit_solution(6258726517766978298)
XLA Ops:
  0.7 155.2 %block.1 = (bf16[1536,256]{1,0:T(8,128)(2,1)}, bf16[1536,1024]{1,0:T(8,128)(2,1)}, bf16[1024,512]{1,0:T(8,128)(2,1)}, bf16[1024,512]{1,0:T(8,128)(2,1)}, bf16[51...) custom-call(bf16[1536,1024]{1,0:T(8,128)(2,1)} %bitcast.16, ...), custom_call_target="tpu_custom_call" | custom-call | tf_op jit(solution)/shard_map/block/pallas_call | solution.py:1043
  155.9 9.2 %write.1 = (bf16[1536,256]{1,0:T(8,128)(2,1)}, bf16[1536,1024]{1,0:T(8,128)(2,1)}, f32[1024,512]{1,0:T(8,128)}, f32[1024,512]{1,0:T(8,128)}, f32[512,1024]{1,0:T...) custom-call(bf16[1536,256]{1,0:T(8,128)(2,1)} %get-tuple-element.36., ...), custom_call_target="tpu_custom_call" | custom-call | tf_op jit(solution)/shard_map/write/pallas_call | solution.py:1066

commit v5 on v4

--- a/solution.py
+++ b/solution.py
@@ -20,7 +20,8 @@
 TN = (((0,), (0,)), ((), ()))
 MESH = pl.DeviceIdType.MESH
 CUM, AUX, DYY, STEP, TO_END, INTO, RMS = 8, 16, 24, 32, 40, 48, 56
-LAG = 4
+LAG = 3
+EARLY = 2
 HEAD_AXIS, SEQ_AXIS, DP_AXIS = "head", "seq", "dp"
 COT, HALO, ENDS, NORM, BACK, SUM, OUT, PART, GRAD, EDGES, BC, BCG, PACK1 = (
     "cot", "halo", "ends", "norm", "back", "sum", "out", "part", "grad", "edge", "bc", "bcg", "pack1"
@@ -202,32 +203,9 @@
     for axis in (HEAD_AXIS, SEQ_AXIS, DP_AXIS):
         for o in range(1, count[axis]):
             pl.semaphore_signal(barrier, inc=1, device_id={axis: other(axis, o)}, device_id_type=MESH)
-    pl.semaphore_wait(barrier, nh + ns + 2 - 3)
-    for load in loads[:4]:
+    for load in loads[:3]:
         load.wait()
-    gather_1(COT, 0, cot_of)
-    x_tail = r.x.at[pl.ds(tokens - TAIL, TAIL)]
-    link(HALO, 0, SEQ_AXIS, 1, x_tail, r.halo_x).start()
-    link(HALO, 1, SEQ_AXIS, 1, r.doc_out, r.doc_in).start()
-
-    taps = jnp.concatenate([r.cv[...], r.cb[...]], axis=1)
-    rate = -jnp.exp(r.alog[...])
-    same = iota((heads, heads), 0) == iota((heads, heads), 1)
-    rate_col = jnp.sum(jnp.where(same, rate, 0.0), axis=1, keepdims=True)
-    skip = dot_left(r.dskip[...], r.spread[...])
     gain, out_gain = r.gain[...], r.og[...]
-
-    def conv_pre(window, taps):
-        pre = taps[n_taps : n_taps + 1, :] + taps[0:1, :] * window[EDGE:]
-        for k in range(1, n_taps):
-            pre = pre + taps[k : k + 1, :] * window[EDGE - k : EDGE - k + BLOCK]
-        return pre
-
-    def doc_row(c):
-        return r.docs[0:1, at(c)].astype(F32)
-
-    def expand_tok(marks, sel, cols=slice(None)):
-        return dot(marks, sel[:, cols])
 
     def project(c):
         rows = at(c)
@@ -238,7 +216,31 @@
         r.cin[inside, inner:] = dot(normed, r.wbc[...])
         r.tok[rows, 0:heads] = dot(normed, r.ws[...], NT) + r.dtb[...]
 
-    repeat(blocks, project)
+    repeat(EARLY, project)
+    pl.semaphore_wait(barrier, nh + ns + 2 - 3)
+    loads[3].wait()
+    gather_1(COT, 0, cot_of)
+    x_tail = r.x.at[pl.ds(tokens - TAIL, TAIL)]
+    link(HALO, 0, SEQ_AXIS, 1, x_tail, r.halo_x).start()
+    link(HALO, 1, SEQ_AXIS, 1, r.doc_out, r.doc_in).start()
+    repeat(blocks - EARLY, lambda i: project(EARLY + i))
+
+    taps = jnp.concatenate([r.cv[...], r.cb[...]], axis=1)
+    rate = -jnp.exp(r.alog[...])
+    same = iota((heads, heads), 0) == iota((heads, heads), 1)
+    rate_col = jnp.sum(jnp.where(same, rate, 0.0), axis=1, keepdims=True)
+    skip = dot_left(r.dskip[...], r.spread[...])
+    def conv_pre(window, taps):
+        pre = taps[n_taps : n_taps + 1, :] + taps[0:1, :] * window[EDGE:]
+        for k in range(1, n_taps):
+            pre = pre + taps[k : k + 1, :] * window[EDGE - k : EDGE - k + BLOCK]
+        return pre
+
+    def doc_row(c):
+        return r.docs[0:1, at(c)].astype(F32)
+
+    def expand_tok(marks, sel, cols=slice(None)):
+        return dot(marks, sel[:, cols])
 
     came(HALO, 0, SEQ_AXIS, -1, r.halo_x)
     came(HALO, 1, SEQ_AXIS, -1, r.doc_in)
@@ -324,18 +326,19 @@
 
     def relay_back(turn):
         distance = ns - 1 - seq
-        pair = turn - 2 * distance
-
-        @pl.when(jnp.logical_and(distance > 0, jnp.logical_and(pair >= 0, pair < pairs)))
-        def _():
-            came(BACK, pair, SEQ_AXIS, 1, r.back_in.at[pair])
-            into = r.back_in[pair].astype(F32)
-            r.back_out[pair] = (r.carry_part[pair] * into + r.own[pair]).astype(BF16)
-            r.own[pair] = into
-
-            @pl.when(seq > 0)
-            def _():
-                link(BACK, pair, SEQ_AXIS, -1, r.back_out.at[pair], r.back_in.at[pair]).start()
+        for i in range(2):
+            pair = 2 * (turn - 2 * distance) + i
+
+            @pl.when(jnp.logical_and(distance > 0, jnp.logical_and(pair >= 0, pair < pairs)))
+            def _(pair=pair):
+                came(BACK, pair, SEQ_AXIS, 1, r.back_in.at[pair])
+                into = r.back_in[pair].astype(F32)
+                r.back_out[pair] = (r.carry_part[pair] * into + r.own[pair]).astype(BF16)
+                r.own[pair] = into
+
+                @pl.when(seq > 0)
+                def _():
+                    link(BACK, pair, SEQ_AXIS, -1, r.back_out.at[pair], r.back_in.at[pair]).start()
 
     first = iota((BLOCK, lanes), 1) < lanes // 2
 
@@ -391,14 +394,13 @@
         for o in range(1, nh):
             index = c * (nh - 1) + o - 1
             link(SUM, index, HEAD_AXIS, o, r.sum_out.at[c], r.sum_in.at[index]).start()
-        r.parts[c, :, :width] = dot((g * out_gain).astype(BF16), r.wo[...]).astype(BF16)
-        scatter_1(OUT, 6 * c, out_block(c), r.out_in)
+        r.parts[c] = dot((g * out_gain).astype(BF16), r.wo[...]).astype(BF16)
 
     def out_block(c):
         half = BLOCK // 2
         return lambda h, i: r.parts.at[c, pl.ds(i * half, half), pl.ds(pl.multiple_of(h * part, part), part)]
 
-    repeat(blocks, sums)
+    repeat(blocks // 2, lambda i: (sums(2 * i), sums(2 * i + 1)))
     r.inc[blocks] = r.end[...]
 
     r.end[...] = jnp.zeros_like(r.end)
@@ -413,6 +415,7 @@
             index = c * (nh - 1) + o - 1
             came(SUM, index, HEAD_AXIS, -o, r.sum_in.at[index])
             total = total + r.sum_in[index]
+        scatter_1(OUT, 6 * c, out_block(c), r.out_in)
         shares = dot_right(r.eye[...], total, NT)
         y, z = r.y[rows, :], r.z[rows, :]
         dgn = dgn_of(rows)
@@ -430,10 +433,12 @@
         r.dy[rows, :] = dyb
         r.dz[rows, :] = (dg * y * (sig * (1.0 + z * (1.0 - sig)))).astype(BF16)
         into = expand_tok(both(r.tok[rows, :]), r.sel_into)
-        r.end[...] += r.prod[...] * dot(r.c[rows, :].astype(BF16), (dy * into).astype(BF16), TN)
+        part_state = dot(r.c[rows, :].astype(BF16), (dy * into).astype(BF16), TN)
+        r.adj[c] = part_state.astype(BF16)
+        r.end[...] += r.prod[...] * part_state
         r.prod[...] = r.prod[...] * r.kept[c]
 
-    repeat(blocks, gate)
+    repeat(blocks // 2, lambda i: (gate(2 * i), gate(2 * i + 1)))
 
     for pair in range(pairs):
         r.own[pair] = r.end[:, pair * lanes : (pair + 1) * lanes]
@@ -451,11 +456,9 @@
     def weight_grads(i):
         rows = pl.ds(pl.multiple_of(i * 2 * BLOCK, 2 * BLOCK), 2 * BLOCK)
         r.gw_out[...] += dot(r.xs[rows, :], r.cot_all[rows, :], TN)
-        scatter_2(OUT, 12 * i, out_block(2 * i), r.out_in)
         relay_back(2 * i)
         r.gw_gate[...] += dot(r.normed[rows, :], r.dz[rows, :], TN)
         r.tok[rows, DYY : DYY + heads] = dot_left(r.dy[rows, :].astype(F32) * r.y[rows, :], r.collect[...])
-        scatter_2(OUT, 12 * i + 6, out_block(2 * i + 1), r.out_in)
         relay_back(2 * i + 1)
 
     repeat(blocks // 2, weight_grads)
@@ -567,11 +570,20 @@
     total_a(WO, r.gw_out).start()
     total_a(WG, r.gw_gate).start()
 
-    repeat(blocks // 2, add_residual)
-    if 2 * (ns - 1) + pairs > blocks:
-        repeat(2 * (ns - 1) + pairs - blocks, lambda i: relay_back(blocks + i))
+    if 2 * (ns - 1) + pairs // 2 > blocks:
+        repeat(2 * (ns - 1) + pairs // 2 - blocks, lambda i: relay_back(blocks + i))
     for pair in range(pairs):
         r.end[:, pair * lanes : (pair + 1) * lanes] = r.own[pair]
+
+    def chain(i):
+        c = blocks - 1 - i
+        here = r.end[...]
+        r.end[...] = r.kept[c] * here + r.adj[c].astype(F32)
+        r.adj[c] = here.astype(BF16)
+
+    repeat(blocks, chain)
+    repeat(blocks, lambda c: scatter_2(OUT, 6 * c, out_block(c), r.out_in))
+    r.tail[...] = r.cin[0:EDGE, :]
     r.g_dt[...] = jnp.zeros_like(r.g_dt)
     r.g_log[...] = jnp.zeros_like(r.g_log)
     r.g_skip[...] = jnp.zeros_like(r.g_skip)
@@ -581,7 +593,6 @@
 
     def back(c):
         rows = at(c)
-        around = pl.ds(pl.multiple_of(c * BLOCK, BLOCK), BLOCK + EDGE)
         inside = pl.ds(pl.multiple_of(c * BLOCK + EDGE, EDGE), BLOCK)
         b_mat, c_full = r.b[rows, :], r.c[rows, :]
         c_mat = c_full.astype(BF16)
@@ -604,11 +615,15 @@
                 shifted = window[EDGE - k : EDGE - k + BLOCK]
                 r.g_conv[k : k + 1, cols] += jnp.sum(d_pre * shifted, axis=0, keepdims=True)
             r.g_conv[n_taps : n_taps + 1, cols] += jnp.sum(d_pre, axis=0, keepdims=True)
+            r.tail[:, cols] = window[BLOCK:]
             r.cin[inside, cols] = d_pre
+
+        def window_of(cols):
+            return jnp.concatenate([r.tail[:, cols], r.cin[inside, cols]], axis=0)
 
         for pair in range(heads // 2):
             cols = slice(pair * lanes, (pair + 1) * lanes)
-            window = r.cin[around, cols]
+            window = window_of(cols)
             pre = conv_pre(window, taps[:, cols])
             sig = sigmoid(pre)
             xh = pre * sig
@@ -617,11 +632,12 @@
             xsb = xs.astype(BF16)
             dyb = r.dy[rows, cols]
             dy = dyb.astype(F32)
-            adj = r.end[:, cols]
+            adjb = r.adj[c, :, cols]
+            adj = adjb.astype(F32)
             dye = dy * into_e
             d_c = d_c + dot3(dye, r.inc[c, :, cols], NT)
-            d_b = d_b + dot3(xs * to_end_e, adj, NT)
-            d_xs_inter = to_end_e * dot(b_mat, adj.astype(BF16))
+            d_b = d_b + dot(both(xs * to_end_e), jnp.concatenate([adjb, adjb], axis=1), NT)
+            d_xs_inter = to_end_e * dot(b_mat, adjb)
             two = split(dyb)
             mixed = []
             for i, h in enumerate((2 * pair, 2 * pair + 1)):
@@ -637,13 +653,12 @@
             ended = jnp.sum(adj * r.inc[c + 1, :, cols], axis=0, keepdims=True)
             through = through + dot(both(ended), collect)
             r.g_skip[:, cols] += jnp.sum(dy * xh, axis=0, keepdims=True)
-            r.end[:, cols] = r.kept[c, :, cols] * adj + dot(c_mat, dye.astype(BF16), TN)
             conv_grad(skip[:, cols] * dy + step_e * d_xs, window, pre, sig, cols)
         d_sb = d_scores.astype(BF16)
         d_b = d_b + dot(d_sb, c_mat)
         d_c = d_c + dot(d_sb, b_mat, TN)
         cols = slice(inner, channels)
-        window = r.cin[around, cols]
+        window = window_of(cols)
         pre = conv_pre(window, taps[:, cols])
         conv_grad(jnp.concatenate([d_b, d_c], axis=1), window, pre, sigmoid(pre), cols)
         d_la = (dot_right(r.upper[...], d_cum) + through) * aux[:, 2:3]
@@ -666,10 +681,10 @@
         r.gw_value[...] += grads[:, :inner]
         r.gw_bc[...] += grads[:, inner:]
         r.pack[0:heads, :] += dot(dstep, normed, TN)
-        d_part = dot(r.dz[rows, :], r.wg[...], NT) + dot(d_val, r.wv[...], NT) + dot(dstep, r.ws[...])
+        d_part = dot(r.dz[rows, :], r.wg[...], NT) + dot(d_val, r.wv[...], NT)
+        d_part = d_part + dot(d_inb[:, inner:], r.wbc[...], NT) + dot(dstep, r.ws[...])
         scatter_sent(OUT, 6 * c, out_block(c))
-        r.parts[c, :, :width] = d_part.astype(BF16)
-        r.parts[c, :, width:] = d_inb[:, inner:]
+        r.parts[c] = d_part.astype(BF16)
         scatter_1(PART, 6 * c, part_block(c), r.part_in)
 
     def part_block(c):
@@ -698,60 +713,56 @@
         x = r.x[rows, :].astype(F32)
         norm = lax.rsqrt(jnp.mean(x * x, axis=1, keepdims=True) + EPS)
         xr = x * norm
-        d_bc = total[:, width:].astype(BF16)
-        d_normed = total[:, :width] + dot(d_bc, r.wbc[...], NT)
+        d_normed = total
         r.g_norm[...] += jnp.sum(d_normed * xr, axis=0, keepdims=True)
         q = d_normed * gain
         d_x = norm * q - xr * (norm * norm * jnp.mean(q * x, axis=1, keepdims=True))
         r.normed[rows, :] = (d_x + r.cot_all[rows, :].astype(F32)).astype(BF16)
         gather_1(GRAD, 4 * c, slab_of(c))
 
-    def reverse(t):
-        c = blocks - 1 - t
+    first_rows = r.cin.at[pl.ds(EDGE, EDGE)]
+    last_rows = r.cin.at[pl.ds(EDGE + tokens, EDGE)]
+
+    def reverse(c):
         back(c)
 
-        @pl.when(t == 0)
+        @pl.when(c == 0)
         def _():
+            link(EDGES, 0, SEQ_AXIS, -1, first_rows, last_rows).start()
             total_b(WO, r.gw_out)
             total_b(WG, r.gw_gate)
             r.gw_value[...] = jnp.zeros_like(r.gw_value)
 
-        @pl.when(t < blocks - blocks // 2)
+        add_residual(c)
+
+        @pl.when(c >= 1)
         def _():
-            add_residual(c)
-
-        @pl.when(t >= 1)
+            project_back(c - 1)
+
+        @pl.when(c >= 2)
         def _():
-            project_back(c)
-
-        @pl.when(t >= 2)
-        def _():
-            combine(c + 1)
-
-        @pl.when(t == 2)
+            combine(c - 2)
+
+        @pl.when(c == 2)
         def _():
             total_c(WO)
 
-        @pl.when(t >= LAG)
+        @pl.when(c >= LAG)
         def _():
-            finish(c + LAG - 1)
-
-        @pl.when(t >= LAG + 2)
+            finish(c - LAG)
+
+        @pl.when(c >= LAG + 2)
         def _():
-            forward(c + LAG + 1)
-
-        @pl.when(t == 4)
+            forward(c - LAG - 2)
+
+        @pl.when(c == 4)
         def _():
             total_c(WG)
             total_d(WO, True)
 
     repeat(blocks, reverse)
 
-    first_rows = r.cin.at[pl.ds(EDGE, EDGE)]
-    last_rows = r.cin.at[pl.ds(EDGE + tokens, EDGE)]
-    link(EDGES, 0, SEQ_AXIS, -1, first_rows, last_rows).start()
-    order = [*range(blocks - 2, -1, -1), blocks - 1]
-    unfinished, unsent = order[blocks - LAG :], order[max(blocks - LAG - 2, 0) :]
+    unfinished, unsent = [*range(blocks - LAG, blocks)], [*range(max(blocks - LAG - 2, 0), blocks)]
     came(EDGES, 0, SEQ_AXIS, 1, last_rows)
 
     @pl.when(seq == ns - 1)
@@ -784,8 +795,8 @@
     came(BC, nh - 1, DP_AXIS, 1, r.bc_pair)
     r.bc_out[...] = (half_bc(dp)[...] + r.bc_pair[...]).astype(BF16)
     for o in range(1, nh):
-        link(BC, o - 1, HEAD_AXIS, o, bc_rows(r.bc_out, 0, square[o]), r.bc_in.at[o - 1]).start()
-    combine(0)
+        link(BC, o - 1, HEAD_AXIS, o, bc_rows(r.bc_out, 0, square[o]), r.bc_in[o - 1]).start()
+    combine(blocks - 2)
     forward(unsent[0])
     finish(unfinished[0])
     total_c(WV, (0, 1))
@@ -803,8 +814,8 @@
     total_d(WV, True, (2, 3))
     mine = bc_rows(r.bc_out, 0, head)[...].astype(F32)
     for o in range(1, nh):
-        came(BC, o - 1, HEAD_AXIS, -o, r.bc_in.at[o - 1])
-        mine = mine + r.bc_in[o - 1].astype(F32)
+        came(BC, o - 1, HEAD_AXIS, -o, r.bc_in[o - 1])
+        mine = mine + r.bc_in[o - 1][...].astype(F32)
     r.wq_mine[...] = mine.astype(BF16)
     start_inward(WQ)
     total_b(WP, r.pack)
@@ -952,7 +963,6 @@
         wv=vmem(w_value.shape, BF16),
         wbc=vmem(w_bc.shape, BF16),
         wo=vmem(w_out.shape, BF16),
-        bc_in=vmem((nh - 1, width // 2 // nh, bc_width), BF16),
         cot_all=vmem((tokens, width), BF16),
         halo_x=vmem((TAIL, width), BF16),
         doc_out=vmem((8, 128), F32),
@@ -976,6 +986,8 @@
         inc=vmem((blocks + 1, state, inner), F32),
         kept=vmem((blocks, 1, inner), F32),
         end=vmem((state, inner), F32),
+        adj=vmem((blocks, state, inner), BF16),
+        tail=vmem((EDGE, channels), F32),
         own=vmem((heads // 2, state, 2 * head_dim), F32),
         end_out=vmem((heads // 2, state, 2 * head_dim), F32),
         end_in=vmem((heads // 2, state, 2 * head_dim), F32),
@@ -992,9 +1004,9 @@
         prod=vmem((1, inner), F32),
         sum_out=vmem((blocks, 8, BLOCK), F32),
         sum_in=vmem((blocks * (nh - 1), 8, BLOCK), F32),
-        parts=vmem((blocks, BLOCK, width + bc_width), BF16),
+        parts=vmem((blocks, BLOCK, width), BF16),
         out_in=vmem((blocks * 6, BLOCK // 2, part), BF16),
-        part_in=vmem((blocks * 6, slab // 2, width + bc_width), BF16),
+        part_in=vmem((blocks * 6, slab // 2, width), BF16),
         gw_out=vmem(w_out.shape, F32),
         wq_sum=vmem((width // 2 // nh, bc_width), BF16),
         dz=vmem((tokens, inner), BF16),
@@ -1037,6 +1049,8 @@
         r.gw_bc = r.y.at[pl.ds(0, width), pl.ds(0, bc_width)]
         r.bc_pair = r.y.at[pl.ds(width, width // 2), pl.ds(0, bc_width)]
         r.bc_out = r.xs.at[pl.ds(0, width // 2), pl.ds(0, bc_width)]
+        free = [pl.ds(width // 2 + o * (width // 2 // nh), width // 2 // nh) for o in range(nh - 1)]
+        r.bc_in = [r.xs.at[rows, pl.ds(0, bc_width)] for rows in free]
         r.wv_mine = r.xs.at[pl.ds(width, width // 2)]
         kernel(r)
 
@@ -1051,7 +1065,7 @@
         ),
         name="block",
     )(*inputs.values())
-    steps = 8
+    steps = 4
     grads = (block_out, grad_in, g_gate, g_value, g_out, g_bc)
     kinds = (BF16, BF16, F32, F32, F32, F32)
     tiny = ((1, width), (heads, width), (n_taps + 1, inner), (n_taps + 1, bc_width), (1, heads), (1, heads), (1, heads),

time: 166 us -> 157 us (0.946)
  Pallas kernels: 164 us -> 156 us
    pallas_call x1, Pallas kernels: 155 us -> 148 us  [on_device(): pl.pallas_call(run, out_shape=[jax.ShapeDtypeStruct(*o) for o in outputs....]
where the time goes in v5:
time: 157 us
  Pallas kernels  156 us (99%)
    pallas_call x1, Pallas kernels, on_device(): pl.pallas_call(run, out_shape=[jax.ShapeDtypeStruct(*o) for o in outputs....  148 us
    pallas_call x1, Pallas kernels, on_device(): pl.pallas_call(functools.partial(write_kernel, len(grads)), grid=(steps,)...  7.88 us

profile of v5, /device:TPU:0, one launch (start us, length us, event | category | flops | bytes accessed | tf_op | source)
XLA Modules:
  0.0 157.1 jit_solution(12146425462207055060)
XLA Ops:
  0.7 148.4 %block.1 = (bf16[1536,256]{1,0:T(8,128)(2,1)}, bf16[1536,1024]{1,0:T(8,128)(2,1)}, bf16[1024,512]{1,0:T(8,128)(2,1)}, bf16[1024,512]{1,0:T(8,128)(2,1)}, bf16[51...) custom-call(bf16[1536,1024]{1,0:T(8,128)(2,1)} %bitcast.16, ...), custom_call_target="tpu_custom_call" | custom-call | tf_op jit(solution)/shard_map/block/pallas_call | solution.py:1057
  149.0 7.9 %write.1 = (bf16[1536,256]{1,0:T(8,128)(2,1)}, bf16[1536,1024]{1,0:T(8,128)(2,1)}, f32[1024,512]{1,0:T(8,128)}, f32[1024,512]{1,0:T(8,128)}, f32[512,1024]{1,0:T...) custom-call(bf16[1536,256]{1,0:T(8,128)(2,1)} %get-tuple-element.36., ...), custom_call_target="tpu_custom_call" | custom-call | tf_op jit(solution)/shard_map/write/pallas_call | solution.py:1080

commit v6 on v5

--- a/solution.py
+++ b/solution.py
@@ -319,10 +319,10 @@
             r.inc[c, :, cols] = inc
             r.own[pair] = r.kept[c, :, cols] * r.own[pair] + inc
 
-        repeat(blocks // 2, lambda i, body=own_states: (body(2 * i), body(2 * i + 1)))
+        repeat(blocks // 3, lambda i, body=own_states: [body(3 * i + k) for k in range(3)])
         relay(pair)
-
-    gather_2(COT, 0, cot_of, cot_half)
+        if pair == pairs - 2:
+            gather_2(COT, 0, cot_of, cot_half)
 
     def relay_back(turn):
         distance = ns - 1 - seq
@@ -363,7 +363,7 @@
         relay(pairs + c)
 
     loads[4].wait()
-    repeat(blocks, intra)
+    repeat(blocks // 2, lambda i: (intra(2 * i), intra(2 * i + 1)))
     loads[5].wait()
 
     if 2 * (ns - 1) > blocks:
@@ -569,6 +569,8 @@
 
     total_a(WO, r.gw_out).start()
     total_a(WG, r.gw_gate).start()
+    total_b(WO, r.gw_out)
+    total_b(WG, r.gw_gate)
 
     if 2 * (ns - 1) + pairs // 2 > blocks:
         repeat(2 * (ns - 1) + pairs // 2 - blocks, lambda i: relay_back(blocks + i))
@@ -729,8 +731,6 @@
         @pl.when(c == 0)
         def _():
             link(EDGES, 0, SEQ_AXIS, -1, first_rows, last_rows).start()
-            total_b(WO, r.gw_out)
-            total_b(WG, r.gw_gate)
             r.gw_value[...] = jnp.zeros_like(r.gw_value)
 
         add_residual(c)
@@ -1065,7 +1065,7 @@
         ),
         name="block",
     )(*inputs.values())
-    steps = 4
+    steps = 2
     grads = (block_out, grad_in, g_gate, g_value, g_out, g_bc)
     kinds = (BF16, BF16, F32, F32, F32, F32)
     tiny = ((1, width), (heads, width), (n_taps + 1, inner), (n_taps + 1, bc_width), (1, heads), (1, heads), (1, heads),

time: 157 us -> 156 us (level)
  no operation moved by 1% of the time
where the time goes in v6:
time: 156 us; the launch traced here: 155 us
  Pallas kernels  155 us (99%)
    pallas_call x1, Pallas kernels, on_device(): pl.pallas_call(run, out_shape=[jax.ShapeDtypeStruct(*o) for o in outputs....  147 us
    pallas_call x1, Pallas kernels, on_device(): pl.pallas_call(functools.partial(write_kernel, len(grads)), grid=(steps,)...  7.24 us

profile of v6, /device:TPU:0, one launch (start us, length us, event | category | flops | bytes accessed | tf_op | source)
XLA Modules:
  0.0 155.4 jit_solution(8695410392509876724)
XLA Ops:
  0.7 147.3 %block.1 = (bf16[1536,256]{1,0:T(8,128)(2,1)}, bf16[1536,1024]{1,0:T(8,128)(2,1)}, bf16[1024,512]{1,0:T(8,128)(2,1)}, bf16[1024,512]{1,0:T(8,128)(2,1)}, bf16[51...) custom-call(bf16[1536,1024]{1,0:T(8,128)(2,1)} %bitcast.16, ...), custom_call_target="tpu_custom_call" | custom-call | tf_op jit(solution)/shard_map/block/pallas_call | solution.py:1057
  148.0 7.2 %write.1 = (bf16[1536,256]{1,0:T(8,128)(2,1)}, bf16[1536,1024]{1,0:T(8,128)(2,1)}, f32[1024,512]{1,0:T(8,128)}, f32[1024,512]{1,0:T(8,128)}, f32[512,1024]{1,0:T...) custom-call(bf16[1536,256]{1,0:T(8,128)(2,1)} %get-tuple-element.36., ...), custom_call_target="tpu_custom_call" | custom-call | tf_op jit(solution)/shard_map/write/pallas_call | solution.py:1080
